TPU v7x, 32 devices: a whole 2x2x4 slice. The times are simulated.
32 devices in a mesh: dp: 8 (over y, x, core), expert: 4 (over z).
Axes of the slice: x: 2, y: 2, z: 4, core: 2. Of those that a mesh axis runs over, the one named last changes fastest.
Arguments:
- tokens: bfloat16 [1024, 2048], P('dp'), may hold values from -6 to 6
- route_expert: int32 [1024, 4], P('dp'), may hold values from 0 to 7, all different within a row; in each aligned block of 128 rows (0 to 127, 128 to 255, ...) at most 128 rows name the same one
- route_weight: float32 [1024, 4], P('dp'), may hold values from 0.1 to 1
- gate_weight: bfloat16 [8, 1408, 2048], P('dp', 'expert'), may hold values from -0.125 to 0.125
- up_weight: bfloat16 [8, 1408, 2048], P('dp', 'expert'), may hold values from -0.125 to 0.125
- down_weight: bfloat16 [8, 1408, 2048], P('dp', 'expert'), may hold values from -0.15625 to 0.15625
- gate_scale: float32 [8, 1408], P('dp', 'expert'), may hold values from 0.5 to 2
- up_scale: float32 [8, 1408], P('dp', 'expert'), may hold values from 0.5 to 2
- down_scale: float32 [8, 2048], replicated, may hold values from 0.5 to 2
- cotangent: bfloat16 [1024, 2048], P('dp', 'expert'), may hold values from -6 to 6
Outputs:
- mixed: bfloat16 [1024, 2048], P('dp', 'expert')
- token_grad: bfloat16 [1024, 2048], P('dp', 'expert')
- route_grad: float32 [1024, 4], P('dp')
- gate_grad: float32 [8, 1408, 2048], P('dp', 'expert')
- up_grad: float32 [8, 1408, 2048], P('dp', 'expert')
- down_grad: float32 [8, 1408, 2048], P('dp', 'expert')
Inputs may be any that keep to these rules, and one draw needn't show every extreme that they name: `route_expert`: each row names 4 different experts. Among the 128 rows of one aligned block (the tokens of one index of dp) no expert is named by more than 128 rows, and in some block one expert is named by exactly 128 rows.
All inputs are finite; a program needn't handle non-finite values.
Results may differ from a plain program's by a relative error of at most 0.0058.
Values may be sent and summed in bfloat16 or wider, within the bound.
A program may use at most 128 MiB of HBM per device.

v0:
```python
import jax
import jax.numpy as jnp
from jax import lax
from jax.sharding import PartitionSpec as P


def local(
    tokens,
    route_expert,
    route_weight,
    gate_weight,
    up_weight,
    down_weight,
    gate_scale,
    up_scale,
    down_scale,
    cotangent,
):
    owners = lax.axis_size("dp")
    tok_rows, width = tokens.shape
    choose = route_expert.shape[1]
    capacity = 2 * tok_rows * choose // owners
    slots = owners * capacity
    assigned = tok_rows * choose
    col_share = width // lax.axis_size("expert")
    col_start = lax.axis_index("expert") * col_share
    flat_expert = route_expert.reshape(-1)
    one_hot = (flat_expert[:, None] == jnp.arange(owners, dtype=jnp.int32)[None, :]).astype(
        jnp.int32
    )
    ranks = jnp.sum((jnp.cumsum(one_hot, axis=0) - 1) * one_hot, axis=1)
    slot_index = flat_expert * capacity + ranks
    slot_token = (
        jnp.zeros((slots,), jnp.int32)
        .at[slot_index]
        .set(jnp.arange(assigned, dtype=jnp.int32) // choose)
    )
    filled = jnp.zeros((slots,), jnp.bool_).at[slot_index].set(True)
    slot_weight = jnp.zeros((slots,), jnp.float32).at[slot_index].set(route_weight.reshape(-1))
    outgoing = jnp.where(
        filled[:, None], jnp.take(tokens, slot_token, axis=0), jnp.zeros((), tokens.dtype)
    )
    arrived = lax.all_to_all(
        outgoing.reshape(owners, capacity, width), "dp", split_axis=0, concat_axis=0, tiled=True
    ).reshape(slots, width)
    gate_local = gate_weight[0]
    up_local = up_weight[0]
    down_local = down_weight[0]
    gate_pre = (
        lax.dot_general(
            arrived, gate_local, (((1,), (1,)), ((), ())), preferred_element_type=jnp.float32
        )
        * gate_scale[0][None, :]
    )
    up_pre = (
        lax.dot_general(
            arrived, up_local, (((1,), (1,)), ((), ())), preferred_element_type=jnp.float32
        )
        * up_scale[0][None, :]
    )
    sigmoid_gate = jax.nn.sigmoid(gate_pre)
    silu_gate = gate_pre * sigmoid_gate
    hidden = (silu_gate * up_pre).astype(jnp.bfloat16)
    summed = lax.psum_scatter(
        lax.dot_general(
            down_local, hidden, (((0,), (1,)), ((), ())), preferred_element_type=jnp.float32
        ),
        "expert",
        scatter_dimension=0,
        tiled=True,
    )
    owner_scale = lax.dynamic_slice(down_scale, (lax.axis_index("dp"), col_start), (1, col_share))[
        0
    ]
    out_cols = (summed * owner_scale[:, None]).astype(jnp.bfloat16)
    returned = lax.all_to_all(
        out_cols.reshape(col_share, owners, capacity), "dp", split_axis=1, concat_axis=1, tiled=True
    ).reshape(col_share, slots)
    picked = (
        jnp.take(returned, slot_index, axis=1)
        .reshape(col_share, tok_rows, choose)
        .astype(jnp.float32)
    )
    mixed = jnp.sum(picked * route_weight[None, :, :], axis=2).T.astype(jnp.bfloat16)
    cot_cols = cotangent.T.astype(jnp.float32)
    route_part = jnp.sum(picked * cot_cols[:, :, None], axis=0)
    route_grad = lax.psum(route_part, "expert")
    slot_scale = jnp.repeat(down_scale, capacity, axis=0)
    cot_slots = jnp.take(cotangent, slot_token, axis=0).astype(jnp.float32)
    scale_share = lax.dynamic_slice_in_dim(slot_scale, col_start, col_share, 1)
    weighted = (cot_slots * slot_weight[:, None] * scale_share).astype(jnp.bfloat16)
    pieces = lax.all_to_all(
        weighted.reshape(owners, capacity, col_share), "dp", split_axis=0, concat_axis=0, tiled=True
    )
    out_grad = lax.all_gather(pieces, "expert", axis=2, tiled=True).reshape(slots, width)
    hidden_grad = lax.dot_general(
        out_grad, down_local, (((1,), (1,)), ((), ())), preferred_element_type=jnp.float32
    )
    gate_in = (
        hidden_grad
        * up_pre
        * sigmoid_gate
        * (1.0 + gate_pre * (1.0 - sigmoid_gate))
        * gate_scale[0][None, :]
    ).astype(jnp.bfloat16)
    up_in = (hidden_grad * silu_gate * up_scale[0][None, :]).astype(jnp.bfloat16)
    down_grad = lax.dot_general(
        hidden, out_grad, (((0,), (0,)), ((), ())), preferred_element_type=jnp.float32
    )
    gate_grad = lax.dot_general(
        gate_in, arrived, (((0,), (0,)), ((), ())), preferred_element_type=jnp.float32
    )
    up_grad = lax.dot_general(
        up_in, arrived, (((0,), (0,)), ((), ())), preferred_element_type=jnp.float32
    )
    first = lax.dot_general(
        gate_local, gate_in, (((0,), (1,)), ((), ())), preferred_element_type=jnp.float32
    )
    second = lax.dot_general(
        up_local, up_in, (((0,), (1,)), ((), ())), preferred_element_type=jnp.float32
    )
    input_cols = lax.psum_scatter(first + second, "expert", scatter_dimension=0, tiled=True)
    input_home = lax.all_to_all(
        input_cols.reshape(col_share, owners, capacity),
        "dp",
        split_axis=1,
        concat_axis=1,
        tiled=True,
    ).reshape(col_share, slots)
    token_grad = jnp.sum(
        jnp.take(input_home, slot_index, axis=1).reshape(col_share, tok_rows, choose), axis=2
    ).T.astype(jnp.bfloat16)
    return (mixed, token_grad, route_grad, gate_grad[None], up_grad[None], down_grad[None])


def solution(mesh):
    return jax.shard_map(
        local,
        mesh=mesh,
        in_specs=(
            P("dp", None),
            P("dp", None),
            P("dp", None),
            P("dp", "expert", None),
            P("dp", "expert", None),
            P("dp", "expert", None),
            P("dp", "expert"),
            P("dp", "expert"),
            P(),
            P("dp", "expert"),
        ),
        out_specs=(
            P("dp", "expert"),
            P("dp", "expert"),
            P("dp", None),
            P("dp", "expert", None),
            P("dp", "expert", None),
            P("dp", "expert", None),
        ),
        check_vma=False,
    )
```

profile of v0, /device:TPU:0, one launch (start us, length us, event | category | flops | bytes accessed | tf_op | source)
XLA Modules:
  0.0 492.3 jit_solution(7259084278115259597)
XLA Ops:
  7.2 0.0 copy-start
  7.2 0.0 all-gather.2.cloned.1.call-start
  7.3 0.9 copy.18
  8.2 0.1 eq.26
  8.3 0.1 reshape.145
  8.4 1.1 reduce-window.6
  9.5 0.2 slice_reduce_fusion
  9.8 0.1 mul.123
  9.9 0.1 fusion.9
  10.0 0.0 copy-start.18
  10.0 2.4 scatter_custom_fusion.1
  12.5 0.8 copy.21
  13.3 0.1 reshape.208
  13.4 0.5 copy-done.14
  13.9 2.4 scatter_custom_fusion.2
  16.4 0.0 copy-start.16
  16.4 4.0 gather_fusion.2
  20.4 1.0 broadcast_in_dim.109
  21.4 0.4 multiply_convert_fusion
  21.9 20.6 %all_to_all.20 = bf16[8,128,512]{2,1,0:T(8,128)(2,1)} all-to-all(bf16[8,128,512]{2,1,0:T(8,128)(2,1)S(1)} %bitcast.86), channel_id=1, replica_groups=mesh['dp'=8,'expert'=4] {'dp'}, dimensions={0} | all-to-all | bytes 2097152 | tf_op jit(solution)/shard_map/all_to_all | solution.py:92
  42.4 0.0 all-gather.2.cloned.1.call-update
  42.5 6.0 %gather_fusion = bf16[1024,2048]{1,0:T(8,128)(2,1)} fusion(bf16[128,2048]{1,0:T(8,128)(2,1)S(1)} %copy-done.2, s32[1024]{0:T(1024)S(1)} %fusion.11), kind=kCustom, calls=%fused_computation | custom fusion | bytes 8392704 | tf_op jit(solution)/shard_map/jit(_take)/gather | solution.py:41
  48.5 2.4 scatter_custom_fusion
  51.0 4.1 select_select_fusion
  55.1 4.7 all-to-all-start
  59.8 0.2 reduce-scatter.3.cloned.1.call-start
  60.1 48.8 %all-to-all-done = bf16[8,128,2048]{2,1,0:T(8,128)(2,1)} async-done(((bf16[8,128,2048]{2,1,0:T(8,128)(2,1)}), bf16[8,128,2048]{2,1,0:T(8,128)(2,1)}, u32[]{:S(2)}, u32[]{:S(2)}) %all-to-all-start) | async-done | bytes 4194336 | tf_op jit(solution)/shard_map/all_to_all | solution.py:43
  108.9 5.5 %convolution_multiply_fusion.1 = f32[1024,352]{0,1:T(8,128)} fusion(bf16[1024,2048]{1,0:T(8,128)(2,1)} %bitcast.7, bf16[1,352,2048]{2,1,0:T(8,128)(2,1)} %param.13, f32[352]{0:T(512)S(1)} %reduce.4), kind=kOutput, calls=%fused_computation.16 | convolution fusion | flops 1476755456 | bytes 7079296 | tf_op jit(solution)/shard_map/dot_general | solution.py:50
  114.4 8.3 %all-gather.2.cloned.1.call-done = bf16[8,128,2048]{2,1,0:T(8,128)(2,1)} async-done(((bf16[8,128,512]{2,1,0:T(8,128)(2,1)}), bf16[8,128,2048]{2,1,0:T(8,128)(2,1)}) %all-gather.2.cloned.1.call-update) | async-done | bytes 4194320 | tf_op jit(solution)/shard_map/all_gather | solution.py:95
  122.7 4.0 fusion
  126.8 4.6 multiply_convert_fusion.4
  131.4 0.0 copy-start.13
  131.4 0.8 copy-done.13
  132.2 5.6 %convolution_bitcast_fusion = f32[2048,1024]{0,1:T(8,128)} fusion(bf16[1024,352]{0,1:T(8,128)(2,1)S(1)} %get-tuple-element.14, bf16[1,352,2048]{2,1,0:T(8,128)(2,1)S(1)} %copy-done.10), kind=kOutput, calls=%fused_computation.8 | convolution fusion | flops 1476395008 | bytes 10551296 | tf_op jit(solution)/shard_map/dot_general | solution.py:65
  137.8 0.0 reduce-scatter.3.cloned.1.call-update
  137.9 0.0 reduce-scatter.5.cloned.1.call-start
  137.9 3.7 fusion.5
  141.7 5.8 %add_bitcast_fusion = f32[2048,1024]{0,1:T(8,128)} fusion(f32[1024,2048]{1,0:T(8,128)S(1)} %fusion.5, bf16[1024,352]{0,1:T(8,128)(2,1)S(1)} %get-tuple-element.16, bf16[1,352,2048]{2,1,0:T(8,128)(2,1)S(1)} %copy-done), kind=kOutput, calls=%fused_computation.7 | convolution fusion | flops 1478492160 | bytes 18939904 | tf_op jit(solution)/shard_map/dot_general | solution.py:119
  147.5 0.0 reduce-scatter.5.cloned.1.call-update
  147.5 0.1 dynamic_slice.6
  147.6 133.4 %reduce-scatter.3.cloned.1.call-done = f32[512,1024]{0,1:T(8,128)} async-done(((f32[2048,1024]{0,1:T(8,128)}), f32[512,1024]{0,1:T(8,128)}) %reduce-scatter.3.cloned.1.call-update) | async-done | bytes 2097168 | tf_op jit(solution)/shard_map/reduce_scatter | solution.py:64
  281.0 2.8 multiply_convert_fusion.1
  283.9 3.8 all-to-all-start.1
  287.6 0.1 reduce_sum.43
  287.8 140.8 %reduce-scatter.5.cloned.1.call-done = f32[512,1024]{0,1:T(8,128)} async-done(((f32[2048,1024]{0,1:T(8,128)}), f32[512,1024]{0,1:T(8,128)}) %reduce-scatter.5.cloned.1.call-update) | async-done | bytes 2097168 | tf_op jit(solution)/shard_map/reduce_scatter | solution.py:122
  428.6 3.8 all-to-all-start.3
  432.4 0.0 copy-start.19
  432.5 0.1 broadcast_in_dim.111
  432.6 1.2 mul.148
  433.7 2.6 mul.149
  436.3 0.0 copy-start.17
  436.3 0.0 copy-start.12
  436.3 5.7 %convolution_bitcast_fusion.1 = f32[1,352,2048]{2,1,0:T(8,128)} fusion(bf16[1024,352]{0,1:T(8,128)(2,1)} %copy-done.13, bf16[1024,2048]{1,0:T(8,128)(2,1)} %bitcast.98), kind=kOutput, calls=%fused_computation.10 | convolution fusion | flops 1476395008 | bytes 7798784 | tf_op jit(solution)/shard_map/dot_general | solution.py:107
  442.1 5.5 %convolution_bitcast_fusion.3 = f32[1,352,2048]{2,1,0:T(8,128)} fusion(bf16[1024,352]{0,1:T(8,128)(2,1)S(1)} %copy-done.12, bf16[1024,2048]{1,0:T(8,128)(2,1)} %bitcast.7), kind=kOutput, calls=%fused_computation.12 | convolution fusion | flops 1476395008 | bytes 7798784 | tf_op jit(solution)/shard_map/dot_general | solution.py:110
  447.6 5.4 %convolution_bitcast_fusion.2 = f32[1,352,2048]{2,1,0:T(8,128)} fusion(bf16[1024,352]{0,1:T(8,128)(2,1)S(1)} %copy-done.5, bf16[1024,2048]{1,0:T(8,128)(2,1)} %bitcast.7), kind=kOutput, calls=%fused_computation.11 | convolution fusion | flops 1476395008 | bytes 7798784 | tf_op jit(solution)/shard_map/dot_general | solution.py:113
  453.0 2.6 gather_fusion.1
  455.6 2.0 gather.25
  457.6 1.6 multiply_reduce_fusion
  459.3 0.1 reduce_sum.48
  459.4 19.3 %psum.7 = f32[128,4]{1,0:T(8,128)S(1)} all-reduce(f32[128,4]{1,0:T(8,128)S(1)} %reduce_sum.48), channel_id=1, replica_groups=mesh['dp'=8,'expert'=4] {'expert'}, use_global_device_ids=true, to_apply=%region_11.12 | all-reduce | flops 512 | bytes 4096 | tf_op jit(solution)/shard_map/psum | solution.py:87
  478.7 0.7 copy.23
  479.4 2.6 gather_fusion.3
  482.0 1.6 gather.28
  483.6 2.2 select_reduce_fusion
  (54 shorter events, 0.3 us)
Async XLA Ops:
  7.2 119.6 %copy-start = (bf16[1,352,2048]{2,1,0:T(8,128)(2,1)S(1)}, bf16[1,352,2048]{2,1,0:T(8,128)(2,1)}, u32[]{:S(2)}) copy-start(bf16[1,352,2048]{2,1,0:T(8,128)(2,1)} %param.14) | copy-start | bytes 4325380
  7.2 9.2 %copy-start.3 = (bf16[128,512]{1,0:T(8,128)(2,1)S(1)}, bf16[128,512]{1,0:T(8,128)(2,1)}, u32[]{:S(2)}) copy-start(bf16[128,512]{1,0:T(8,128)(2,1)} %param.19) | copy-start | bytes 393220
  7.2 115.5 %all-gather.2.cloned.1.call-start = ((), (), s32[]{:S(2)}) async-start(), calls=%async_computation.7 | async-start | bytes 5242880 | tf_op jit(solution)/shard_map/all_gather | solution.py:95
  8.1 5.3 %copy-start.7 = (s32[128,4]{1,0:T(8,128)}, s32[128,4]{1,0:T(8,128)S(1)}, u32[]{:S(2)}) copy-start(s32[128,4]{1,0:T(8,128)S(1)} %copy.18) | copy-start | bytes 6148
  10.0 38.5 %copy-start.18 = (s32[512,1]{0,1:T(1,128)}, s32[512,1]{0,1:T(1,128)S(1)}, u32[]{:S(2)}) copy-start(s32[512,1]{0,1:T(1,128)S(1)} %compare_select_fusion.1) | copy-start | bytes 6148
  13.3 0.6 copy-start.14
  16.4 4.0 copy-start.16
  21.8 20.6 %copy-start.2 = (bf16[128,2048]{1,0:T(8,128)(2,1)S(1)}, bf16[128,2048]{1,0:T(8,128)(2,1)}, u32[]{:S(2)}) copy-start(bf16[128,2048]{1,0:T(8,128)(2,1)} %param.10) | copy-start | bytes 1572868
  55.1 4.9 %copy-start.20 = (f32[1,352]{1,0:T(1,128)S(1)}, f32[1,352]{1,0:T(1,128)}, u32[]{:S(2)}) copy-start(f32[1,352]{1,0:T(1,128)} %param.16) | copy-start | bytes 4228
  55.1 5.0 %copy-start.21 = (f32[1,352]{1,0:T(1,128)S(1)}, f32[1,352]{1,0:T(1,128)}, u32[]{:S(2)}) copy-start(f32[1,352]{1,0:T(1,128)} %param.17) | copy-start | bytes 4228
  55.1 53.8 %all-to-all-start = ((bf16[8,128,2048]{2,1,0:T(8,128)(2,1)}), bf16[8,128,2048]{2,1,0:T(8,128)(2,1)}, u32[]{:S(2)}, u32[]{:S(2)}) async-start(bf16[8,128,2048]{2,1,0:T(8,128)(2,1)} %select_select_fusion), calls=%async_computation | async-start | bytes 8388608 | tf_op jit(solution)/shard_map/all_to_all | solution.py:43
  59.8 221.2 %reduce-scatter.3.cloned.1.call-start = ((), (), s32[]{:S(2)}) async-start(), calls=%async_computation.6 | async-start | bytes 10485760 | tf_op jit(solution)/shard_map/reduce_scatter | solution.py:64
  108.9 13.8 %copy-start.9 = (bf16[1,352,2048]{2,1,0:T(8,128)(2,1)S(1)}, bf16[1,352,2048]{2,1,0:T(8,128)(2,1)}, u32[]{:S(2)}) copy-start(bf16[1,352,2048]{2,1,0:T(8,128)(2,1)} %param.15) | copy-start | bytes 4325380
  122.7 4.0 copy-start.22
  126.7 5.5 %copy-start.10 = (bf16[1,352,2048]{2,1,0:T(8,128)(2,1)S(1)}, bf16[1,352,2048]{2,1,0:T(8,128)(2,1)}, u32[]{:S(2)}) copy-start(bf16[1,352,2048]{2,1,0:T(8,128)(2,1)} %param.15) | copy-start | bytes 4325380
  131.4 0.9 copy-start.13
  131.4 6.5 %copy-start.11 = (bf16[1024,352]{0,1:T(8,128)(2,1)}, bf16[1024,352]{0,1:T(8,128)(2,1)S(1)}, u32[]{:S(2)}) copy-start(bf16[1024,352]{0,1:T(8,128)(2,1)S(1)} %get-tuple-element.15) | copy-start | bytes 2162692
  131.4 10.3 %copy-start.4 = (bf16[1024,352]{0,1:T(8,128)(2,1)}, bf16[1024,352]{0,1:T(8,128)(2,1)S(1)}, u32[]{:S(2)}) copy-start(bf16[1024,352]{0,1:T(8,128)(2,1)S(1)} %get-tuple-element.16) | copy-start | bytes 2162692
  137.9 290.8 %reduce-scatter.5.cloned.1.call-start = ((), (), s32[]{:S(2)}) async-start(), calls=%async_computation.8 | async-start | bytes 10485760 | tf_op jit(solution)/shard_map/reduce_scatter | solution.py:122
  283.9 144.8 %all-to-all-start.1 = ((bf16[512,8,128]{0,2,1:T(8,128)(2,1)}), bf16[512,8,128]{0,2,1:T(8,128)(2,1)S(1)}, u32[]{:S(2)}, u32[]{:S(2)}) async-start(bf16[512,8,128]{0,2,1:T(8,128)(2,1)} %bitcast.13), calls=%async_computation.2 | async-start | bytes 2097152 | tf_op jit(solution)/shard_map/all_to_all | solution.py:76
  428.6 3.8 copy-start.8
  428.6 50.7 %all-to-all-start.3 = ((f32[512,8,128]{0,2,1:T(8,128)}), f32[512,8,128]{0,2,1:T(8,128)S(1)}, u32[]{:S(2)}, u32[]{:S(2)}) async-start(f32[512,8,128]{0,2,1:T(8,128)} %bitcast.87), calls=%async_computation.5 | async-start | bytes 4194304 | tf_op jit(solution)/shard_map/all_to_all | solution.py:123
  432.4 3.9 copy-start.19
  436.3 16.7 %copy-start.17 = (s32[1024]{0:T(1024)}, s32[1024]{0:T(1024)S(1)}, u32[]{:S(2)}) copy-start(s32[1024]{0:T(1024)S(1)} %pad_clamp_fusion) | copy-start | bytes 12292
  436.3 5.7 %copy-start.12 = (bf16[1024,352]{0,1:T(8,128)(2,1)S(1)}, bf16[1024,352]{0,1:T(8,128)(2,1)}, u32[]{:S(2)}) copy-start(bf16[1024,352]{0,1:T(8,128)(2,1)} %copy-done.11) | copy-start | bytes 2162692
  442.1 5.5 %copy-start.5 = (bf16[1024,352]{0,1:T(8,128)(2,1)S(1)}, bf16[1024,352]{0,1:T(8,128)(2,1)}, u32[]{:S(2)}) copy-start(bf16[1024,352]{0,1:T(8,128)(2,1)} %copy-done.4) | copy-start | bytes 2162692
  479.4 6.4 %copy-start.1 = (bf16[1,352,2048]{2,1,0:T(8,128)(2,1)S(1)}, bf16[1,352,2048]{2,1,0:T(8,128)(2,1)}, u32[]{:S(2)}) copy-start(bf16[1,352,2048]{2,1,0:T(8,128)(2,1)} %param.14) | copy-start | bytes 4325380
  482.0 1.6 copy-start.6
  482.0 1.6 copy-start.15
Sparse Core Ops, SparseCore 0:
  42.6 80.1 all-gather.1
  138.0 143.0 reduce-scatter.2
  283.4 145.1 reduce-scatter.4
where the time goes:
time: 493 us; the launch traced here: 492 us
  waiting for transfers between devices  331 us (67%)
  matrix products  45.9 us (9%)
  blocking collectives  39.9 us (8%)
  local copies, waits for them, and re-layouts  35.7 us (7%)
  between operations  14.2 us (3%)
  other arithmetic  12.6 us (3%)
  starting transfers between devices  12.5 us (3%)
    reduce_scatter x1, waiting for transfers between devices, local(): lax.psum_scatter(first + second, 'expert', scatter_dimension=0, tiled=True)  141 us
    reduce_scatter x1, waiting for transfers between devices, local(): lax.psum_scatter(lax.dot_general(down_local, hidden, (((0,), (1,)), ((),...  133 us
    all_to_all x1, waiting for transfers between devices, local(): lax.all_to_all(outgoing.reshape(owners, capacity, width), 'dp', split_axi...  48.8 us
    all_to_all x1, blocking collectives, local(): lax.all_to_all(weighted.reshape(owners, capacity, col_share), 'dp', split...  20.6 us
    psum x1, blocking collectives, local(): route_grad = lax.psum(route_part, 'expert')  19.3 us
  transfers between devices with their start and end apart: 6, of which 4 were waited for; matrix products, arithmetic and copies ran while one was open for 12% of the time, Pallas kernels for 0%

commit v1 on v0

--- a/solution.py
+++ b/solution.py
@@ -4,7 +4,7 @@
 from jax.sharding import PartitionSpec as P
 
 
-def local(
+def routed(
     tokens,
     route_expert,
     route_weight,
@@ -28,7 +28,10 @@
     one_hot = (flat_expert[:, None] == jnp.arange(owners, dtype=jnp.int32)[None, :]).astype(
         jnp.int32
     )
-    ranks = jnp.sum((jnp.cumsum(one_hot, axis=0) - 1) * one_hot, axis=1)
+    order = jnp.arange(assigned, dtype=jnp.int32)
+    before = (order[:, None] > order[None, :]).astype(jnp.bfloat16)
+    earlier = jnp.dot(before, one_hot.astype(jnp.bfloat16), preferred_element_type=jnp.float32)
+    ranks = jnp.sum(earlier.astype(jnp.int32) * one_hot, axis=1)
     slot_index = flat_expert * capacity + ranks
     slot_token = (
         jnp.zeros((slots,), jnp.int32)
@@ -133,6 +136,104 @@
     return (mixed, token_grad, route_grad, gate_grad[None], up_grad[None], down_grad[None])
 
 
+def dense(
+    tokens,
+    route_expert,
+    route_weight,
+    gate_weight,
+    up_weight,
+    down_weight,
+    gate_scale,
+    up_scale,
+    down_scale,
+    cotangent,
+):
+    me = lax.axis_index("dp")
+    arrived = lax.all_gather(tokens, "dp", axis=0, tiled=True)
+    cot_mine = lax.all_gather(cotangent, "expert", axis=1, tiled=True)
+    cot_all = lax.all_gather(cot_mine, "dp", axis=0, tiled=True)
+    experts = lax.all_gather(route_expert.astype(jnp.float32), "dp", axis=0, tiled=True)
+    weights = lax.all_gather(route_weight, "dp", axis=0, tiled=True)
+    chosen = experts == me.astype(jnp.float32)
+    row_weight = jnp.sum(jnp.where(chosen, weights, 0.0), axis=1, keepdims=True)
+    gate_local, up_local, down_local = gate_weight[0], up_weight[0], down_weight[0]
+    scale = lax.dynamic_slice_in_dim(down_scale, me, 1, 0)
+    gate_pre = (
+        lax.dot_general(
+            arrived, gate_local, (((1,), (1,)), ((), ())), preferred_element_type=jnp.float32
+        )
+        * gate_scale
+    )
+    up_pre = (
+        lax.dot_general(
+            arrived, up_local, (((1,), (1,)), ((), ())), preferred_element_type=jnp.float32
+        )
+        * up_scale
+    )
+    sigmoid_gate = jax.nn.sigmoid(gate_pre)
+    silu_gate = gate_pre * sigmoid_gate
+    hidden = (silu_gate * up_pre).astype(jnp.bfloat16)
+    out_part = (
+        lax.dot_general(
+            hidden, down_local, (((1,), (0,)), ((), ())), preferred_element_type=jnp.float32
+        )
+        * row_weight
+        * scale
+    ).astype(jnp.bfloat16)
+    mixed = reduce_home(out_part)
+    out_grad = (cot_all.astype(jnp.float32) * row_weight * scale).astype(jnp.bfloat16)
+    hidden_grad = lax.dot_general(
+        out_grad, down_local, (((1,), (1,)), ((), ())), preferred_element_type=jnp.float32
+    )
+    gate_in = (
+        hidden_grad * up_pre * sigmoid_gate * (1.0 + gate_pre * (1.0 - sigmoid_gate)) * gate_scale
+    ).astype(jnp.bfloat16)
+    up_in = (hidden_grad * silu_gate * up_scale).astype(jnp.bfloat16)
+    input_part = (
+        lax.dot_general(
+            gate_in, gate_local, (((1,), (0,)), ((), ())), preferred_element_type=jnp.float32
+        )
+        + lax.dot_general(
+            up_in, up_local, (((1,), (0,)), ((), ())), preferred_element_type=jnp.float32
+        )
+    ).astype(jnp.bfloat16)
+    token_grad = reduce_home(input_part)
+    route_row = jnp.sum(hidden.astype(jnp.float32) * hidden_grad, axis=1, keepdims=True)
+    route_row = route_row / jnp.where(row_weight > 0.0, row_weight, 1.0)
+    route_part = jnp.where(chosen, route_row, 0.0)
+    route_sum = lax.psum(route_part, ("dp", "expert"))
+    rows = tokens.shape[0]
+    route_grad = lax.dynamic_slice_in_dim(route_sum, me * rows, rows, 0)
+    down_grad = lax.dot_general(
+        hidden, out_grad, (((0,), (0,)), ((), ())), preferred_element_type=jnp.float32
+    )
+    gate_grad = lax.dot_general(
+        gate_in, arrived, (((0,), (0,)), ((), ())), preferred_element_type=jnp.float32
+    )
+    up_grad = lax.dot_general(
+        up_in, arrived, (((0,), (0,)), ((), ())), preferred_element_type=jnp.float32
+    )
+    return (mixed, token_grad, route_grad, gate_grad[None], up_grad[None], down_grad[None])
+
+
+def reduce_home(part):
+    rows, width = part.shape
+    owners, shares = lax.axis_size("dp"), lax.axis_size("expert")
+    blocks = part.reshape(owners, rows // owners, width)
+    blocks = lax.all_to_all(blocks, "dp", split_axis=0, concat_axis=0, tiled=True)
+    home = jnp.sum(blocks.astype(jnp.float32), axis=0).astype(jnp.bfloat16)
+    cols = home.reshape(rows // owners, shares, width // shares)
+    cols = lax.all_to_all(cols, "expert", split_axis=1, concat_axis=1, tiled=True)
+    return jnp.sum(cols.astype(jnp.float32), axis=1).astype(jnp.bfloat16)
+
+
+def local(tokens, route_expert, *rest):
+    owners = lax.axis_size("dp")
+    rows, choose = route_expert.shape
+    full = 2 * rows * choose >= owners * rows
+    return (dense if full else routed)(tokens, route_expert, *rest)
+
+
 def solution(mesh):
     return jax.shard_map(
         local,

time: 493 us -> 285 us (0.58)
  waiting for transfers between devices: 331 us -> 118 us
  blocking collectives: 39.9 us -> 77.3 us
  local copies, waits for them, and re-layouts: 35.7 us -> 4.04 us
  starting transfers between devices: 12.5 us -> 19.1 us
    reduce_scatter x2 -> x0, waiting for transfers between devices: 274 us -> none  [the longest x1 141 us: local(): lax.psum_scatter(first + second, 'expert', scatter_dimension=0, tiled=True)]
    all_gather x0 -> x3, blocking collectives: none -> 37.2 us  [the longest x1 19.4 us: dense(): cot_mine = lax.all_gather(cotangent, 'expert', axis=1, tiled=True)]
    all_to_all x3 -> x4, waiting for transfers between devices: 48.8 us -> 85.6 us  [the longest x2 85.6 us: reduce_home(): lax.all_to_all(blocks, 'dp', split_axis=0, concat_axis=0, tiled=True)]
    all_gather x1 -> x2, waiting for transfers between devices: 8.3 us -> 31.5 us  [the longest x1 30.2 us: dense(): cot_all = lax.all_gather(cot_mine, 'dp', axis=0, tiled=True)]
    psum x1, blocking collectives: 19.3 us -> 40.1 us  [dense(): route_sum = lax.psum(route_part, ('dp', 'expert'))]
    all_to_all x1 -> x0, blocking collectives: 20.6 us -> none  [local(): lax.all_to_all(weighted.reshape(owners, capacity, col_share), 'dp', split...]
    gather x6 -> x0, local copies, waits for them, and re-layouts: 18.8 us -> none  [the longest x1 6.03 us: local(): jnp.take(tokens, slot_token, axis=0)]
    scatter x3 -> x0, local copies, waits for them, and re-layouts: 7.33 us -> none  [the longest x1 2.45 us: local(): filled = jnp.zeros((slots,), jnp.bool_).at[slot_index].set(True)]
  transfers between devices with their start and end apart: 6 -> 6, of which waited for: 4 -> 4; matrix products, arithmetic and copies ran while one was open for 12% -> 15% of each run, Pallas kernels for 0% -> 0%
where the time goes in v1:
time: 285 us; the launch traced here: 284 us
  waiting for transfers between devices  118 us (41%)
  blocking collectives  77.3 us (27%)
  matrix products  42.2 us (15%)
  starting transfers between devices  19.1 us (7%)
  between operations  14.2 us (5%)
  other arithmetic  9.58 us (3%)
  local copies, waits for them, and re-layouts  4.04 us (1%)
    all_to_all x2, waiting for transfers between devices, reduce_home(): lax.all_to_all(blocks, 'dp', split_axis=0, concat_axis=0, tiled=True)  85.6 us
    psum x1, blocking collectives, dense(): route_sum = lax.psum(route_part, ('dp', 'expert'))  40.1 us
    all_gather x1, waiting for transfers between devices, dense(): cot_all = lax.all_gather(cot_mine, 'dp', axis=0, tiled=True)  30.2 us
    all_gather x1, blocking collectives, dense(): cot_mine = lax.all_gather(cotangent, 'expert', axis=1, tiled=True)  19.4 us
    all_to_all x2, starting transfers between devices, reduce_home(): lax.all_to_all(cols, 'expert', split_axis=1, concat_axis=1, tiled=True)  9.69 us
    all_to_all x2, starting transfers between devices, reduce_home(): lax.all_to_all(blocks, 'dp', split_axis=0, concat_axis=0, tiled=True)  9.36 us
    all_gather x1, blocking collectives, dense(): lax.all_gather(route_expert.astype(jnp.float32), 'dp', axis=0, tiled=True)  8.9 us
    all_gather x1, blocking collectives, dense(): weights = lax.all_gather(route_weight, 'dp', axis=0, tiled=True)  8.89 us
  transfers between devices with their start and end apart: 6, of which 4 were waited for; matrix products, arithmetic and copies ran while one was open for 15% of the time, Pallas kernels for 0%

profile of v1, /device:TPU:0, one launch (start us, length us, event | category | flops | bytes accessed | tf_op | source)
XLA Modules:
  0.0 284.2 jit_solution(1381057140474687026)
XLA Ops:
  7.2 0.0 copy-start
  7.2 0.0 all-gather.3.cloned.1.call-start
  7.2 0.7 all-gather.3.cloned.1.call-update
  7.9 0.0 all-gather.5.cloned.1.call-start
  8.0 19.4 %all_gather.18 = bf16[128,2048]{1,0:T(8,128)(2,1)} all-gather(bf16[128,512]{1,0:T(8,128)(2,1)} %param.19), channel_id=1, replica_groups=mesh['dp'=8,'expert'=4] {'expert'}, dimensions={1}, use_global_device_ids=true | all-gather | bytes 655360 | tf_op jit(solution)/shard_map/all_gather | solution.py:153
  27.4 0.0 all-gather.5.cloned.1.call-update
  27.4 0.7 reduce.4
  28.1 0.7 reduce.5
  28.8 0.7 convert_element_type.39
  29.5 8.9 %all_gather.16 = f32[1024,4]{0,1:T(4,128)S(1)} all-gather(f32[128,4]{0,1:T(4,128)S(1)} %convert_element_type.39), channel_id=1, replica_groups=mesh['dp'=8,'expert'=4] {'dp'}, dimensions={0}, use_global_device_ids=true | all-gather | bytes 18432 | tf_op jit(solution)/shard_map/all_gather | solution.py:155
  38.4 8.9 %all_gather.17 = f32[1024,4]{0,1:T(4,128)S(1)} all-gather(f32[128,4]{0,1:T(4,128)} %param.12), channel_id=1, replica_groups=mesh['dp'=8,'expert'=4] {'dp'}, dimensions={0}, use_global_device_ids=true | all-gather | bytes 18432 | tf_op jit(solution)/shard_map/all_gather | solution.py:156
  47.3 0.8 constant_dynamic-slice_fusion.1
  48.1 0.0 copy-start.1
  48.2 1.3 all-gather.3.cloned.1.call-done
  49.4 0.0 copy-start.6
  49.4 5.6 %convolution_multiply_fusion = f32[1024,352]{0,1:T(8,128)} fusion(bf16[1024,2048]{1,0:T(8,128)(2,1)} %all-gather.3.cloned.1.call-done, bf16[1,352,2048]{2,1,0:T(8,128)(2,1)} %param.14, f32[352]{0:T(512)S(1)} %reduce.5), kind=kOutput, calls=%fused_computation.6 | convolution fusion | flops 1476755456 | bytes 7079296 | tf_op jit(solution)/shard_map/dot_general | solution.py:168
  55.0 0.0 copy-done.1
  55.0 0.0 copy-done.6
  55.0 2.9 %convolution_multiply_fusion.1 = f32[1024,352]{0,1:T(8,128)} fusion(bf16[1024,2048]{1,0:T(8,128)(2,1)S(1)} %copy-done.6, bf16[1,352,2048]{2,1,0:T(8,128)(2,1)S(1)} %copy-done.1, f32[352]{0:T(512)S(1)} %reduce.4), kind=kOutput, calls=%fused_computation.7 | convolution fusion | flops 1476755456 | bytes 7079296 | tf_op jit(solution)/shard_map/dot_general | solution.py:162
  57.9 30.2 %all-gather.5.cloned.1.call-done = bf16[1024,2048]{1,0:T(8,128)(2,1)} async-done(((bf16[128,2048]{1,0:T(8,128)(2,1)}), bf16[1024,2048]{1,0:T(8,128)(2,1)}) %all-gather.5.cloned.1.call-update) | async-done | bytes 4194320 | tf_op jit(solution)/shard_map/all_gather | solution.py:154
  88.1 0.0 copy-done
  88.1 6.6 %multiply_reduce_fusion = (f32[1024]{0:T(1024)S(1)}, bf16[1024,352]{0,1:T(8,128)(2,1)S(1)}, bf16[1024,352]{0,1:T(8,128)(2,1)}, bf16[1024,352]{0,1:T(8,128)(2,1)}) fusion(f32[1024,352]{0,1:T(8,128)} %convolution_multiply_fusion, f32[1024,352]{0,1:T(8,128)} %convolution_multiply_fusion.1, f32[352]{0:T(512)S(1)} %reduce.4, f32[352]{0:T(512)S(1)} %reduce.5, ...), kind=kOutput, calls=%fused_computation.16 | convolution fusion | flops 1491991552 | bytes 10701568 | tf_op jit(solution)/shard_map/dot_general | solution.py:185
  94.7 0.0 copy-start.8
  94.7 4.4 %multiply_convert_fusion.1 = bf16[1024,2048]{1,0:T(8,128)(2,1)} fusion(bf16[1024,352]{0,1:T(8,128)(2,1)S(1)} %get-tuple-element.7, f32[2048]{0:T(1024)S(1)} %bitcast.43, f32[1024]{0:T(1024)S(1)} %get-tuple-element.8, bf16[1,352,2048]{2,1,0:T(8,128)(2,1)S(1)} %copy-done), kind=kOutput, calls=%fused_computation.2 | convolution fusion | flops 1482686464 | bytes 6369280 | tf_op jit(solution)/shard_map/dot_general | solution.py:177
  99.1 0.0 copy-done.8
  99.1 4.8 %all-to-all-start = ((bf16[8,128,2048]{2,1,0:T(8,128)(2,1)}), bf16[8,128,2048]{2,1,0:T(8,128)(2,1)}, u32[]{:S(2)}, u32[]{:S(2)}) async-start(bf16[8,128,2048]{2,1,0:T(8,128)(2,1)} %bitcast.39), calls=%async_computation | async-start | bytes 8388608 | tf_op jit(solution)/shard_map/all_to_all | solution.py:223
  103.8 0.0 copy-start.2
  103.8 0.0 copy-start.3
  103.8 3.6 %fusion.5 = f32[1024,2048]{1,0:T(8,128)S(1)} fusion(bf16[1024,352]{0,1:T(8,128)(2,1)} %get-tuple-element.10, bf16[1,352,2048]{2,1,0:T(8,128)(2,1)S(1)} %copy-done.1), kind=kOutput, calls=%fused_computation.13 | convolution fusion | flops 1476395008 | bytes 10551296 | tf_op jit(solution)/shard_map/dot_general | solution.py:193
  107.5 0.0 copy-done.2
  107.5 0.0 copy-done.3
  107.5 4.5 %add_convert_fusion = bf16[1024,2048]{1,0:T(8,128)(2,1)} fusion(f32[1024,2048]{1,0:T(8,128)S(1)} %fusion.5, bf16[1024,352]{0,1:T(8,128)(2,1)S(1)} %copy-done.3, bf16[1,352,2048]{2,1,0:T(8,128)(2,1)S(1)} %copy-done.2), kind=kOutput, calls=%fused_computation | convolution fusion | flops 1480589312 | bytes 14745600 | tf_op jit(solution)/shard_map/dot_general | solution.py:196
  112.0 40.8 %all-to-all-done = bf16[8,128,2048]{2,1,0:T(8,128)(2,1)} async-done(((bf16[8,128,2048]{2,1,0:T(8,128)(2,1)}), bf16[8,128,2048]{2,1,0:T(8,128)(2,1)}, u32[]{:S(2)}, u32[]{:S(2)}) %all-to-all-start) | async-done | bytes 4194336 | tf_op jit(solution)/shard_map/all_to_all | solution.py:223
  152.8 4.6 %all-to-all-start.2 = ((bf16[8,128,2048]{2,1,0:T(8,128)(2,1)}), bf16[8,128,2048]{2,1,0:T(8,128)(2,1)}, u32[]{:S(2)}, u32[]{:S(2)}) async-start(bf16[8,128,2048]{2,1,0:T(8,128)(2,1)} %bitcast.38), calls=%async_computation.2 | async-start | bytes 8388608 | tf_op jit(solution)/shard_map/all_to_all | solution.py:223
  157.4 0.0 copy-start.5
  157.4 3.0 %reduce_sum.67 = bf16[128,2048]{1,0:T(8,128)(2,1)S(1)} reduce(bf16[8,128,2048]{2,1,0:T(8,128)(2,1)} %all-to-all-done, bf16[]{:T(256)} %constant.22.clone.1), dimensions={0}, to_apply=%region_1.2 | reduce | flops 1835008 | bytes 4718594 | tf_op jit(solution)/shard_map/reduce_sum | solution.py:224
  160.4 0.3 copy.18
  160.7 1.0 copy.19
  161.7 44.8 %all-to-all-done.2 = bf16[8,128,2048]{2,1,0:T(8,128)(2,1)} async-done(((bf16[8,128,2048]{2,1,0:T(8,128)(2,1)}), bf16[8,128,2048]{2,1,0:T(8,128)(2,1)}, u32[]{:S(2)}, u32[]{:S(2)}) %all-to-all-start.2) | async-done | bytes 4194336 | tf_op jit(solution)/shard_map/all_to_all | solution.py:223
  206.5 4.6 %all-to-all-start.1 = ((bf16[128,4,512]{2,0,1:T(8,128)(2,1)}), bf16[128,4,512]{2,0,1:T(8,128)(2,1)S(1)}, u32[]{:S(2)}, u32[]{:S(2)}) async-start(bf16[128,4,512]{2,0,1:T(8,128)(2,1)} %copy.19), calls=%async_computation.1 | async-start | bytes 1048576 | tf_op jit(solution)/shard_map/all_to_all | solution.py:226
  211.1 0.0 copy-done.5
  211.1 0.0 copy-start.4
  211.1 0.0 copy-start.7
  211.1 5.6 %convolution_bitcast_fusion.2 = f32[1,352,2048]{2,1,0:T(8,128)} fusion(bf16[1024,352]{0,1:T(8,128)(2,1)S(1)} %copy-done.5, bf16[1024,2048]{1,0:T(8,128)(2,1)} %all-gather.3.cloned.1.call-done), kind=kOutput, calls=%fused_computation.5 | convolution fusion | flops 1476395008 | bytes 7798784 | tf_op jit(solution)/shard_map/dot_general | solution.py:210
  216.7 0.0 copy-done.4
  216.7 0.0 copy-done.7
  216.7 3.3 %convolution_bitcast_fusion.1 = f32[1,352,2048]{2,1,0:T(8,128)} fusion(bf16[1024,352]{0,1:T(8,128)(2,1)S(1)} %copy-done.4, bf16[1024,2048]{1,0:T(8,128)(2,1)S(1)} %copy-done.7), kind=kOutput, calls=%fused_computation.4 | convolution fusion | flops 1476395008 | bytes 7798784 | tf_op jit(solution)/shard_map/dot_general | solution.py:213
  220.0 3.0 %reduce_sum.69 = bf16[128,2048]{1,0:T(8,128)(2,1)S(1)} reduce(bf16[8,128,2048]{2,1,0:T(8,128)(2,1)} %all-to-all-done.2, bf16[]{:T(256)} %constant.22.clone.1), dimensions={0}, to_apply=%region_3.4 | reduce | flops 1835008 | bytes 4718594 | tf_op jit(solution)/shard_map/reduce_sum | solution.py:224
  222.9 0.3 copy.20
  223.2 1.0 copy.21
  224.2 0.0 all-to-all-done.1
  224.2 5.1 %all-to-all-start.3 = ((bf16[128,4,512]{2,0,1:T(8,128)(2,1)}), bf16[128,4,512]{2,0,1:T(8,128)(2,1)S(1)}, u32[]{:S(2)}, u32[]{:S(2)}) async-start(bf16[128,4,512]{2,0,1:T(8,128)(2,1)} %copy.21), calls=%async_computation.3 | async-start | bytes 1048576 | tf_op jit(solution)/shard_map/all_to_all | solution.py:226
  229.3 40.1 %psum.7 = f32[1024,4]{0,1:T(4,128)S(1)} all-reduce(f32[1024,4]{0,1:T(4,128)S(1)} %broadcast_select_fusion), channel_id=1, replica_groups=mesh['dp'=8,'expert'=4] {'dp','expert'}, use_global_device_ids=true, to_apply=%region_6.7 | all-reduce | flops 4096 | bytes 32768 | tf_op jit(solution)/shard_map/psum | solution.py:204
  269.5 0.6 constant_dynamic-slice_fusion
  270.1 5.8 %convolution_bitcast_fusion = f32[1,352,2048]{2,1,0:T(8,128)} fusion(bf16[1024,352]{0,1:T(8,128)(2,1)} %copy-done.8, bf16[1024,2048]{1,0:T(8,128)(2,1)} %all-gather.5.cloned.1.call-done, f32[2048]{0:T(1024)S(1)} %bitcast.44, f32[1024]{0:T(1024)S(1)} %get-tuple-element.8), kind=kOutput, calls=%fused_computation.3 | convolution fusion | flops 1484783616 | bytes 7811072 | tf_op jit(solution)/shard_map/dot_general | solution.py:207
  275.9 0.7 reduce_sum.68
  276.6 0.0 all-to-all-done.3
  276.6 0.7 reduce_sum.70
  (3 shorter events, 0.0 us)
Async XLA Ops:
  7.2 80.9 %copy-start = (bf16[1,352,2048]{2,1,0:T(8,128)(2,1)S(1)}, bf16[1,352,2048]{2,1,0:T(8,128)(2,1)}, u32[]{:S(2)}) copy-start(bf16[1,352,2048]{2,1,0:T(8,128)(2,1)} %param.15) | copy-start | bytes 4325380
  7.2 42.3 %all-gather.3.cloned.1.call-start = ((), (), s32[]{:S(2)}) async-start(), calls=%async_computation.4 | async-start | bytes 4718592 | tf_op jit(solution)/shard_map/all_gather | solution.py:152
  7.9 80.1 %all-gather.5.cloned.1.call-start = ((), (), s32[]{:S(2)}) async-start(), calls=%async_computation.5 | async-start | bytes 4718592 | tf_op jit(solution)/shard_map/all_gather | solution.py:154
  48.1 6.9 %copy-start.1 = (bf16[1,352,2048]{2,1,0:T(8,128)(2,1)S(1)}, bf16[1,352,2048]{2,1,0:T(8,128)(2,1)}, u32[]{:S(2)}) copy-start(bf16[1,352,2048]{2,1,0:T(8,128)(2,1)} %param.13) | copy-start | bytes 4325380
  49.4 5.6 %copy-start.6 = (bf16[1024,2048]{1,0:T(8,128)(2,1)S(1)}, bf16[1024,2048]{1,0:T(8,128)(2,1)}, u32[]{:S(2)}) copy-start(bf16[1024,2048]{1,0:T(8,128)(2,1)} %all-gather.3.cloned.1.call-done) | copy-start | bytes 12582916
  94.7 4.4 %copy-start.8 = (bf16[1024,352]{0,1:T(8,128)(2,1)}, bf16[1024,352]{0,1:T(8,128)(2,1)S(1)}, u32[]{:S(2)}) copy-start(bf16[1024,352]{0,1:T(8,128)(2,1)S(1)} %get-tuple-element.7) | copy-start | bytes 2162692
  99.1 53.7 %all-to-all-start = ((bf16[8,128,2048]{2,1,0:T(8,128)(2,1)}), bf16[8,128,2048]{2,1,0:T(8,128)(2,1)}, u32[]{:S(2)}, u32[]{:S(2)}) async-start(bf16[8,128,2048]{2,1,0:T(8,128)(2,1)} %bitcast.39), calls=%async_computation | async-start | bytes 8388608 | tf_op jit(solution)/shard_map/all_to_all | solution.py:223
  103.8 3.7 %copy-start.2 = (bf16[1,352,2048]{2,1,0:T(8,128)(2,1)S(1)}, bf16[1,352,2048]{2,1,0:T(8,128)(2,1)}, u32[]{:S(2)}) copy-start(bf16[1,352,2048]{2,1,0:T(8,128)(2,1)} %param.14) | copy-start | bytes 4325380
  103.8 3.7 %copy-start.3 = (bf16[1024,352]{0,1:T(8,128)(2,1)S(1)}, bf16[1024,352]{0,1:T(8,128)(2,1)}, u32[]{:S(2)}) copy-start(bf16[1024,352]{0,1:T(8,128)(2,1)} %get-tuple-element.11) | copy-start | bytes 2162692
  152.8 53.7 %all-to-all-start.2 = ((bf16[8,128,2048]{2,1,0:T(8,128)(2,1)}), bf16[8,128,2048]{2,1,0:T(8,128)(2,1)}, u32[]{:S(2)}, u32[]{:S(2)}) async-start(bf16[8,128,2048]{2,1,0:T(8,128)(2,1)} %bitcast.38), calls=%async_computation.2 | async-start | bytes 8388608 | tf_op jit(solution)/shard_map/all_to_all | solution.py:223
  157.4 53.7 %copy-start.5 = (bf16[1024,352]{0,1:T(8,128)(2,1)S(1)}, bf16[1024,352]{0,1:T(8,128)(2,1)}, u32[]{:S(2)}) copy-start(bf16[1024,352]{0,1:T(8,128)(2,1)} %get-tuple-element.10) | copy-start | bytes 2162692
  206.5 17.7 %all-to-all-start.1 = ((bf16[128,4,512]{2,0,1:T(8,128)(2,1)}), bf16[128,4,512]{2,0,1:T(8,128)(2,1)S(1)}, u32[]{:S(2)}, u32[]{:S(2)}) async-start(bf16[128,4,512]{2,0,1:T(8,128)(2,1)} %copy.19), calls=%async_computation.1 | async-start | bytes 1048576 | tf_op jit(solution)/shard_map/all_to_all | solution.py:226
  211.1 5.6 %copy-start.4 = (bf16[1024,352]{0,1:T(8,128)(2,1)S(1)}, bf16[1024,352]{0,1:T(8,128)(2,1)}, u32[]{:S(2)}) copy-start(bf16[1024,352]{0,1:T(8,128)(2,1)} %get-tuple-element.11) | copy-start | bytes 2162692
  211.1 5.6 %copy-start.7 = (bf16[1024,2048]{1,0:T(8,128)(2,1)S(1)}, bf16[1024,2048]{1,0:T(8,128)(2,1)}, u32[]{:S(2)}) copy-start(bf16[1024,2048]{1,0:T(8,128)(2,1)} %all-gather.3.cloned.1.call-done) | copy-start | bytes 12582916
  224.2 52.4 %all-to-all-start.3 = ((bf16[128,4,512]{2,0,1:T(8,128)(2,1)}), bf16[128,4,512]{2,0,1:T(8,128)(2,1)S(1)}, u32[]{:S(2)}, u32[]{:S(2)}) async-start(bf16[128,4,512]{2,0,1:T(8,128)(2,1)} %copy.21), calls=%async_computation.3 | async-start | bytes 1048576 | tf_op jit(solution)/shard_map/all_to_all | solution.py:226
Sparse Core Ops, SparseCore 0:
  9.9 39.4 all-gather.2
  51.3 36.6 all-gather.4

commit v2 on v1

--- a/solution.py
+++ b/solution.py
@@ -149,11 +149,12 @@
     cotangent,
 ):
     me = lax.axis_index("dp")
-    arrived = lax.all_gather(tokens, "dp", axis=0, tiled=True)
-    cot_mine = lax.all_gather(cotangent, "expert", axis=1, tiled=True)
-    cot_all = lax.all_gather(cot_mine, "dp", axis=0, tiled=True)
-    experts = lax.all_gather(route_expert.astype(jnp.float32), "dp", axis=0, tiled=True)
-    weights = lax.all_gather(route_weight, "dp", axis=0, tiled=True)
+    choose = route_expert.shape[1]
+    routes = jnp.concatenate([route_expert.astype(jnp.float32), route_weight], axis=1)
+    arrived = gather_tokens(tokens)
+    routes = lax.all_gather(routes, "dp", axis=0, tiled=True)
+    cot_all = gather_tokens(gather_columns(cotangent))
+    experts, weights = routes[:, :choose], routes[:, choose:]
     chosen = experts == me.astype(jnp.float32)
     row_weight = jnp.sum(jnp.where(chosen, weights, 0.0), axis=1, keepdims=True)
     gate_local, up_local, down_local = gate_weight[0], up_weight[0], down_weight[0]
@@ -201,9 +202,7 @@
     route_row = jnp.sum(hidden.astype(jnp.float32) * hidden_grad, axis=1, keepdims=True)
     route_row = route_row / jnp.where(row_weight > 0.0, row_weight, 1.0)
     route_part = jnp.where(chosen, route_row, 0.0)
-    route_sum = lax.psum(route_part, ("dp", "expert"))
-    rows = tokens.shape[0]
-    route_grad = lax.dynamic_slice_in_dim(route_sum, me * rows, rows, 0)
+    route_grad = sum_shares(sum_tokens(route_part.reshape(-1, tokens.shape[0], choose)))
     down_grad = lax.dot_general(
         hidden, out_grad, (((0,), (0,)), ((), ())), preferred_element_type=jnp.float32
     )
@@ -216,21 +215,103 @@
     return (mixed, token_grad, route_grad, gate_grad[None], up_grad[None], down_grad[None])
 
 
+def swap(block, bit):
+    owners = lax.axis_size("dp")
+    return lax.ppermute(block, "dp", [(i, i ^ bit) for i in range(owners)])
+
+
+def bits():
+    owners = lax.axis_size("dp")
+    return [1 << i for i in range(owners.bit_length() - 1)]
+
+
+def orders():
+    upper = bits()[1:]
+    return (upper, upper[::-1])
+
+
+def in_order(block, bit):
+    other = swap(block, bit)
+    first = (lax.axis_index("dp") & bit) == 0
+    return jnp.where(first, block, other), jnp.where(first, other, block)
+
+
+def gather_tokens(mine):
+    rows, width = mine.shape
+    upper = bits()[1:]
+    halves = []
+    for order, half in zip(orders(), jnp.split(mine, 2, axis=1)):
+        block = half.reshape((1,) * len(upper) + half.shape)
+        for bit in order:
+            axis = len(upper) - 1 - upper.index(bit)
+            block = jnp.concatenate(in_order(block, bit), axis=axis)
+        halves.append(block.reshape(-1, rows, width // 2))
+    both = [jnp.stack(in_order(half, bits()[0]), axis=1) for half in halves]
+    return jnp.concatenate(both, axis=-1).reshape(-1, width)
+
+
+def shift(block, by):
+    shares = lax.axis_size("expert")
+    return lax.ppermute(block, "expert", [(i, (i + by) % shares) for i in range(shares)])
+
+
+def gather_columns(mine):
+    shares, me = lax.axis_size("expert"), lax.axis_index("expert")
+    width = mine.shape[1]
+    out = jnp.zeros((mine.shape[0], shares * width), mine.dtype)
+    for by in range(shares):
+        block = mine if by == 0 else shift(mine, by)
+        source = lax.rem(me - by + shares, shares)
+        out = lax.dynamic_update_slice_in_dim(out, block, source * width, 1)
+    return out
+
+
+def sum_shares(mine):
+    return sum([shift(mine, by) for by in range(1, lax.axis_size("expert"))], mine)
+
+
+def add_wide(a, b):
+    return (a.astype(jnp.float32) + b.astype(jnp.float32)).astype(a.dtype)
+
+
+def halve(block, axis, bit):
+    own = (lax.axis_index("dp") & bit) // bit
+    keep = lax.dynamic_index_in_dim(block, own, axis, keepdims=True)
+    give = lax.dynamic_index_in_dim(block, 1 - own, axis, keepdims=True)
+    return add_wide(keep, swap(give, bit))
+
+
+def sum_tokens(blocks):
+    count = len(bits())
+    shape = blocks.shape[1:]
+    block = blocks.reshape((2,) * count + shape)
+    block = halve(block, count - 1, bits()[0])
+    parts = jnp.split(block, 2, axis=-1)
+    done = []
+    for order, part in zip(orders(), parts):
+        for bit in order:
+            part = halve(part, count - 1 - bits().index(bit), bit)
+        done.append(part.reshape(shape[0], -1))
+    return jnp.concatenate(done, axis=1)
+
+
 def reduce_home(part):
-    rows, width = part.shape
     owners, shares = lax.axis_size("dp"), lax.axis_size("expert")
-    blocks = part.reshape(owners, rows // owners, width)
-    blocks = lax.all_to_all(blocks, "dp", split_axis=0, concat_axis=0, tiled=True)
-    home = jnp.sum(blocks.astype(jnp.float32), axis=0).astype(jnp.bfloat16)
-    cols = home.reshape(rows // owners, shares, width // shares)
-    cols = lax.all_to_all(cols, "expert", split_axis=1, concat_axis=1, tiled=True)
-    return jnp.sum(cols.astype(jnp.float32), axis=1).astype(jnp.bfloat16)
+    home = sum_tokens(part.reshape(owners, -1, part.shape[1]))
+    me = lax.axis_index("expert")
+    width = part.shape[1] // shares
+    total = lax.dynamic_slice_in_dim(home, me * width, width, 1).astype(jnp.float32)
+    for by in range(1, shares):
+        target = lax.rem(me + by, shares)
+        sent = lax.dynamic_slice_in_dim(home, target * width, width, 1)
+        total = total + shift(sent, by).astype(jnp.float32)
+    return total.astype(jnp.bfloat16)
 
 
 def local(tokens, route_expert, *rest):
     owners = lax.axis_size("dp")
     rows, choose = route_expert.shape
-    full = 2 * rows * choose >= owners * rows
+    full = 2 * rows * choose >= owners * rows and owners & (owners - 1) == 0
     return (dense if full else routed)(tokens, route_expert, *rest)
 
 

time: 285 us -> 168 us (0.59)
  waiting for transfers between devices: 118 us -> 43.6 us
  blocking collectives: 77.3 us -> 23.3 us
  starting transfers between devices: 19.1 us -> 44.3 us
  matrix products: 42.2 us -> 24.6 us
  between operations: 14.2 us -> 1.26 us
  other arithmetic: 9.58 us -> 18.2 us
  local copies, waits for them, and re-layouts: 4.04 us -> 12.6 us
    all_to_all x4 -> x0, waiting for transfers between devices: 85.6 us -> none  [the longest x2 85.6 us: reduce_home(): lax.all_to_all(blocks, 'dp', split_axis=0, concat_axis=0, tiled=True)]
    ppermute x0 -> x39, starting transfers between devices: none -> 44.3 us  [the longest x27 24.4 us: swap(): return lax.ppermute(block, 'dp', [(i, i ^ bit) for i in range(owners)])]
    ppermute x0 -> x39, waiting for transfers between devices: none -> 43.6 us  [the longest x27 32.4 us: swap(): return lax.ppermute(block, 'dp', [(i, i ^ bit) for i in range(owners)])]
    psum x1 -> x0, blocking collectives: 40.1 us -> none  [dense(): route_sum = lax.psum(route_part, ('dp', 'expert'))]
    all_gather x2 -> x0, waiting for transfers between devices: 31.5 us -> none  [the longest x1 30.2 us: dense(): cot_all = lax.all_gather(cot_mine, 'dp', axis=0, tiled=True)]
    all_to_all x4 -> x0, starting transfers between devices: 19.1 us -> none  [the longest x2 9.69 us: reduce_home(): lax.all_to_all(cols, 'expert', split_axis=1, concat_axis=1, tiled=True)]
    all_gather x3 -> x1, blocking collectives: 37.2 us -> 23.3 us  [dense(): routes = lax.all_gather(routes, 'dp', axis=0, tiled=True)]
    convert_element_type x0 -> x10, other arithmetic: none -> 9.45 us  [the longest x1 4.2 us: dense(): (cot_all.astype(jnp.float32) * row_weight * scale).astype(jnp.bfloat16)]
  transfers between devices with their start and end apart: 6 -> 39, of which waited for: 4 -> 17; matrix products, arithmetic and copies ran while one was open for 15% -> 16% of each run, Pallas kernels for 0% -> 0%
where the time goes in v2:
time: 168 us
  starting transfers between devices  44.3 us (26%)
  waiting for transfers between devices  43.6 us (26%)
  matrix products  24.6 us (15%)
  blocking collectives  23.3 us (14%)
  other arithmetic  18.2 us (11%)
  local copies, waits for them, and re-layouts  12.6 us (8%)
    ppermute x27, waiting for transfers between devices, swap(): return lax.ppermute(block, 'dp', [(i, i ^ bit) for i in range(owners)])  32.4 us
    ppermute x27, starting transfers between devices, swap(): return lax.ppermute(block, 'dp', [(i, i ^ bit) for i in range(owners)])  24.4 us
    all_gather x1, blocking collectives, dense(): routes = lax.all_gather(routes, 'dp', axis=0, tiled=True)  23.3 us
    ppermute x12, starting transfers between devices, shift(): lax.ppermute(block, 'expert', [(i, (i + by) % shares) for i in range(shar...  19.9 us
    ppermute x12, waiting for transfers between devices, shift(): lax.ppermute(block, 'expert', [(i, (i + by) % shares) for i in range(shar...  11.1 us
    convert_element_type x1, other arithmetic, dense(): (cot_all.astype(jnp.float32) * row_weight * scale).astype(jnp.bfloat16)  4.2 us
    convert_element_type x1, local copies, waits for them, and re-layouts, dense(): cot_all.astype(jnp.float32) * row_weight * scale  3.89 us
    dot_general x1, matrix products, dense(): lax.dot_general(arrived, up_local, (((1,), (1,)), ((), ())), preferred_el...  3.61 us
  transfers between devices with their start and end apart: 39, of which 17 were waited for; matrix products, arithmetic and copies ran while one was open for 16% of the time, Pallas kernels for 0%

profile of v2, /device:TPU:0, one launch (start us, length us, event | category | flops | bytes accessed | tf_op | source)
XLA Modules:
  0.0 167.8 jit_solution(14379830535601755931)
XLA Ops:
  0.7 3.1 %collective-permute-start.14 = (bf16[128,512]{1,0:T(8,128)(2,1)}, bf16[128,512]{1,0:T(8,128)(2,1)}, u32[]{:S(2)}, u32[]{:S(2)}) collective-permute-start(bf16[128,512]{1,0:T(8,128)(2,1)} %param.19), channel_id=1, source_target_pairs={{0,1},{1,2},{2,3},{3,0},{4,5},{5,6},{6,7},{7,4},{8,9},{9,10},{10,1... | collective-permute-start | bytes 393224 | tf_op jit(solution)/shard_map/ppermute | solution.py:255
  3.7 2.6 %collective-permute-start.15 = (bf16[128,512]{1,0:T(8,128)(2,1)}, bf16[128,512]{1,0:T(8,128)(2,1)S(1)}, u32[]{:S(2)}, u32[]{:S(2)}) collective-permute-start(bf16[128,512]{1,0:T(8,128)(2,1)} %param.19), channel_id=1, source_target_pairs={{0,2},{1,3},{2,0},{3,1},{4,6},{5,7},{6,4},{7,5},{8,10},{9,11},{10,... | collective-permute-start | bytes 393224 | tf_op jit(solution)/shard_map/ppermute | solution.py:255
  6.3 1.3 collective-permute-start.16
  7.7 1.1 slice_bitcast_fusion.3
  8.7 1.6 collective-permute-start
  10.3 1.5 collective-permute-start.3
  11.9 0.9 constant_dynamic-update-slice_fusion.3
  12.8 0.9 constant_dynamic-update-slice_fusion.2
  13.8 1.4 collective-permute-done.15
  15.3 1.6 collective-permute-start.17
  16.8 1.5 collective-permute-start.20
  18.4 0.7 copy-done.6
  19.1 1.1 broadcast_select_fusion.15
  20.2 0.8 pad_maximum_fusion.7
  21.5 1.9 %collective-permute-done.17 = bf16[1,1,128,1024]{3,2,1,0:T(8,128)(2,1)S(1)} collective-permute-done((bf16[1,1,128,1024]{3,2,1,0:T(8,128)(2,1)S(1)}, bf16[1,1,128,1024]{3,2,1,0:T(8,128)(2,1)S(1)}, u32[]{:S(2)}, u32[]{:S(2)}) %collective-permute-start.17) | collective-permute-done | bytes 262176 | tf_op jit(solution)/shard_map/ppermute | solution.py:220
  23.5 2.6 %collective-permute-done.20 = bf16[1,1,128,1024]{3,2,1,0:T(8,128)(2,1)S(1)} collective-permute-done((bf16[1,1,128,1024]{3,2,1,0:T(8,128)(2,1)S(1)}, bf16[1,1,128,1024]{3,2,1,0:T(8,128)(2,1)S(1)}, u32[]{:S(2)}, u32[]{:S(2)}) %collective-permute-start.20) | collective-permute-done | bytes 262176 | tf_op jit(solution)/shard_map/ppermute | solution.py:220
  26.8 0.8 pad_maximum_fusion.9
  27.7 1.5 collective-permute-start.18
  29.2 0.7 reduce.1
  30.7 1.6 collective-permute-start.21
  32.2 23.3 %all_gather.3 = f32[1024,8]{0,1:T(8,128)S(1)} all-gather(f32[128,8]{0,1:T(8,128)S(1)} %pad_maximum_fusion.11), channel_id=1, replica_groups=mesh['dp'=8,'expert'=4] {'dp'}, dimensions={0}, use_global_device_ids=true | all-gather | bytes 36864 | tf_op jit(solution)/shard_map/all_gather | solution.py:155
  55.5 1.3 broadcast_select_fusion.5
  57.9 0.8 constant_dynamic-slice_fusion.20
  59.9 1.3 collective-permute-done.22
  62.9 1.1 maximum_convert_fusion
  64.9 0.8 copy-done.4
  65.8 1.7 %convolution_multiply_fusion.1 = f32[1024,352]{0,1:T(8,128)S(1)} fusion(bf16[1024,2048]{1,0:T(8,128)(2,1)S(1)} %bitcast.121, bf16[1,352,2048]{2,1,0:T(8,128)(2,1)S(1)} %copy-done.4, f32[352]{0:T(512)S(1)} %reduce), kind=kOutput, calls=%fused_computation.23 | convolution fusion | flops 1476755456 | bytes 7079296 | tf_op jit(solution)/shard_map/dot_general | solution.py:163
  67.5 1.8 %fusion.2 = f32[1024,352]{0,1:T(8,128)S(1)} fusion(bf16[1024,1024]{1,0:T(8,128)(2,1)S(1)} %bitcast.126, bf16[1024,1024]{1,0:T(8,128)(2,1)S(1)} %bitcast.125, f32[2048]{0:T(1024)S(1)} %bitcast.129, f32[1024]{0:T(1024)S(1)} %get-tuple-element.8, bf16[1,352,2048]{2,1,0:T(8,128)(2,1)S(1)} %copy-done.10), kind=kOutput, calls=%fused_computation.6 | convolution fusion | flops 1491075072 | bytes 7090176 | tf_op jit(solution)/shard_map/dot_general | solution.py:186
  69.3 3.6 %multiply_reduce_fusion = (f32[1024]{0:T(1024)S(1)}, bf16[1024,352]{0,1:T(8,128)(2,1)}, bf16[1024,352]{0,1:T(8,128)(2,1)S(1)}, bf16[1024,352]{0,1:T(8,128)(2,1)}) fusion(f32[1024,352]{0,1:T(8,128)S(1)} %fusion.2, f32[1024,352]{0,1:T(8,128)S(1)} %convolution_multiply_fusion.1, f32[352]{0:T(512)S(1)} %reduce, f32[352]{0:T(512)S(1)} %reduce.1, ...), kind=kOutput, calls=%fused_computation.31 | convolution fusion | flops 1483963392 | bytes 10689280 | tf_op jit(solution)/shard_map/dot_general | solution.py:169
  73.0 3.3 %convolution_bitcast_fusion.2 = f32[1,352,2048]{2,1,0:T(8,128)} fusion(bf16[1024,352]{0,1:T(8,128)(2,1)S(1)} %get-tuple-element.10, bf16[1024,2048]{1,0:T(8,128)(2,1)S(1)} %bitcast.123), kind=kOutput, calls=%fused_computation.18 | convolution fusion | flops 1476395008 | bytes 7798784 | tf_op jit(solution)/shard_map/dot_general | solution.py:209
  76.2 2.4 %fusion.12 = f32[1024,2048]{1,0:T(8,128)S(1)} fusion(bf16[1024,352]{0,1:T(8,128)(2,1)S(1)} %get-tuple-element.10, bf16[1,352,2048]{2,1,0:T(8,128)(2,1)S(1)} %copy-done.4), kind=kOutput, calls=%fused_computation.28 | convolution fusion | flops 1476395008 | bytes 10551296 | tf_op jit(solution)/shard_map/dot_general | solution.py:194
  78.6 3.9 %copy.23 = f32[4,2,128,2048]{3,2,1,0:T(8,128)} copy(f32[4,2,128,2048]{3,2,0,1:T(8,128)S(1)} %maximum_convert_fusion) | data formatting | bytes 16777216 | tf_op jit(solution)/shard_map/convert_element_type | solution.py:185
  82.5 4.2 %fusion.1 = bf16[1024,2048]{1,0:T(8,128)(2,1)S(1)} fusion(f32[4,2,128,2048]{3,2,1,0:T(8,128)} %copy.23, f32[2048]{0:T(1024)S(1)} %bitcast.130, f32[1024]{0:T(1024)S(1)} %get-tuple-element.8), kind=kLoop, calls=%fused_computation.2 | loop fusion | flops 6291456 | bytes 12595200 | tf_op jit(solution)/shard_map/convert_element_type | solution.py:185
  86.7 3.3 %convolution_bitcast_fusion.1 = f32[1,352,2048]{2,1,0:T(8,128)} fusion(bf16[1024,352]{0,1:T(8,128)(2,1)S(1)} %copy-done.5, bf16[1024,2048]{1,0:T(8,128)(2,1)S(1)} %bitcast.124), kind=kOutput, calls=%fused_computation.17 | convolution fusion | flops 1476395008 | bytes 7798784 | tf_op jit(solution)/shard_map/dot_general | solution.py:212
  90.4 2.8 %add_convert_fusion = bf16[1024,2048]{1,0:T(8,128)(2,1)S(1)} fusion(f32[1024,2048]{1,0:T(8,128)S(1)} %fusion.12, bf16[1024,352]{0,1:T(8,128)(2,1)S(1)} %copy-done.5, bf16[1,352,2048]{2,1,0:T(8,128)(2,1)S(1)} %copy-done), kind=kOutput, calls=%fused_computation.3 | convolution fusion | flops 1480589312 | bytes 14745600 | tf_op jit(solution)/shard_map/dot_general | solution.py:197
  93.8 0.8 copy-done.11
  94.8 2.4 %multiply_convert_fusion.1 = bf16[1024,2048]{1,0:T(8,128)(2,1)S(1)} fusion(bf16[1024,352]{0,1:T(8,128)(2,1)S(1)} %copy-done.12, f32[2048]{0:T(1024)S(1)} %bitcast.131, f32[1024]{0:T(1024)S(1)} %get-tuple-element.8, bf16[1,352,2048]{2,1,0:T(8,128)(2,1)S(1)} %copy-done.11), kind=kOutput, calls=%fused_computation.5 | convolution fusion | flops 1482686464 | bytes 6369280 | tf_op jit(solution)/shard_map/dot_general | solution.py:178
  97.8 1.5 collective-permute-start.32
  99.8 1.6 collective-permute-done.32
  101.9 0.9 collective-permute-done.34
  103.4 1.5 collective-permute-done.33
  105.0 1.4 collective-permute-done.35
  106.4 3.5 %collective-permute-start.36 = (f32[128,4]{0,1:T(4,128)S(1)}, f32[128,4]{0,1:T(4,128)S(1)}, u32[]{:S(2)}, u32[]{:S(2)}) collective-permute-start(f32[128,4]{0,1:T(4,128)S(1)} %pad_maximum_fusion.12), channel_id=1, source_target_pairs={{0,1},{1,2},{2,3},{3,0},{4,5},{5,6},{6,7},{7,4},{8,9},{9,10},{10,1... | collective-permute-start | bytes 6152 | tf_op jit(solution)/shard_map/ppermute | solution.py:255
  109.9 2.4 %collective-permute-start.38 = (f32[128,4]{0,1:T(4,128)S(1)}, f32[128,4]{0,1:T(4,128)S(1)}, u32[]{:S(2)}, u32[]{:S(2)}) collective-permute-start(f32[128,4]{0,1:T(4,128)S(1)} %pad_maximum_fusion.12), channel_id=1, source_target_pairs={{0,3},{1,0},{2,1},{3,2},{4,7},{5,4},{6,5},{7,6},{8,11},{9,8},{10,9... | collective-permute-start | bytes 6152 | tf_op jit(solution)/shard_map/ppermute | solution.py:255
  112.4 3.3 %convolution_bitcast_fusion = f32[1,352,2048]{2,1,0:T(8,128)} fusion(bf16[1024,352]{0,1:T(8,128)(2,1)S(1)} %copy-done.12, bf16[1024,2048]{1,0:T(8,128)(2,1)S(1)} %fusion.1), kind=kOutput, calls=%fused_computation.16 | convolution fusion | flops 1476395008 | bytes 7798784 | tf_op jit(solution)/shard_map/dot_general | solution.py:206
  116.2 0.9 add_convert_fusion.1
  117.4 0.7 collective-permute-start.26
  118.2 1.5 collective-permute-start.24
  119.7 0.9 add_convert_fusion.2
  121.5 1.5 collective-permute-start.7
  123.0 9.4 %collective-permute-done.26 = bf16[1,2,1,128,1024]{4,3,2,1,0:T(8,128)(2,1)S(1)} collective-permute-done((bf16[1,2,1,128,1024]{4,3,2,1,0:T(8,128)(2,1)S(1)}, bf16[1,2,1,128,1024]{4,3,2,1,0:T(8,128)(2,1)S(1)}, u32[]{:S(2)}, u32[]{:S(2)}) %collective-permute-start.26) | collective-permute-done | bytes 524320 | tf_op jit(solution)/shard_map/ppermute | solution.py:220
  133.5 1.6 collective-permute-start.25
  135.1 8.5 %collective-permute-done.9 = bf16[1,2,1,128,1024]{4,3,2,1,0:T(8,128)(2,1)S(1)} collective-permute-done((bf16[1,2,1,128,1024]{4,3,2,1,0:T(8,128)(2,1)S(1)}, bf16[1,2,1,128,1024]{4,3,2,1,0:T(8,128)(2,1)S(1)}, u32[]{:S(2)}, u32[]{:S(2)}) %collective-permute-start.9) | collective-permute-done | bytes 524320 | tf_op jit(solution)/shard_map/ppermute | solution.py:220
  144.8 1.6 collective-permute-start.8
  146.3 2.4 %collective-permute-done.27 = bf16[1,1,1,128,1024]{4,3,2,1,0:T(8,128)(2,1)S(1)} collective-permute-done((bf16[1,1,1,128,1024]{4,3,2,1,0:T(8,128)(2,1)S(1)}, bf16[1,1,1,128,1024]{4,3,2,1,0:T(8,128)(2,1)S(1)}, u32[]{:S(2)}, u32[]{:S(2)}) %collective-permute-start.27) | collective-permute-done | bytes 262176 | tf_op jit(solution)/shard_map/ppermute | solution.py:220
  149.2 2.2 %collective-permute-start.29 = (bf16[128,512]{1,0:T(8,128)(2,1)S(1)}, bf16[128,512]{1,0:T(8,128)(2,1)S(1)}, u32[]{:S(2)}, u32[]{:S(2)}) collective-permute-start(bf16[128,512]{1,0:T(8,128)(2,1)S(1)} %get-tuple-element.41), channel_id=1, source_target_pairs={{0,2},{1,3},{2,0},{3,1},{4,6},{5,7},{6,4},{7,5},{8,10},{9,11},{10,... | collective-permute-start | bytes 393224 | tf_op jit(solution)/shard_map/ppermute | solution.py:255
  151.4 1.6 collective-permute-start.30
  154.0 1.5 collective-permute-start.12
  155.6 1.9 %collective-permute-done.28 = bf16[128,512]{1,0:T(8,128)(2,1)S(1)} collective-permute-done((bf16[128,512]{1,0:T(8,128)(2,1)S(1)}, bf16[128,512]{1,0:T(8,128)(2,1)S(1)}, u32[]{:S(2)}, u32[]{:S(2)}) %collective-permute-start.28) | collective-permute-done | bytes 131104 | tf_op jit(solution)/shard_map/ppermute | solution.py:255
  157.4 1.0 collective-permute-start.13
  158.4 5.4 %collective-permute-done.29 = bf16[128,512]{1,0:T(8,128)(2,1)S(1)} collective-permute-done((bf16[128,512]{1,0:T(8,128)(2,1)S(1)}, bf16[128,512]{1,0:T(8,128)(2,1)S(1)}, u32[]{:S(2)}, u32[]{:S(2)}) %collective-permute-start.29) | collective-permute-done | bytes 131104 | tf_op jit(solution)/shard_map/ppermute | solution.py:255
  163.8 0.8 add_convert_fusion.11
  164.6 2.4 %collective-permute-done.12 = bf16[128,512]{1,0:T(8,128)(2,1)S(1)} collective-permute-done((bf16[128,512]{1,0:T(8,128)(2,1)S(1)}, bf16[128,512]{1,0:T(8,128)(2,1)S(1)}, u32[]{:S(2)}, u32[]{:S(2)}) %collective-permute-start.12) | collective-permute-done | bytes 131104 | tf_op jit(solution)/shard_map/ppermute | solution.py:255
  167.0 0.8 add_convert_fusion.12
  (128 shorter events, 15.6 us)
Async XLA Ops:
  0.6 68.7 %copy-start = (bf16[1,352,2048]{2,1,0:T(8,128)(2,1)S(1)}, bf16[1,352,2048]{2,1,0:T(8,128)(2,1)}, u32[]{:S(2)}) copy-start(bf16[1,352,2048]{2,1,0:T(8,128)(2,1)} %param.14) | copy-start | bytes 4325380
  0.6 18.4 %copy-start.3 = (bf16[128,2048]{1,0:T(8,128)(2,1)S(1)}, bf16[128,2048]{1,0:T(8,128)(2,1)}, u32[]{:S(2)}) copy-start(bf16[128,2048]{1,0:T(8,128)(2,1)} %param.10) | copy-start | bytes 1572868
  0.7 12.2 %collective-permute-start.14 = (bf16[128,512]{1,0:T(8,128)(2,1)}, bf16[128,512]{1,0:T(8,128)(2,1)}, u32[]{:S(2)}, u32[]{:S(2)}) collective-permute-start(bf16[128,512]{1,0:T(8,128)(2,1)} %param.19), channel_id=1, source_target_pairs={{0,1},{1,2},{2,3},{3,0},{4,5},{5,6},{6,7},{7,4},{8,9},{9,10},{10,1... | collective-permute-start | bytes 393224 | tf_op jit(solution)/shard_map/ppermute | solution.py:255
  3.7 11.4 %collective-permute-start.15 = (bf16[128,512]{1,0:T(8,128)(2,1)}, bf16[128,512]{1,0:T(8,128)(2,1)S(1)}, u32[]{:S(2)}, u32[]{:S(2)}) collective-permute-start(bf16[128,512]{1,0:T(8,128)(2,1)} %param.19), channel_id=1, source_target_pairs={{0,2},{1,3},{2,0},{3,1},{4,6},{5,7},{6,4},{7,5},{8,10},{9,11},{10,... | collective-permute-start | bytes 393224 | tf_op jit(solution)/shard_map/ppermute | solution.py:255
  6.3 8.9 %collective-permute-start.16 = (bf16[128,512]{1,0:T(8,128)(2,1)}, bf16[128,512]{1,0:T(8,128)(2,1)S(1)}, u32[]{:S(2)}, u32[]{:S(2)}) collective-permute-start(bf16[128,512]{1,0:T(8,128)(2,1)} %param.19), channel_id=1, source_target_pairs={{0,3},{1,0},{2,1},{3,2},{4,7},{5,4},{6,5},{7,6},{8,11},{9,8},{10,9... | collective-permute-start | bytes 393224 | tf_op jit(solution)/shard_map/ppermute | solution.py:255
  8.7 9.6 %collective-permute-start = (bf16[1,1,128,1024]{3,2,1,0:T(8,128)(2,1)S(1)}, bf16[1,1,128,1024]{3,2,1,0:T(8,128)(2,1)S(1)}, u32[]{:S(2)}, u32[]{:S(2)}) collective-permute-start(bf16[1,1,128,1024]{3,2,1,0:T(8,128)(2,1)S(1)} %get-tuple-element.48), channel_id=1, source_target_pairs={{0,8},{4,12},{8,0},{12,4},{16,24},{20,28},{24,16},{28,20},{1,9},{5... | collective-permute-start | bytes 786440 | tf_op jit(solution)/shard_map/ppermute | solution.py:220
  10.3 8.8 %collective-permute-start.3 = (bf16[1,1,128,1024]{3,2,1,0:T(8,128)(2,1)S(1)}, bf16[1,1,128,1024]{3,2,1,0:T(8,128)(2,1)}, u32[]{:S(2)}, u32[]{:S(2)}) collective-permute-start(bf16[1,1,128,1024]{3,2,1,0:T(8,128)(2,1)S(1)} %get-tuple-element.49), channel_id=1, source_target_pairs={{0,16},{4,20},{8,24},{12,28},{16,0},{20,4},{24,8},{28,12},{1,17},{... | collective-permute-start | bytes 786440 | tf_op jit(solution)/shard_map/ppermute | solution.py:220
  15.3 8.2 %collective-permute-start.17 = (bf16[1,1,128,1024]{3,2,1,0:T(8,128)(2,1)S(1)}, bf16[1,1,128,1024]{3,2,1,0:T(8,128)(2,1)S(1)}, u32[]{:S(2)}, u32[]{:S(2)}) collective-permute-start(bf16[1,1,128,1024]{3,2,1,0:T(8,128)(2,1)S(1)} %get-tuple-element.52), channel_id=1, source_target_pairs={{0,8},{4,12},{8,0},{12,4},{16,24},{20,28},{24,16},{28,20},{1,9},{5... | collective-permute-start | bytes 786440 | tf_op jit(solution)/shard_map/ppermute | solution.py:220
  16.8 12.4 %copy-start.7 = (s32[128,4]{0,1:T(4,128)S(1)}, s32[128,4]{0,1:T(4,128)}, u32[]{:S(2)}) copy-start(s32[128,4]{0,1:T(4,128)} %param.11) | copy-start | bytes 6148
  16.8 12.4 %copy-start.9 = (f32[1,352]{1,0:T(1,128)S(1)}, f32[1,352]{1,0:T(1,128)}, u32[]{:S(2)}) copy-start(f32[1,352]{1,0:T(1,128)} %param.16) | copy-start | bytes 4228
  16.8 9.2 %collective-permute-start.20 = (bf16[1,1,128,1024]{3,2,1,0:T(8,128)(2,1)S(1)}, bf16[1,1,128,1024]{3,2,1,0:T(8,128)(2,1)S(1)}, u32[]{:S(2)}, u32[]{:S(2)}) collective-permute-start(bf16[1,1,128,1024]{3,2,1,0:T(8,128)(2,1)S(1)} %get-tuple-element.53), channel_id=1, source_target_pairs={{0,16},{4,20},{8,24},{12,28},{16,0},{20,4},{24,8},{28,12},{1,17},{... | collective-permute-start | bytes 786440 | tf_op jit(solution)/shard_map/ppermute | solution.py:220
  18.4 0.7 copy-start.6
  21.0 11.2 %copy-start.8 = (f32[128,4]{0,1:T(4,128)S(1)}, f32[128,4]{0,1:T(4,128)}, u32[]{:S(2)}) copy-start(f32[128,4]{0,1:T(4,128)} %param.12) | copy-start | bytes 6148
  21.0 34.5 %collective-permute-start.1 = (bf16[1,2,128,1024]{3,2,1,0:T(8,128)(2,1)}, bf16[1,2,128,1024]{3,2,1,0:T(8,128)(2,1)}, u32[]{:S(2)}, u32[]{:S(2)}) collective-permute-start(bf16[1,2,128,1024]{3,2,1,0:T(8,128)(2,1)} %pad_maximum_fusion.7), channel_id=1, source_target_pairs={{0,16},{4,20},{8,24},{12,28},{16,0},{20,4},{24,8},{28,12},{1,17},{... | collective-permute-start | bytes 1572872 | tf_op jit(solution)/shard_map/ppermute | solution.py:220
  26.1 0.7 copy-start.1
  26.1 1.5 copy-start.2
  27.7 27.9 %collective-permute-start.18 = (bf16[1,2,128,1024]{3,2,1,0:T(8,128)(2,1)}, bf16[1,2,128,1024]{3,2,1,0:T(8,128)(2,1)S(1)}, u32[]{:S(2)}, u32[]{:S(2)}) collective-permute-start(bf16[1,2,128,1024]{3,2,1,0:T(8,128)(2,1)} %pad_maximum_fusion.9), channel_id=1, source_target_pairs={{0,16},{4,20},{8,24},{12,28},{16,0},{20,4},{24,8},{28,12},{1,17},{... | collective-permute-start | bytes 1572872 | tf_op jit(solution)/shard_map/ppermute | solution.py:220
  30.0 27.4 %collective-permute-start.4 = (bf16[2,1,128,1024]{3,2,1,0:T(8,128)(2,1)S(1)}, bf16[2,1,128,1024]{3,2,1,0:T(8,128)(2,1)S(1)}, u32[]{:S(2)}, u32[]{:S(2)}) collective-permute-start(bf16[2,1,128,1024]{3,2,1,0:T(8,128)(2,1)S(1)} %pad_maximum_fusion.8), channel_id=1, source_target_pairs={{0,8},{4,12},{8,0},{12,4},{16,24},{20,28},{24,16},{28,20},{1,9},{5... | collective-permute-start | bytes 1572872 | tf_op jit(solution)/shard_map/ppermute | solution.py:220
  30.7 26.7 %collective-permute-start.21 = (bf16[2,1,128,1024]{3,2,1,0:T(8,128)(2,1)S(1)}, bf16[2,1,128,1024]{3,2,1,0:T(8,128)(2,1)S(1)}, u32[]{:S(2)}, u32[]{:S(2)}) collective-permute-start(bf16[2,1,128,1024]{3,2,1,0:T(8,128)(2,1)S(1)} %pad_maximum_fusion.10), channel_id=1, source_target_pairs={{0,8},{4,12},{8,0},{12,4},{16,24},{20,28},{24,16},{28,20},{1,9},{5... | collective-permute-start | bytes 1572872 | tf_op jit(solution)/shard_map/ppermute | solution.py:220
  57.0 2.7 %collective-permute-start.19 = (bf16[4,128,1024]{2,1,0:T(8,128)(2,1)S(1)}, bf16[4,128,1024]{2,1,0:T(8,128)(2,1)S(1)}, u32[]{:S(2)}, u32[]{:S(2)}) collective-permute-start(bf16[4,128,1024]{2,1,0:T(8,128)(2,1)S(1)} %bitcast.117), channel_id=1, source_target_pairs={{0,4},{4,0},{8,12},{12,8},{16,20},{20,16},{24,28},{28,24},{1,5},{5... | collective-permute-start | bytes 3145736 | tf_op jit(solution)/shard_map/ppermute | solution.py:220
  57.7 3.5 %collective-permute-start.22 = (bf16[4,128,1024]{2,1,0:T(8,128)(2,1)S(1)}, bf16[4,128,1024]{2,1,0:T(8,128)(2,1)S(1)}, u32[]{:S(2)}, u32[]{:S(2)}) collective-permute-start(bf16[4,128,1024]{2,1,0:T(8,128)(2,1)S(1)} %bitcast.120), channel_id=1, source_target_pairs={{0,4},{4,0},{8,12},{12,8},{16,20},{20,16},{24,28},{28,24},{1,5},{5... | collective-permute-start | bytes 3145736 | tf_op jit(solution)/shard_map/ppermute | solution.py:220
  58.9 3.8 %collective-permute-start.2 = (bf16[4,128,1024]{2,1,0:T(8,128)(2,1)S(1)}, bf16[4,128,1024]{2,1,0:T(8,128)(2,1)S(1)}, u32[]{:S(2)}, u32[]{:S(2)}) collective-permute-start(bf16[4,128,1024]{2,1,0:T(8,128)(2,1)S(1)} %bitcast.119), channel_id=1, source_target_pairs={{0,4},{4,0},{8,12},{12,8},{16,20},{20,16},{24,28},{28,24},{1,5},{5... | collective-permute-start | bytes 3145736 | tf_op jit(solution)/shard_map/ppermute | solution.py:220
  59.4 4.8 %collective-permute-start.5 = (bf16[4,128,1024]{2,1,0:T(8,128)(2,1)S(1)}, bf16[4,128,1024]{2,1,0:T(8,128)(2,1)S(1)}, u32[]{:S(2)}, u32[]{:S(2)}) collective-permute-start(bf16[4,128,1024]{2,1,0:T(8,128)(2,1)S(1)} %bitcast.118), channel_id=1, source_target_pairs={{0,4},{4,0},{8,12},{12,8},{16,20},{20,16},{24,28},{28,24},{1,5},{5... | collective-permute-start | bytes 3145736 | tf_op jit(solution)/shard_map/ppermute | solution.py:220
  64.4 1.4 copy-start.4
  65.8 1.7 %copy-start.10 = (bf16[1,352,2048]{2,1,0:T(8,128)(2,1)S(1)}, bf16[1,352,2048]{2,1,0:T(8,128)(2,1)}, u32[]{:S(2)}) copy-start(bf16[1,352,2048]{2,1,0:T(8,128)(2,1)} %param.15) | copy-start | bytes 4325380
  82.5 4.2 %copy-start.5 = (bf16[1024,352]{0,1:T(8,128)(2,1)S(1)}, bf16[1024,352]{0,1:T(8,128)(2,1)}, u32[]{:S(2)}) copy-start(bf16[1024,352]{0,1:T(8,128)(2,1)} %get-tuple-element.11) | copy-start | bytes 2162692
  90.0 7.7 %collective-permute-start.31 = (f32[2,2,1,128,4]{3,4,2,1,0:T(4,128)S(1)}, f32[2,2,1,128,4]{3,4,2,1,0:T(4,128)S(1)}, u32[]{:S(2)}, u32[]{:S(2)}) collective-permute-start(f32[2,2,1,128,4]{3,4,2,1,0:T(4,128)S(1)} %constant_dynamic-slice_fusion.8), channel_id=1, source_target_pairs={{0,4},{4,0},{8,12},{12,8},{16,20},{20,16},{24,28},{28,24},{1,5},{5... | collective-permute-start | bytes 24584 | tf_op jit(solution)/shard_map/ppermute | solution.py:220
  93.3 1.4 copy-start.11
  93.3 1.5 copy-start.12
  93.5 22.7 %collective-permute-start.23 = (bf16[2,2,1,128,2048]{4,3,2,1,0:T(8,128)(2,1)S(1)}, bf16[2,2,1,128,2048]{4,3,2,1,0:T(8,128)(2,1)S(1)}, u32[]{:S(2)}, u32[]{:S(2)}) collective-permute-start(bf16[2,2,1,128,2048]{4,3,2,1,0:T(8,128)(2,1)S(1)} %constant_dynamic-slice_fusion.14), channel_id=1, source_target_pairs={{0,4},{4,0},{8,12},{12,8},{16,20},{20,16},{24,28},{28,24},{1,5},{5... | collective-permute-start | bytes 6291464 | tf_op jit(solution)/shard_map/ppermute | solution.py:220
  97.5 22.2 %collective-permute-start.6 = (bf16[2,2,1,128,2048]{4,3,2,1,0:T(8,128)(2,1)S(1)}, bf16[2,2,1,128,2048]{4,3,2,1,0:T(8,128)(2,1)S(1)}, u32[]{:S(2)}, u32[]{:S(2)}) collective-permute-start(bf16[2,2,1,128,2048]{4,3,2,1,0:T(8,128)(2,1)S(1)} %constant_dynamic-slice_fusion.19), channel_id=1, source_target_pairs={{0,4},{4,0},{8,12},{12,8},{16,20},{20,16},{24,28},{28,24},{1,5},{5... | collective-permute-start | bytes 6291464 | tf_op jit(solution)/shard_map/ppermute | solution.py:220
  97.8 3.7 %collective-permute-start.32 = (f32[2,1,1,128,2]{3,4,2,1,0:T(2,128)S(1)}, f32[2,1,1,128,2]{3,4,2,1,0:T(2,128)S(1)}, u32[]{:S(2)}, u32[]{:S(2)}) collective-permute-start(f32[2,1,1,128,2]{3,4,2,1,0:T(2,128)S(1)} %constant_dynamic-slice_fusion.6), channel_id=1, source_target_pairs={{0,8},{4,12},{8,0},{12,4},{16,24},{20,28},{24,16},{28,20},{1,9},{5... | collective-permute-start | bytes 6152 | tf_op jit(solution)/shard_map/ppermute | solution.py:220
  99.3 3.6 %collective-permute-start.34 = (f32[1,2,1,128,2]{3,4,2,1,0:T(2,128)S(1)}, f32[1,2,1,128,2]{3,4,2,1,0:T(2,128)S(1)}, u32[]{:S(2)}, u32[]{:S(2)}) collective-permute-start(f32[1,2,1,128,2]{3,4,2,1,0:T(2,128)S(1)} %constant_dynamic-slice_fusion.2), channel_id=1, source_target_pairs={{0,16},{4,20},{8,24},{12,28},{16,0},{20,4},{24,8},{28,12},{1,17},{... | collective-permute-start | bytes 6152 | tf_op jit(solution)/shard_map/ppermute | solution.py:220
  101.4 3.6 %collective-permute-start.33 = (f32[1,1,1,128,2]{3,4,2,1,0:T(2,128)S(1)}, f32[1,1,1,128,2]{3,4,2,1,0:T(2,128)S(1)}, u32[]{:S(2)}, u32[]{:S(2)}) collective-permute-start(f32[1,1,1,128,2]{3,4,2,1,0:T(2,128)S(1)} %constant_dynamic-slice_fusion.4), channel_id=1, source_target_pairs={{0,16},{4,20},{8,24},{12,28},{16,0},{20,4},{24,8},{28,12},{1,17},{... | collective-permute-start | bytes 3080 | tf_op jit(solution)/shard_map/ppermute | solution.py:220
  102.9 3.6 %collective-permute-start.35 = (f32[1,1,1,128,2]{3,4,2,1,0:T(2,128)S(1)}, f32[1,1,1,128,2]{3,4,2,1,0:T(2,128)S(1)}, u32[]{:S(2)}, u32[]{:S(2)}) collective-permute-start(f32[1,1,1,128,2]{3,4,2,1,0:T(2,128)S(1)} %constant_dynamic-slice_fusion), channel_id=1, source_target_pairs={{0,8},{4,12},{8,0},{12,4},{16,24},{20,28},{24,16},{28,20},{1,9},{5... | collective-permute-start | bytes 3080 | tf_op jit(solution)/shard_map/ppermute | solution.py:220
  106.4 9.2 %collective-permute-start.36 = (f32[128,4]{0,1:T(4,128)S(1)}, f32[128,4]{0,1:T(4,128)S(1)}, u32[]{:S(2)}, u32[]{:S(2)}) collective-permute-start(f32[128,4]{0,1:T(4,128)S(1)} %pad_maximum_fusion.12), channel_id=1, source_target_pairs={{0,1},{1,2},{2,3},{3,0},{4,5},{5,6},{6,7},{7,4},{8,9},{9,10},{10,1... | collective-permute-start | bytes 6152 | tf_op jit(solution)/shard_map/ppermute | solution.py:255
  109.9 5.7 %collective-permute-start.37 = (f32[128,4]{0,1:T(4,128)S(1)}, f32[128,4]{0,1:T(4,128)S(1)}, u32[]{:S(2)}, u32[]{:S(2)}) collective-permute-start(f32[128,4]{0,1:T(4,128)S(1)} %pad_maximum_fusion.12), channel_id=1, source_target_pairs={{0,2},{1,3},{2,0},{3,1},{4,6},{5,7},{6,4},{7,5},{8,10},{9,11},{10,... | collective-permute-start | bytes 6152 | tf_op jit(solution)/shard_map/ppermute | solution.py:255
  109.9 5.7 %collective-permute-start.38 = (f32[128,4]{0,1:T(4,128)S(1)}, f32[128,4]{0,1:T(4,128)S(1)}, u32[]{:S(2)}, u32[]{:S(2)}) collective-permute-start(f32[128,4]{0,1:T(4,128)S(1)} %pad_maximum_fusion.12), channel_id=1, source_target_pairs={{0,3},{1,0},{2,1},{3,2},{4,7},{5,4},{6,5},{7,6},{8,11},{9,8},{10,9... | collective-permute-start | bytes 6152 | tf_op jit(solution)/shard_map/ppermute | solution.py:255
  117.4 14.9 %collective-permute-start.26 = (bf16[1,2,1,128,1024]{4,3,2,1,0:T(8,128)(2,1)S(1)}, bf16[1,2,1,128,1024]{4,3,2,1,0:T(8,128)(2,1)S(1)}, u32[]{:S(2)}, u32[]{:S(2)}) collective-permute-start(bf16[1,2,1,128,1024]{4,3,2,1,0:T(8,128)(2,1)S(1)} %constant_dynamic-slice_fusion.11), channel_id=1, source_target_pairs={{0,16},{4,20},{8,24},{12,28},{16,0},{20,4},{24,8},{28,12},{1,17},{... | collective-permute-start | bytes 1572872 | tf_op jit(solution)/shard_map/ppermute | solution.py:220
  118.2 15.1 %collective-permute-start.24 = (bf16[2,1,1,128,1024]{4,3,2,1,0:T(8,128)(2,1)S(1)}, bf16[2,1,1,128,1024]{4,3,2,1,0:T(8,128)(2,1)S(1)}, u32[]{:S(2)}, u32[]{:S(2)}) collective-permute-start(bf16[2,1,1,128,1024]{4,3,2,1,0:T(8,128)(2,1)S(1)} %constant_dynamic-slice_fusion.13), channel_id=1, source_target_pairs={{0,8},{4,12},{8,0},{12,4},{16,24},{20,28},{24,16},{28,20},{1,9},{5... | collective-permute-start | bytes 1572872 | tf_op jit(solution)/shard_map/ppermute | solution.py:220
  120.9 22.8 %collective-permute-start.9 = (bf16[1,2,1,128,1024]{4,3,2,1,0:T(8,128)(2,1)S(1)}, bf16[1,2,1,128,1024]{4,3,2,1,0:T(8,128)(2,1)S(1)}, u32[]{:S(2)}, u32[]{:S(2)}) collective-permute-start(bf16[1,2,1,128,1024]{4,3,2,1,0:T(8,128)(2,1)S(1)} %constant_dynamic-slice_fusion.16), channel_id=1, source_target_pairs={{0,16},{4,20},{8,24},{12,28},{16,0},{20,4},{24,8},{28,12},{1,17},{... | collective-permute-start | bytes 1572872 | tf_op jit(solution)/shard_map/ppermute | solution.py:220
  121.5 23.0 %collective-permute-start.7 = (bf16[2,1,1,128,1024]{4,3,2,1,0:T(8,128)(2,1)S(1)}, bf16[2,1,1,128,1024]{4,3,2,1,0:T(8,128)(2,1)S(1)}, u32[]{:S(2)}, u32[]{:S(2)}) collective-permute-start(bf16[2,1,1,128,1024]{4,3,2,1,0:T(8,128)(2,1)S(1)} %constant_dynamic-slice_fusion.18), channel_id=1, source_target_pairs={{0,8},{4,12},{8,0},{12,4},{16,24},{20,28},{24,16},{28,20},{1,9},{5... | collective-permute-start | bytes 1572872 | tf_op jit(solution)/shard_map/ppermute | solution.py:220
  132.6 16.1 %collective-permute-start.27 = (bf16[1,1,1,128,1024]{4,3,2,1,0:T(8,128)(2,1)S(1)}, bf16[1,1,1,128,1024]{4,3,2,1,0:T(8,128)(2,1)S(1)}, u32[]{:S(2)}, u32[]{:S(2)}) collective-permute-start(bf16[1,1,1,128,1024]{4,3,2,1,0:T(8,128)(2,1)S(1)} %constant_dynamic-slice_fusion.10), channel_id=1, source_target_pairs={{0,8},{4,12},{8,0},{12,4},{16,24},{20,28},{24,16},{28,20},{1,9},{5... | collective-permute-start | bytes 786440 | tf_op jit(solution)/shard_map/ppermute | solution.py:220
  133.5 15.2 %collective-permute-start.25 = (bf16[1,1,1,128,1024]{4,3,2,1,0:T(8,128)(2,1)S(1)}, bf16[1,1,1,128,1024]{4,3,2,1,0:T(8,128)(2,1)S(1)}, u32[]{:S(2)}, u32[]{:S(2)}) collective-permute-start(bf16[1,1,1,128,1024]{4,3,2,1,0:T(8,128)(2,1)S(1)} %constant_dynamic-slice_fusion.12), channel_id=1, source_target_pairs={{0,16},{4,20},{8,24},{12,28},{16,0},{20,4},{24,8},{28,12},{1,17},{... | collective-permute-start | bytes 786440 | tf_op jit(solution)/shard_map/ppermute | solution.py:220
  143.9 9.1 %collective-permute-start.10 = (bf16[1,1,1,128,1024]{4,3,2,1,0:T(8,128)(2,1)S(1)}, bf16[1,1,1,128,1024]{4,3,2,1,0:T(8,128)(2,1)S(1)}, u32[]{:S(2)}, u32[]{:S(2)}) collective-permute-start(bf16[1,1,1,128,1024]{4,3,2,1,0:T(8,128)(2,1)S(1)} %constant_dynamic-slice_fusion.15), channel_id=1, source_target_pairs={{0,8},{4,12},{8,0},{12,4},{16,24},{20,28},{24,16},{28,20},{1,9},{5... | collective-permute-start | bytes 786440 | tf_op jit(solution)/shard_map/ppermute | solution.py:220
  144.8 8.3 %collective-permute-start.8 = (bf16[1,1,1,128,1024]{4,3,2,1,0:T(8,128)(2,1)S(1)}, bf16[1,1,1,128,1024]{4,3,2,1,0:T(8,128)(2,1)S(1)}, u32[]{:S(2)}, u32[]{:S(2)}) collective-permute-start(bf16[1,1,1,128,1024]{4,3,2,1,0:T(8,128)(2,1)S(1)} %constant_dynamic-slice_fusion.17), channel_id=1, source_target_pairs={{0,16},{4,20},{8,24},{12,28},{16,0},{20,4},{24,8},{28,12},{1,17},{... | collective-permute-start | bytes 786440 | tf_op jit(solution)/shard_map/ppermute | solution.py:220
  149.1 8.3 %collective-permute-start.28 = (bf16[128,512]{1,0:T(8,128)(2,1)S(1)}, bf16[128,512]{1,0:T(8,128)(2,1)S(1)}, u32[]{:S(2)}, u32[]{:S(2)}) collective-permute-start(bf16[128,512]{1,0:T(8,128)(2,1)S(1)} %get-tuple-element.40), channel_id=1, source_target_pairs={{0,1},{1,2},{2,3},{3,0},{4,5},{5,6},{6,7},{7,4},{8,9},{9,10},{10,1... | collective-permute-start | bytes 393224 | tf_op jit(solution)/shard_map/ppermute | solution.py:255
  149.2 14.6 %collective-permute-start.29 = (bf16[128,512]{1,0:T(8,128)(2,1)S(1)}, bf16[128,512]{1,0:T(8,128)(2,1)S(1)}, u32[]{:S(2)}, u32[]{:S(2)}) collective-permute-start(bf16[128,512]{1,0:T(8,128)(2,1)S(1)} %get-tuple-element.41), channel_id=1, source_target_pairs={{0,2},{1,3},{2,0},{3,1},{4,6},{5,7},{6,4},{7,5},{8,10},{9,11},{10,... | collective-permute-start | bytes 393224 | tf_op jit(solution)/shard_map/ppermute | solution.py:255
  151.4 12.4 %collective-permute-start.30 = (bf16[128,512]{1,0:T(8,128)(2,1)S(1)}, bf16[128,512]{1,0:T(8,128)(2,1)S(1)}, u32[]{:S(2)}, u32[]{:S(2)}) collective-permute-start(bf16[128,512]{1,0:T(8,128)(2,1)S(1)} %get-tuple-element.42), channel_id=1, source_target_pairs={{0,3},{1,0},{2,1},{3,2},{4,7},{5,4},{6,5},{7,6},{8,11},{9,8},{10,9... | collective-permute-start | bytes 393224 | tf_op jit(solution)/shard_map/ppermute | solution.py:255
  153.4 11.2 %collective-permute-start.11 = (bf16[128,512]{1,0:T(8,128)(2,1)S(1)}, bf16[128,512]{1,0:T(8,128)(2,1)S(1)}, u32[]{:S(2)}, u32[]{:S(2)}) collective-permute-start(bf16[128,512]{1,0:T(8,128)(2,1)S(1)} %get-tuple-element.43), channel_id=1, source_target_pairs={{0,1},{1,2},{2,3},{3,0},{4,5},{5,6},{6,7},{7,4},{8,9},{9,10},{10,1... | collective-permute-start | bytes 393224 | tf_op jit(solution)/shard_map/ppermute | solution.py:255
  154.0 13.0 %collective-permute-start.12 = (bf16[128,512]{1,0:T(8,128)(2,1)S(1)}, bf16[128,512]{1,0:T(8,128)(2,1)S(1)}, u32[]{:S(2)}, u32[]{:S(2)}) collective-permute-start(bf16[128,512]{1,0:T(8,128)(2,1)S(1)} %get-tuple-element.44), channel_id=1, source_target_pairs={{0,2},{1,3},{2,0},{3,1},{4,6},{5,7},{6,4},{7,5},{8,10},{9,11},{10,... | collective-permute-start | bytes 393224 | tf_op jit(solution)/shard_map/ppermute | solution.py:255
  157.4 9.6 %collective-permute-start.13 = (bf16[128,512]{1,0:T(8,128)(2,1)S(1)}, bf16[128,512]{1,0:T(8,128)(2,1)S(1)}, u32[]{:S(2)}, u32[]{:S(2)}) collective-permute-start(bf16[128,512]{1,0:T(8,128)(2,1)S(1)} %get-tuple-element.45), channel_id=1, source_target_pairs={{0,3},{1,0},{2,1},{3,2},{4,7},{5,4},{6,5},{7,6},{8,11},{9,8},{10,9... | collective-permute-start | bytes 393224 | tf_op jit(solution)/shard_map/ppermute | solution.py:255

commit v3 on v2

--- a/solution.py
+++ b/solution.py
@@ -152,7 +152,7 @@
     choose = route_expert.shape[1]
     routes = jnp.concatenate([route_expert.astype(jnp.float32), route_weight], axis=1)
     arrived = gather_tokens(tokens)
-    routes = lax.all_gather(routes, "dp", axis=0, tiled=True)
+    routes = gather_small(routes.T[None]).swapaxes(1, 2).reshape(-1, 2 * choose)
     cot_all = gather_tokens(gather_columns(cotangent))
     experts, weights = routes[:, :choose], routes[:, choose:]
     chosen = experts == me.astype(jnp.float32)
@@ -250,6 +250,12 @@
     return jnp.concatenate(both, axis=-1).reshape(-1, width)
 
 
+def gather_small(block):
+    for bit in bits():
+        block = jnp.concatenate(in_order(block, bit), axis=0)
+    return block
+
+
 def shift(block, by):
     shares = lax.axis_size("expert")
     return lax.ppermute(block, "expert", [(i, (i + by) % shares) for i in range(shares)])

time: 168 us -> 164 us (0.976)
  blocking collectives: 23.3 us -> 0 us
  waiting for transfers between devices: 43.6 us -> 65.6 us
  local copies, waits for them, and re-layouts: 12.6 us -> 10.9 us
    ppermute x27 -> x30, waiting for transfers between devices: 32.4 us -> 56.1 us  [swap(): return lax.ppermute(block, 'dp', [(i, i ^ bit) for i in range(owners)])]
    all_gather x1 -> x0, blocking collectives: 23.3 us -> none  [dense(): routes = lax.all_gather(routes, 'dp', axis=0, tiled=True)]
    ppermute x12, starting transfers between devices: 19.9 us -> 17.9 us  [shift(): lax.ppermute(block, 'expert', [(i, (i + by) % shares) for i in range(shar...]
    unnamed x2, other arithmetic: 0.72 us -> 2.55 us
    ppermute x27 -> x30, starting transfers between devices: 24.4 us -> 25.2 us  [swap(): return lax.ppermute(block, 'dp', [(i, i ^ bit) for i in range(owners)])]
  transfers between devices with their start and end apart: 39 -> 42, of which waited for: 17 -> 18; matrix products, arithmetic and copies ran while one was open for 16% -> 16% of each run, Pallas kernels for 0% -> 0%
where the time goes in v3:
time: 164 us
  waiting for transfers between devices  65.6 us (40%)
  starting transfers between devices  43.1 us (26%)
  matrix products  24.6 us (15%)
  other arithmetic  18.4 us (11%)
  local copies, waits for them, and re-layouts  10.9 us (7%)
    ppermute x30, waiting for transfers between devices, swap(): return lax.ppermute(block, 'dp', [(i, i ^ bit) for i in range(owners)])  56.1 us
    ppermute x30, starting transfers between devices, swap(): return lax.ppermute(block, 'dp', [(i, i ^ bit) for i in range(owners)])  25.2 us
    ppermute x12, starting transfers between devices, shift(): lax.ppermute(block, 'expert', [(i, (i + by) % shares) for i in range(shar...  17.9 us
    ppermute x12, waiting for transfers between devices, shift(): lax.ppermute(block, 'expert', [(i, (i + by) % shares) for i in range(shar...  9.54 us
    convert_element_type x1, other arithmetic, dense(): (cot_all.astype(jnp.float32) * row_weight * scale).astype(jnp.bfloat16)  4.2 us
    convert_element_type x1, local copies, waits for them, and re-layouts, dense(): cot_all.astype(jnp.float32) * row_weight * scale  3.88 us
    dot_general x1, matrix products, dense(): lax.dot_general(arrived, up_local, (((1,), (1,)), ((), ())), preferred_el...  3.63 us
  transfers between devices with their start and end apart: 42, of which 18 were waited for; matrix products, arithmetic and copies ran while one was open for 16% of the time, Pallas kernels for 0%

profile of v3, /device:TPU:0, one launch (start us, length us, event | category | flops | bytes accessed | tf_op | source)
XLA Modules:
  0.0 164.0 jit_solution(15075123321030735415)
XLA Ops:
  0.7 3.1 %collective-permute-start.17 = (bf16[128,512]{1,0:T(8,128)(2,1)}, bf16[128,512]{1,0:T(8,128)(2,1)}, u32[]{:S(2)}, u32[]{:S(2)}) collective-permute-start(bf16[128,512]{1,0:T(8,128)(2,1)} %param.19), channel_id=1, source_target_pairs={{0,1},{1,2},{2,3},{3,0},{4,5},{5,6},{6,7},{7,4},{8,9},{9,10},{10,1... | collective-permute-start | bytes 393224 | tf_op jit(solution)/shard_map/ppermute | solution.py:261
  3.7 2.6 %collective-permute-start.18 = (bf16[128,512]{1,0:T(8,128)(2,1)}, bf16[128,512]{1,0:T(8,128)(2,1)S(1)}, u32[]{:S(2)}, u32[]{:S(2)}) collective-permute-start(bf16[128,512]{1,0:T(8,128)(2,1)} %param.19), channel_id=1, source_target_pairs={{0,2},{1,3},{2,0},{3,1},{4,6},{5,7},{6,4},{7,5},{8,10},{9,11},{10,... | collective-permute-start | bytes 393224 | tf_op jit(solution)/shard_map/ppermute | solution.py:261
  6.3 1.3 collective-permute-start.19
  7.7 1.1 slice_bitcast_fusion.3
  8.7 1.6 collective-permute-start
  10.3 0.7 convert_element_type.162
  11.0 0.7 maximum_bitcast_fusion.1
  11.7 0.9 constant_dynamic-update-slice_fusion.3
  12.7 0.9 constant_dynamic-slice_fusion.20
  13.5 1.3 reduce
  14.8 1.3 reduce.1
  16.1 1.5 collective-permute-start.3
  17.6 0.7 broadcast_select_fusion.22
  18.9 0.9 constant_dynamic-update-slice_fusion.2
  19.9 1.6 collective-permute-start.20
  22.0 3.2 %collective-permute-done.3 = bf16[1,1,128,1024]{3,2,1,0:T(8,128)(2,1)S(1)} collective-permute-done((bf16[1,1,128,1024]{3,2,1,0:T(8,128)(2,1)S(1)}, bf16[1,1,128,1024]{3,2,1,0:T(8,128)(2,1)S(1)}, u32[]{:S(2)}, u32[]{:S(2)}) %collective-permute-start.3) | collective-permute-done | bytes 262176 | tf_op jit(solution)/shard_map/ppermute | solution.py:220
  25.3 1.6 collective-permute-start.1
  26.9 1.2 collective-permute-done.20
  28.1 2.7 %collective-permute-done.23 = bf16[1,1,128,1024]{3,2,1,0:T(8,128)(2,1)S(1)} collective-permute-done((bf16[1,1,128,1024]{3,2,1,0:T(8,128)(2,1)S(1)}, bf16[1,1,128,1024]{3,2,1,0:T(8,128)(2,1)S(1)}, u32[]{:S(2)}, u32[]{:S(2)}) %collective-permute-start.23) | collective-permute-done | bytes 262176 | tf_op jit(solution)/shard_map/ppermute | solution.py:220
  30.9 1.6 collective-permute-start.21
  33.2 1.6 collective-permute-start.24
  35.3 6.7 %collective-permute-done.1 = bf16[1,2,128,1024]{3,2,1,0:T(8,128)(2,1)S(1)} collective-permute-done((bf16[1,2,128,1024]{3,2,1,0:T(8,128)(2,1)S(1)}, bf16[1,2,128,1024]{3,2,1,0:T(8,128)(2,1)S(1)}, u32[]{:S(2)}, u32[]{:S(2)}) %collective-permute-start.1) | collective-permute-done | bytes 524320 | tf_op jit(solution)/shard_map/ppermute | solution.py:220
  42.0 11.0 %collective-permute-done.21 = bf16[1,2,128,1024]{3,2,1,0:T(8,128)(2,1)S(1)} collective-permute-done((bf16[1,2,128,1024]{3,2,1,0:T(8,128)(2,1)S(1)}, bf16[1,2,128,1024]{3,2,1,0:T(8,128)(2,1)S(1)}, u32[]{:S(2)}, u32[]{:S(2)}) %collective-permute-start.21) | collective-permute-done | bytes 524320 | tf_op jit(solution)/shard_map/ppermute | solution.py:220
  53.4 3.3 %collective-permute-done.24 = bf16[2,1,128,1024]{3,2,1,0:T(8,128)(2,1)S(1)} collective-permute-done((bf16[2,1,128,1024]{3,2,1,0:T(8,128)(2,1)S(1)}, bf16[2,1,128,1024]{3,2,1,0:T(8,128)(2,1)S(1)}, u32[]{:S(2)}, u32[]{:S(2)}) %collective-permute-start.24) | collective-permute-done | bytes 524320 | tf_op jit(solution)/shard_map/ppermute | solution.py:220
  58.3 1.5 collective-permute-done.25
  61.5 1.1 maximum_convert_fusion
  63.6 0.7 copy-done.2
  64.4 1.7 %convolution_multiply_fusion.1 = f32[1024,352]{0,1:T(8,128)S(1)} fusion(bf16[1024,2048]{1,0:T(8,128)(2,1)S(1)} %bitcast.133, bf16[1,352,2048]{2,1,0:T(8,128)(2,1)S(1)} %copy-done.2, f32[352]{0:T(512)S(1)} %copy-done.4), kind=kOutput, calls=%fused_computation.23 | convolution fusion | flops 1476755456 | bytes 7079296 | tf_op jit(solution)/shard_map/dot_general | solution.py:163
  66.1 1.8 %fusion.2 = f32[1024,352]{0,1:T(8,128)S(1)} fusion(bf16[1024,1024]{1,0:T(8,128)(2,1)S(1)} %bitcast.138, bf16[1024,1024]{1,0:T(8,128)(2,1)S(1)} %bitcast.137, f32[2048]{0:T(1024)S(1)} %bitcast.141, f32[1024]{0:T(1024)S(1)} %get-tuple-element.8, bf16[1,352,2048]{2,1,0:T(8,128)(2,1)S(1)} %copy-done.6), kind=kOutput, calls=%fused_computation.6 | convolution fusion | flops 1491075072 | bytes 7090176 | tf_op jit(solution)/shard_map/dot_general | solution.py:186
  67.9 3.6 %multiply_reduce_fusion = (f32[1024]{0:T(1024)S(1)}, bf16[1024,352]{0,1:T(8,128)(2,1)}, bf16[1024,352]{0,1:T(8,128)(2,1)S(1)}, bf16[1024,352]{0,1:T(8,128)(2,1)}) fusion(f32[1024,352]{0,1:T(8,128)S(1)} %fusion.2, f32[1024,352]{0,1:T(8,128)S(1)} %convolution_multiply_fusion.1, f32[352]{0:T(512)S(1)} %copy-done.4, f32[352]{0:T(512)S(1)} %copy-done.5, ...), kind=kOutput, calls=%fused_computation.31 | convolution fusion | flops 1483963392 | bytes 10689280 | tf_op jit(solution)/shard_map/dot_general | solution.py:169
  71.6 3.3 %convolution_bitcast_fusion.2 = f32[1,352,2048]{2,1,0:T(8,128)} fusion(bf16[1024,352]{0,1:T(8,128)(2,1)S(1)} %get-tuple-element.10, bf16[1024,2048]{1,0:T(8,128)(2,1)S(1)} %bitcast.135), kind=kOutput, calls=%fused_computation.18 | convolution fusion | flops 1476395008 | bytes 7798784 | tf_op jit(solution)/shard_map/dot_general | solution.py:209
  74.8 2.4 %fusion.12 = f32[1024,2048]{1,0:T(8,128)S(1)} fusion(bf16[1024,352]{0,1:T(8,128)(2,1)S(1)} %get-tuple-element.10, bf16[1,352,2048]{2,1,0:T(8,128)(2,1)S(1)} %copy-done.2), kind=kOutput, calls=%fused_computation.28 | convolution fusion | flops 1476395008 | bytes 10551296 | tf_op jit(solution)/shard_map/dot_general | solution.py:194
  77.2 3.9 %copy.23 = f32[4,2,128,2048]{3,2,1,0:T(8,128)} copy(f32[4,2,128,2048]{3,2,0,1:T(8,128)S(1)} %maximum_convert_fusion) | data formatting | bytes 16777216 | tf_op jit(solution)/shard_map/convert_element_type | solution.py:185
  81.1 4.2 %fusion.1 = bf16[1024,2048]{1,0:T(8,128)(2,1)S(1)} fusion(f32[4,2,128,2048]{3,2,1,0:T(8,128)} %copy.23, f32[2048]{0:T(1024)S(1)} %bitcast.142, f32[1024]{0:T(1024)S(1)} %get-tuple-element.8), kind=kLoop, calls=%fused_computation.2 | loop fusion | flops 6291456 | bytes 12595200 | tf_op jit(solution)/shard_map/convert_element_type | solution.py:185
  85.3 3.3 %convolution_bitcast_fusion.1 = f32[1,352,2048]{2,1,0:T(8,128)} fusion(bf16[1024,352]{0,1:T(8,128)(2,1)S(1)} %copy-done.3, bf16[1024,2048]{1,0:T(8,128)(2,1)S(1)} %bitcast.136), kind=kOutput, calls=%fused_computation.17 | convolution fusion | flops 1476395008 | bytes 7798784 | tf_op jit(solution)/shard_map/dot_general | solution.py:212
  88.8 2.8 %add_convert_fusion = bf16[1024,2048]{1,0:T(8,128)(2,1)S(1)} fusion(f32[1024,2048]{1,0:T(8,128)S(1)} %fusion.12, bf16[1024,352]{0,1:T(8,128)(2,1)S(1)} %copy-done.3, bf16[1,352,2048]{2,1,0:T(8,128)(2,1)S(1)} %copy-done), kind=kOutput, calls=%fused_computation.3 | convolution fusion | flops 1480589312 | bytes 14745600 | tf_op jit(solution)/shard_map/dot_general | solution.py:197
  92.4 0.7 copy-done.7
  93.2 2.4 %multiply_convert_fusion.1 = bf16[1024,2048]{1,0:T(8,128)(2,1)S(1)} fusion(bf16[1024,352]{0,1:T(8,128)(2,1)S(1)} %copy-done.8, f32[2048]{0:T(1024)S(1)} %bitcast.143, f32[1024]{0:T(1024)S(1)} %get-tuple-element.8, bf16[1,352,2048]{2,1,0:T(8,128)(2,1)S(1)} %copy-done.7), kind=kOutput, calls=%fused_computation.5 | convolution fusion | flops 1482686464 | bytes 6369280 | tf_op jit(solution)/shard_map/dot_general | solution.py:178
  97.5 2.5 %collective-permute-done.35 = f32[2,1,1,128,2]{3,4,2,1,0:T(2,128)S(1)} collective-permute-done((f32[2,1,1,128,2]{3,4,2,1,0:T(2,128)S(1)}, f32[2,1,1,128,2]{3,4,2,1,0:T(2,128)S(1)}, u32[]{:S(2)}, u32[]{:S(2)}) %collective-permute-start.35) | collective-permute-done | bytes 2080 | tf_op jit(solution)/shard_map/ppermute | solution.py:220
  100.6 1.5 collective-permute-start.38
  102.0 1.5 collective-permute-done.36
  104.2 0.7 collective-permute-start.39
  105.3 2.8 %collective-permute-start.41 = (f32[128,4]{0,1:T(4,128)S(1)}, f32[128,4]{0,1:T(4,128)S(1)}, u32[]{:S(2)}, u32[]{:S(2)}) collective-permute-start(f32[128,4]{0,1:T(4,128)S(1)} %pad_maximum_fusion.13), channel_id=1, source_target_pairs={{0,3},{1,0},{2,1},{3,2},{4,7},{5,4},{6,5},{7,6},{8,11},{9,8},{10,9... | collective-permute-start | bytes 6152 | tf_op jit(solution)/shard_map/ppermute | solution.py:261
  108.1 3.3 %convolution_bitcast_fusion = f32[1,352,2048]{2,1,0:T(8,128)} fusion(bf16[1024,352]{0,1:T(8,128)(2,1)S(1)} %copy-done.8, bf16[1024,2048]{1,0:T(8,128)(2,1)S(1)} %fusion.1), kind=kOutput, calls=%fused_computation.16 | convolution fusion | flops 1476395008 | bytes 7798784 | tf_op jit(solution)/shard_map/dot_general | solution.py:206
  111.9 0.9 add_convert_fusion.1
  113.2 1.6 collective-permute-start.29
  115.4 0.9 add_convert_fusion.2
  116.5 1.5 collective-permute-start.12
  118.7 9.4 %collective-permute-done.29 = bf16[1,2,1,128,1024]{4,3,2,1,0:T(8,128)(2,1)S(1)} collective-permute-done((bf16[1,2,1,128,1024]{4,3,2,1,0:T(8,128)(2,1)S(1)}, bf16[1,2,1,128,1024]{4,3,2,1,0:T(8,128)(2,1)S(1)}, u32[]{:S(2)}, u32[]{:S(2)}) %collective-permute-start.29) | collective-permute-done | bytes 524320 | tf_op jit(solution)/shard_map/ppermute | solution.py:220
  128.3 1.5 collective-permute-start.30
  130.1 0.7 collective-permute-start.28
  130.8 8.5 %collective-permute-done.12 = bf16[1,2,1,128,1024]{4,3,2,1,0:T(8,128)(2,1)S(1)} collective-permute-done((bf16[1,2,1,128,1024]{4,3,2,1,0:T(8,128)(2,1)S(1)}, bf16[1,2,1,128,1024]{4,3,2,1,0:T(8,128)(2,1)S(1)}, u32[]{:S(2)}, u32[]{:S(2)}) %collective-permute-start.12) | collective-permute-done | bytes 524320 | tf_op jit(solution)/shard_map/ppermute | solution.py:220
  139.6 1.5 collective-permute-start.13
  141.3 0.7 collective-permute-start.11
  142.0 3.0 %collective-permute-done.30 = bf16[1,1,1,128,1024]{4,3,2,1,0:T(8,128)(2,1)S(1)} collective-permute-done((bf16[1,1,1,128,1024]{4,3,2,1,0:T(8,128)(2,1)S(1)}, bf16[1,1,1,128,1024]{4,3,2,1,0:T(8,128)(2,1)S(1)}, u32[]{:S(2)}, u32[]{:S(2)}) %collective-permute-start.30) | collective-permute-done | bytes 262176 | tf_op jit(solution)/shard_map/ppermute | solution.py:220
  146.1 1.3 collective-permute-start.32
  147.3 2.8 %collective-permute-start.33 = (bf16[128,512]{1,0:T(8,128)(2,1)S(1)}, bf16[128,512]{1,0:T(8,128)(2,1)S(1)}, u32[]{:S(2)}, u32[]{:S(2)}) collective-permute-start(bf16[128,512]{1,0:T(8,128)(2,1)S(1)} %get-tuple-element.42), channel_id=1, source_target_pairs={{0,3},{1,0},{2,1},{3,2},{4,7},{5,4},{6,5},{7,6},{8,11},{9,8},{10,9... | collective-permute-start | bytes 393224 | tf_op jit(solution)/shard_map/ppermute | solution.py:261
  150.7 1.2 collective-permute-start.15
  151.9 1.9 %collective-permute-done.31 = bf16[128,512]{1,0:T(8,128)(2,1)S(1)} collective-permute-done((bf16[128,512]{1,0:T(8,128)(2,1)S(1)}, bf16[128,512]{1,0:T(8,128)(2,1)S(1)}, u32[]{:S(2)}, u32[]{:S(2)}) %collective-permute-start.31) | collective-permute-done | bytes 131104 | tf_op jit(solution)/shard_map/ppermute | solution.py:261
  153.8 1.0 collective-permute-start.16
  154.8 5.2 %collective-permute-done.32 = bf16[128,512]{1,0:T(8,128)(2,1)S(1)} collective-permute-done((bf16[128,512]{1,0:T(8,128)(2,1)S(1)}, bf16[128,512]{1,0:T(8,128)(2,1)S(1)}, u32[]{:S(2)}, u32[]{:S(2)}) %collective-permute-start.32) | collective-permute-done | bytes 131104 | tf_op jit(solution)/shard_map/ppermute | solution.py:261
  160.0 0.8 add_convert_fusion.11
  160.7 2.4 %collective-permute-done.15 = bf16[128,512]{1,0:T(8,128)(2,1)S(1)} collective-permute-done((bf16[128,512]{1,0:T(8,128)(2,1)S(1)}, bf16[128,512]{1,0:T(8,128)(2,1)S(1)}, u32[]{:S(2)}, u32[]{:S(2)}) %collective-permute-start.15) | collective-permute-done | bytes 131104 | tf_op jit(solution)/shard_map/ppermute | solution.py:261
  163.2 0.8 add_convert_fusion.12
  (131 shorter events, 16.4 us)
Async XLA Ops:
  0.6 67.3 %copy-start = (bf16[1,352,2048]{2,1,0:T(8,128)(2,1)S(1)}, bf16[1,352,2048]{2,1,0:T(8,128)(2,1)}, u32[]{:S(2)}) copy-start(bf16[1,352,2048]{2,1,0:T(8,128)(2,1)} %param.14) | copy-start | bytes 4325380
  0.6 24.5 %copy-start.1 = (bf16[128,2048]{1,0:T(8,128)(2,1)S(1)}, bf16[128,2048]{1,0:T(8,128)(2,1)}, u32[]{:S(2)}) copy-start(bf16[128,2048]{1,0:T(8,128)(2,1)} %param.10) | copy-start | bytes 1572868
  0.7 17.6 %collective-permute-start.17 = (bf16[128,512]{1,0:T(8,128)(2,1)}, bf16[128,512]{1,0:T(8,128)(2,1)}, u32[]{:S(2)}, u32[]{:S(2)}) collective-permute-start(bf16[128,512]{1,0:T(8,128)(2,1)} %param.19), channel_id=1, source_target_pairs={{0,1},{1,2},{2,3},{3,0},{4,5},{5,6},{6,7},{7,4},{8,9},{9,10},{10,1... | collective-permute-start | bytes 393224 | tf_op jit(solution)/shard_map/ppermute | solution.py:261
  3.7 16.1 %collective-permute-start.18 = (bf16[128,512]{1,0:T(8,128)(2,1)}, bf16[128,512]{1,0:T(8,128)(2,1)S(1)}, u32[]{:S(2)}, u32[]{:S(2)}) collective-permute-start(bf16[128,512]{1,0:T(8,128)(2,1)} %param.19), channel_id=1, source_target_pairs={{0,2},{1,3},{2,0},{3,1},{4,6},{5,7},{6,4},{7,5},{8,10},{9,11},{10,... | collective-permute-start | bytes 393224 | tf_op jit(solution)/shard_map/ppermute | solution.py:261
  6.3 13.5 %collective-permute-start.19 = (bf16[128,512]{1,0:T(8,128)(2,1)}, bf16[128,512]{1,0:T(8,128)(2,1)S(1)}, u32[]{:S(2)}, u32[]{:S(2)}) collective-permute-start(bf16[128,512]{1,0:T(8,128)(2,1)} %param.19), channel_id=1, source_target_pairs={{0,3},{1,0},{2,1},{3,2},{4,7},{5,4},{6,5},{7,6},{8,11},{9,8},{10,9... | collective-permute-start | bytes 393224 | tf_op jit(solution)/shard_map/ppermute | solution.py:261
  8.7 13.3 %collective-permute-start = (bf16[1,1,128,1024]{3,2,1,0:T(8,128)(2,1)S(1)}, bf16[1,1,128,1024]{3,2,1,0:T(8,128)(2,1)S(1)}, u32[]{:S(2)}, u32[]{:S(2)}) collective-permute-start(bf16[1,1,128,1024]{3,2,1,0:T(8,128)(2,1)S(1)} %get-tuple-element.48), channel_id=1, source_target_pairs={{0,8},{4,12},{8,0},{12,4},{16,24},{20,28},{24,16},{28,20},{1,9},{5... | collective-permute-start | bytes 786440 | tf_op jit(solution)/shard_map/ppermute | solution.py:220
  11.7 4.4 %collective-permute-start.6 = (f32[1,8,128]{2,1,0:T(8,128)S(1)}, f32[1,8,128]{2,1,0:T(8,128)}, u32[]{:S(2)}, u32[]{:S(2)}) collective-permute-start(f32[1,8,128]{2,1,0:T(8,128)S(1)} %maximum_bitcast_fusion.1), channel_id=1, source_target_pairs={{0,4},{4,0},{8,12},{12,8},{16,20},{20,16},{24,28},{28,24},{1,5},{5... | collective-permute-start | bytes 12296 | tf_op jit(solution)/shard_map/ppermute | solution.py:220
  16.1 9.1 %collective-permute-start.3 = (bf16[1,1,128,1024]{3,2,1,0:T(8,128)(2,1)S(1)}, bf16[1,1,128,1024]{3,2,1,0:T(8,128)(2,1)S(1)}, u32[]{:S(2)}, u32[]{:S(2)}) collective-permute-start(bf16[1,1,128,1024]{3,2,1,0:T(8,128)(2,1)S(1)} %get-tuple-element.49), channel_id=1, source_target_pairs={{0,16},{4,20},{8,24},{12,28},{16,0},{20,4},{24,8},{28,12},{1,17},{... | collective-permute-start | bytes 786440 | tf_op jit(solution)/shard_map/ppermute | solution.py:220
  18.3 14.2 %collective-permute-start.7 = (f32[2,8,128]{2,1,0:T(8,128)S(1)}, f32[2,8,128]{2,1,0:T(8,128)S(1)}, u32[]{:S(2)}, u32[]{:S(2)}) collective-permute-start(f32[2,8,128]{2,1,0:T(8,128)S(1)} %pad_maximum_fusion.12), channel_id=1, source_target_pairs={{0,8},{4,12},{8,0},{12,4},{16,24},{20,28},{24,16},{28,20},{1,9},{5... | collective-permute-start | bytes 24584 | tf_op jit(solution)/shard_map/ppermute | solution.py:220
  19.9 8.2 %collective-permute-start.20 = (bf16[1,1,128,1024]{3,2,1,0:T(8,128)(2,1)S(1)}, bf16[1,1,128,1024]{3,2,1,0:T(8,128)(2,1)S(1)}, u32[]{:S(2)}, u32[]{:S(2)}) collective-permute-start(bf16[1,1,128,1024]{3,2,1,0:T(8,128)(2,1)S(1)} %get-tuple-element.52), channel_id=1, source_target_pairs={{0,8},{4,12},{8,0},{12,4},{16,24},{20,28},{24,16},{28,20},{1,9},{5... | collective-permute-start | bytes 786440 | tf_op jit(solution)/shard_map/ppermute | solution.py:220
  21.5 9.3 %collective-permute-start.23 = (bf16[1,1,128,1024]{3,2,1,0:T(8,128)(2,1)S(1)}, bf16[1,1,128,1024]{3,2,1,0:T(8,128)(2,1)S(1)}, u32[]{:S(2)}, u32[]{:S(2)}) collective-permute-start(bf16[1,1,128,1024]{3,2,1,0:T(8,128)(2,1)S(1)} %get-tuple-element.53), channel_id=1, source_target_pairs={{0,16},{4,20},{8,24},{12,28},{16,0},{20,4},{24,8},{28,12},{1,17},{... | collective-permute-start | bytes 786440 | tf_op jit(solution)/shard_map/ppermute | solution.py:220
  25.3 16.7 %collective-permute-start.1 = (bf16[1,2,128,1024]{3,2,1,0:T(8,128)(2,1)S(1)}, bf16[1,2,128,1024]{3,2,1,0:T(8,128)(2,1)S(1)}, u32[]{:S(2)}, u32[]{:S(2)}) collective-permute-start(bf16[1,2,128,1024]{3,2,1,0:T(8,128)(2,1)S(1)} %pad_maximum_fusion.7), channel_id=1, source_target_pairs={{0,16},{4,20},{8,24},{12,28},{16,0},{20,4},{24,8},{28,12},{1,17},{... | collective-permute-start | bytes 1572872 | tf_op jit(solution)/shard_map/ppermute | solution.py:220
  30.9 22.1 %collective-permute-start.21 = (bf16[1,2,128,1024]{3,2,1,0:T(8,128)(2,1)S(1)}, bf16[1,2,128,1024]{3,2,1,0:T(8,128)(2,1)S(1)}, u32[]{:S(2)}, u32[]{:S(2)}) collective-permute-start(bf16[1,2,128,1024]{3,2,1,0:T(8,128)(2,1)S(1)} %pad_maximum_fusion.9), channel_id=1, source_target_pairs={{0,16},{4,20},{8,24},{12,28},{16,0},{20,4},{24,8},{28,12},{1,17},{... | collective-permute-start | bytes 1572872 | tf_op jit(solution)/shard_map/ppermute | solution.py:220
  32.6 20.8 %collective-permute-start.4 = (bf16[2,1,128,1024]{3,2,1,0:T(8,128)(2,1)S(1)}, bf16[2,1,128,1024]{3,2,1,0:T(8,128)(2,1)S(1)}, u32[]{:S(2)}, u32[]{:S(2)}) collective-permute-start(bf16[2,1,128,1024]{3,2,1,0:T(8,128)(2,1)S(1)} %pad_maximum_fusion.8), channel_id=1, source_target_pairs={{0,8},{4,12},{8,0},{12,4},{16,24},{20,28},{24,16},{28,20},{1,9},{5... | collective-permute-start | bytes 1572872 | tf_op jit(solution)/shard_map/ppermute | solution.py:220
  33.2 23.5 %collective-permute-start.24 = (bf16[2,1,128,1024]{3,2,1,0:T(8,128)(2,1)S(1)}, bf16[2,1,128,1024]{3,2,1,0:T(8,128)(2,1)S(1)}, u32[]{:S(2)}, u32[]{:S(2)}) collective-permute-start(bf16[2,1,128,1024]{3,2,1,0:T(8,128)(2,1)S(1)} %pad_maximum_fusion.10), channel_id=1, source_target_pairs={{0,8},{4,12},{8,0},{12,4},{16,24},{20,28},{24,16},{28,20},{1,9},{5... | collective-permute-start | bytes 1572872 | tf_op jit(solution)/shard_map/ppermute | solution.py:220
  34.8 22.3 %collective-permute-start.8 = (f32[4,8,128]{2,1,0:T(8,128)S(1)}, f32[4,8,128]{2,1,0:T(8,128)S(1)}, u32[]{:S(2)}, u32[]{:S(2)}) collective-permute-start(f32[4,8,128]{2,1,0:T(8,128)S(1)} %pad_maximum_fusion.11), channel_id=1, source_target_pairs={{0,16},{4,20},{8,24},{12,28},{16,0},{20,4},{24,8},{28,12},{1,17},{... | collective-permute-start | bytes 49160 | tf_op jit(solution)/shard_map/ppermute | solution.py:220
  53.3 4.8 %collective-permute-start.22 = (bf16[4,128,1024]{2,1,0:T(8,128)(2,1)S(1)}, bf16[4,128,1024]{2,1,0:T(8,128)(2,1)S(1)}, u32[]{:S(2)}, u32[]{:S(2)}) collective-permute-start(bf16[4,128,1024]{2,1,0:T(8,128)(2,1)S(1)} %bitcast.129), channel_id=1, source_target_pairs={{0,4},{4,0},{8,12},{12,8},{16,20},{20,16},{24,28},{28,24},{1,5},{5... | collective-permute-start | bytes 3145736 | tf_op jit(solution)/shard_map/ppermute | solution.py:220
  57.1 2.7 %collective-permute-start.25 = (bf16[4,128,1024]{2,1,0:T(8,128)(2,1)S(1)}, bf16[4,128,1024]{2,1,0:T(8,128)(2,1)S(1)}, u32[]{:S(2)}, u32[]{:S(2)}) collective-permute-start(bf16[4,128,1024]{2,1,0:T(8,128)(2,1)S(1)} %bitcast.130), channel_id=1, source_target_pairs={{0,4},{4,0},{8,12},{12,8},{16,20},{20,16},{24,28},{28,24},{1,5},{5... | collective-permute-start | bytes 3145736 | tf_op jit(solution)/shard_map/ppermute | solution.py:220
  57.3 4.0 %collective-permute-start.2 = (bf16[4,128,1024]{2,1,0:T(8,128)(2,1)S(1)}, bf16[4,128,1024]{2,1,0:T(8,128)(2,1)S(1)}, u32[]{:S(2)}, u32[]{:S(2)}) collective-permute-start(bf16[4,128,1024]{2,1,0:T(8,128)(2,1)S(1)} %bitcast.132), channel_id=1, source_target_pairs={{0,4},{4,0},{8,12},{12,8},{16,20},{20,16},{24,28},{28,24},{1,5},{5... | collective-permute-start | bytes 3145736 | tf_op jit(solution)/shard_map/ppermute | solution.py:220
  58.0 4.8 %collective-permute-start.5 = (bf16[4,128,1024]{2,1,0:T(8,128)(2,1)S(1)}, bf16[4,128,1024]{2,1,0:T(8,128)(2,1)S(1)}, u32[]{:S(2)}, u32[]{:S(2)}) collective-permute-start(bf16[4,128,1024]{2,1,0:T(8,128)(2,1)S(1)} %bitcast.131), channel_id=1, source_target_pairs={{0,4},{4,0},{8,12},{12,8},{16,20},{20,16},{24,28},{28,24},{1,5},{5... | collective-permute-start | bytes 3145736 | tf_op jit(solution)/shard_map/ppermute | solution.py:220
  63.0 1.4 copy-start.2
  63.0 1.4 copy-start.4
  64.4 1.7 %copy-start.6 = (bf16[1,352,2048]{2,1,0:T(8,128)(2,1)S(1)}, bf16[1,352,2048]{2,1,0:T(8,128)(2,1)}, u32[]{:S(2)}) copy-start(bf16[1,352,2048]{2,1,0:T(8,128)(2,1)} %param.15) | copy-start | bytes 4325380
  66.1 1.9 %copy-start.5 = (f32[352]{0:T(512)S(1)}, f32[352]{0:T(512)}, u32[]{:S(2)}) copy-start(f32[352]{0:T(512)} %reduce.1) | copy-start | bytes 4228
  81.1 4.2 %copy-start.3 = (bf16[1024,352]{0,1:T(8,128)(2,1)S(1)}, bf16[1024,352]{0,1:T(8,128)(2,1)}, u32[]{:S(2)}) copy-start(bf16[1024,352]{0,1:T(8,128)(2,1)} %get-tuple-element.11) | copy-start | bytes 2162692
  88.6 7.7 %collective-permute-start.34 = (f32[2,2,1,128,4]{3,4,2,1,0:T(4,128)S(1)}, f32[2,2,1,128,4]{3,4,2,1,0:T(4,128)S(1)}, u32[]{:S(2)}, u32[]{:S(2)}) collective-permute-start(f32[2,2,1,128,4]{3,4,2,1,0:T(4,128)S(1)} %constant_dynamic-slice_fusion.8), channel_id=1, source_target_pairs={{0,4},{4,0},{8,12},{12,8},{16,20},{20,16},{24,28},{28,24},{1,5},{5... | collective-permute-start | bytes 24584 | tf_op jit(solution)/shard_map/ppermute | solution.py:220
  91.7 1.4 copy-start.7
  91.7 1.5 copy-start.8
  91.9 20.0 %collective-permute-start.26 = (bf16[2,2,1,128,2048]{4,3,2,1,0:T(8,128)(2,1)S(1)}, bf16[2,2,1,128,2048]{4,3,2,1,0:T(8,128)(2,1)S(1)}, u32[]{:S(2)}, u32[]{:S(2)}) collective-permute-start(bf16[2,2,1,128,2048]{4,3,2,1,0:T(8,128)(2,1)S(1)} %constant_dynamic-slice_fusion.14), channel_id=1, source_target_pairs={{0,4},{4,0},{8,12},{12,8},{16,20},{20,16},{24,28},{28,24},{1,5},{5... | collective-permute-start | bytes 6291464 | tf_op jit(solution)/shard_map/ppermute | solution.py:220
  95.9 19.5 %collective-permute-start.9 = (bf16[2,2,1,128,2048]{4,3,2,1,0:T(8,128)(2,1)S(1)}, bf16[2,2,1,128,2048]{4,3,2,1,0:T(8,128)(2,1)S(1)}, u32[]{:S(2)}, u32[]{:S(2)}) collective-permute-start(bf16[2,2,1,128,2048]{4,3,2,1,0:T(8,128)(2,1)S(1)} %constant_dynamic-slice_fusion.19), channel_id=1, source_target_pairs={{0,4},{4,0},{8,12},{12,8},{16,20},{20,16},{24,28},{28,24},{1,5},{5... | collective-permute-start | bytes 6291464 | tf_op jit(solution)/shard_map/ppermute | solution.py:220
  96.4 3.7 %collective-permute-start.35 = (f32[2,1,1,128,2]{3,4,2,1,0:T(2,128)S(1)}, f32[2,1,1,128,2]{3,4,2,1,0:T(2,128)S(1)}, u32[]{:S(2)}, u32[]{:S(2)}) collective-permute-start(f32[2,1,1,128,2]{3,4,2,1,0:T(2,128)S(1)} %constant_dynamic-slice_fusion.6), channel_id=1, source_target_pairs={{0,8},{4,12},{8,0},{12,4},{16,24},{20,28},{24,16},{28,20},{1,9},{5... | collective-permute-start | bytes 6152 | tf_op jit(solution)/shard_map/ppermute | solution.py:220
  97.0 3.6 %collective-permute-start.37 = (f32[1,2,1,128,2]{3,4,2,1,0:T(2,128)S(1)}, f32[1,2,1,128,2]{3,4,2,1,0:T(2,128)S(1)}, u32[]{:S(2)}, u32[]{:S(2)}) collective-permute-start(f32[1,2,1,128,2]{3,4,2,1,0:T(2,128)S(1)} %constant_dynamic-slice_fusion.2), channel_id=1, source_target_pairs={{0,16},{4,20},{8,24},{12,28},{16,0},{20,4},{24,8},{28,12},{1,17},{... | collective-permute-start | bytes 6152 | tf_op jit(solution)/shard_map/ppermute | solution.py:220
  100.0 3.6 %collective-permute-start.36 = (f32[1,1,1,128,2]{3,4,2,1,0:T(2,128)S(1)}, f32[1,1,1,128,2]{3,4,2,1,0:T(2,128)S(1)}, u32[]{:S(2)}, u32[]{:S(2)}) collective-permute-start(f32[1,1,1,128,2]{3,4,2,1,0:T(2,128)S(1)} %constant_dynamic-slice_fusion.4), channel_id=1, source_target_pairs={{0,16},{4,20},{8,24},{12,28},{16,0},{20,4},{24,8},{28,12},{1,17},{... | collective-permute-start | bytes 3080 | tf_op jit(solution)/shard_map/ppermute | solution.py:220
  100.6 3.6 %collective-permute-start.38 = (f32[1,1,1,128,2]{3,4,2,1,0:T(2,128)S(1)}, f32[1,1,1,128,2]{3,4,2,1,0:T(2,128)S(1)}, u32[]{:S(2)}, u32[]{:S(2)}) collective-permute-start(f32[1,1,1,128,2]{3,4,2,1,0:T(2,128)S(1)} %constant_dynamic-slice_fusion), channel_id=1, source_target_pairs={{0,8},{4,12},{8,0},{12,4},{16,24},{20,28},{24,16},{28,20},{1,9},{5... | collective-permute-start | bytes 3080 | tf_op jit(solution)/shard_map/ppermute | solution.py:220
  104.2 7.1 %collective-permute-start.39 = (f32[128,4]{0,1:T(4,128)S(1)}, f32[128,4]{0,1:T(4,128)S(1)}, u32[]{:S(2)}, u32[]{:S(2)}) collective-permute-start(f32[128,4]{0,1:T(4,128)S(1)} %pad_maximum_fusion.13), channel_id=1, source_target_pairs={{0,1},{1,2},{2,3},{3,0},{4,5},{5,6},{6,7},{7,4},{8,9},{9,10},{10,1... | collective-permute-start | bytes 6152 | tf_op jit(solution)/shard_map/ppermute | solution.py:261
  104.9 6.4 %collective-permute-start.40 = (f32[128,4]{0,1:T(4,128)S(1)}, f32[128,4]{0,1:T(4,128)S(1)}, u32[]{:S(2)}, u32[]{:S(2)}) collective-permute-start(f32[128,4]{0,1:T(4,128)S(1)} %pad_maximum_fusion.13), channel_id=1, source_target_pairs={{0,2},{1,3},{2,0},{3,1},{4,6},{5,7},{6,4},{7,5},{8,10},{9,11},{10,... | collective-permute-start | bytes 6152 | tf_op jit(solution)/shard_map/ppermute | solution.py:261
  105.3 6.1 %collective-permute-start.41 = (f32[128,4]{0,1:T(4,128)S(1)}, f32[128,4]{0,1:T(4,128)S(1)}, u32[]{:S(2)}, u32[]{:S(2)}) collective-permute-start(f32[128,4]{0,1:T(4,128)S(1)} %pad_maximum_fusion.13), channel_id=1, source_target_pairs={{0,3},{1,0},{2,1},{3,2},{4,7},{5,4},{6,5},{7,6},{8,11},{9,8},{10,9... | collective-permute-start | bytes 6152 | tf_op jit(solution)/shard_map/ppermute | solution.py:261
  113.2 14.9 %collective-permute-start.29 = (bf16[1,2,1,128,1024]{4,3,2,1,0:T(8,128)(2,1)S(1)}, bf16[1,2,1,128,1024]{4,3,2,1,0:T(8,128)(2,1)S(1)}, u32[]{:S(2)}, u32[]{:S(2)}) collective-permute-start(bf16[1,2,1,128,1024]{4,3,2,1,0:T(8,128)(2,1)S(1)} %constant_dynamic-slice_fusion.11), channel_id=1, source_target_pairs={{0,16},{4,20},{8,24},{12,28},{16,0},{20,4},{24,8},{28,12},{1,17},{... | collective-permute-start | bytes 1572872 | tf_op jit(solution)/shard_map/ppermute | solution.py:220
  114.8 15.1 %collective-permute-start.27 = (bf16[2,1,1,128,1024]{4,3,2,1,0:T(8,128)(2,1)S(1)}, bf16[2,1,1,128,1024]{4,3,2,1,0:T(8,128)(2,1)S(1)}, u32[]{:S(2)}, u32[]{:S(2)}) collective-permute-start(bf16[2,1,1,128,1024]{4,3,2,1,0:T(8,128)(2,1)S(1)} %constant_dynamic-slice_fusion.13), channel_id=1, source_target_pairs={{0,8},{4,12},{8,0},{12,4},{16,24},{20,28},{24,16},{28,20},{1,9},{5... | collective-permute-start | bytes 1572872 | tf_op jit(solution)/shard_map/ppermute | solution.py:220
  116.5 22.8 %collective-permute-start.12 = (bf16[1,2,1,128,1024]{4,3,2,1,0:T(8,128)(2,1)S(1)}, bf16[1,2,1,128,1024]{4,3,2,1,0:T(8,128)(2,1)S(1)}, u32[]{:S(2)}, u32[]{:S(2)}) collective-permute-start(bf16[1,2,1,128,1024]{4,3,2,1,0:T(8,128)(2,1)S(1)} %constant_dynamic-slice_fusion.16), channel_id=1, source_target_pairs={{0,16},{4,20},{8,24},{12,28},{16,0},{20,4},{24,8},{28,12},{1,17},{... | collective-permute-start | bytes 1572872 | tf_op jit(solution)/shard_map/ppermute | solution.py:220
  118.1 23.0 %collective-permute-start.10 = (bf16[2,1,1,128,1024]{4,3,2,1,0:T(8,128)(2,1)S(1)}, bf16[2,1,1,128,1024]{4,3,2,1,0:T(8,128)(2,1)S(1)}, u32[]{:S(2)}, u32[]{:S(2)}) collective-permute-start(bf16[2,1,1,128,1024]{4,3,2,1,0:T(8,128)(2,1)S(1)} %constant_dynamic-slice_fusion.18), channel_id=1, source_target_pairs={{0,8},{4,12},{8,0},{12,4},{16,24},{20,28},{24,16},{28,20},{1,9},{5... | collective-permute-start | bytes 1572872 | tf_op jit(solution)/shard_map/ppermute | solution.py:220
  128.3 16.7 %collective-permute-start.30 = (bf16[1,1,1,128,1024]{4,3,2,1,0:T(8,128)(2,1)S(1)}, bf16[1,1,1,128,1024]{4,3,2,1,0:T(8,128)(2,1)S(1)}, u32[]{:S(2)}, u32[]{:S(2)}) collective-permute-start(bf16[1,1,1,128,1024]{4,3,2,1,0:T(8,128)(2,1)S(1)} %constant_dynamic-slice_fusion.10), channel_id=1, source_target_pairs={{0,8},{4,12},{8,0},{12,4},{16,24},{20,28},{24,16},{28,20},{1,9},{5... | collective-permute-start | bytes 786440 | tf_op jit(solution)/shard_map/ppermute | solution.py:220
  130.1 15.0 %collective-permute-start.28 = (bf16[1,1,1,128,1024]{4,3,2,1,0:T(8,128)(2,1)S(1)}, bf16[1,1,1,128,1024]{4,3,2,1,0:T(8,128)(2,1)S(1)}, u32[]{:S(2)}, u32[]{:S(2)}) collective-permute-start(bf16[1,1,1,128,1024]{4,3,2,1,0:T(8,128)(2,1)S(1)} %constant_dynamic-slice_fusion.12), channel_id=1, source_target_pairs={{0,16},{4,20},{8,24},{12,28},{16,0},{20,4},{24,8},{28,12},{1,17},{... | collective-permute-start | bytes 786440 | tf_op jit(solution)/shard_map/ppermute | solution.py:220
  139.6 10.6 %collective-permute-start.13 = (bf16[1,1,1,128,1024]{4,3,2,1,0:T(8,128)(2,1)S(1)}, bf16[1,1,1,128,1024]{4,3,2,1,0:T(8,128)(2,1)S(1)}, u32[]{:S(2)}, u32[]{:S(2)}) collective-permute-start(bf16[1,1,1,128,1024]{4,3,2,1,0:T(8,128)(2,1)S(1)} %constant_dynamic-slice_fusion.15), channel_id=1, source_target_pairs={{0,8},{4,12},{8,0},{12,4},{16,24},{20,28},{24,16},{28,20},{1,9},{5... | collective-permute-start | bytes 786440 | tf_op jit(solution)/shard_map/ppermute | solution.py:220
  141.3 9.0 %collective-permute-start.11 = (bf16[1,1,1,128,1024]{4,3,2,1,0:T(8,128)(2,1)S(1)}, bf16[1,1,1,128,1024]{4,3,2,1,0:T(8,128)(2,1)S(1)}, u32[]{:S(2)}, u32[]{:S(2)}) collective-permute-start(bf16[1,1,1,128,1024]{4,3,2,1,0:T(8,128)(2,1)S(1)} %constant_dynamic-slice_fusion.17), channel_id=1, source_target_pairs={{0,16},{4,20},{8,24},{12,28},{16,0},{20,4},{24,8},{28,12},{1,17},{... | collective-permute-start | bytes 786440 | tf_op jit(solution)/shard_map/ppermute | solution.py:220
  145.5 8.3 %collective-permute-start.31 = (bf16[128,512]{1,0:T(8,128)(2,1)S(1)}, bf16[128,512]{1,0:T(8,128)(2,1)S(1)}, u32[]{:S(2)}, u32[]{:S(2)}) collective-permute-start(bf16[128,512]{1,0:T(8,128)(2,1)S(1)} %get-tuple-element.40), channel_id=1, source_target_pairs={{0,1},{1,2},{2,3},{3,0},{4,5},{5,6},{6,7},{7,4},{8,9},{9,10},{10,1... | collective-permute-start | bytes 393224 | tf_op jit(solution)/shard_map/ppermute | solution.py:261
  146.1 13.9 %collective-permute-start.32 = (bf16[128,512]{1,0:T(8,128)(2,1)S(1)}, bf16[128,512]{1,0:T(8,128)(2,1)S(1)}, u32[]{:S(2)}, u32[]{:S(2)}) collective-permute-start(bf16[128,512]{1,0:T(8,128)(2,1)S(1)} %get-tuple-element.41), channel_id=1, source_target_pairs={{0,2},{1,3},{2,0},{3,1},{4,6},{5,7},{6,4},{7,5},{8,10},{9,11},{10,... | collective-permute-start | bytes 393224 | tf_op jit(solution)/shard_map/ppermute | solution.py:261
  147.3 12.6 %collective-permute-start.33 = (bf16[128,512]{1,0:T(8,128)(2,1)S(1)}, bf16[128,512]{1,0:T(8,128)(2,1)S(1)}, u32[]{:S(2)}, u32[]{:S(2)}) collective-permute-start(bf16[128,512]{1,0:T(8,128)(2,1)S(1)} %get-tuple-element.42), channel_id=1, source_target_pairs={{0,3},{1,0},{2,1},{3,2},{4,7},{5,4},{6,5},{7,6},{8,11},{9,8},{10,9... | collective-permute-start | bytes 393224 | tf_op jit(solution)/shard_map/ppermute | solution.py:261
  150.6 10.1 %collective-permute-start.14 = (bf16[128,512]{1,0:T(8,128)(2,1)S(1)}, bf16[128,512]{1,0:T(8,128)(2,1)S(1)}, u32[]{:S(2)}, u32[]{:S(2)}) collective-permute-start(bf16[128,512]{1,0:T(8,128)(2,1)S(1)} %get-tuple-element.43), channel_id=1, source_target_pairs={{0,1},{1,2},{2,3},{3,0},{4,5},{5,6},{6,7},{7,4},{8,9},{9,10},{10,1... | collective-permute-start | bytes 393224 | tf_op jit(solution)/shard_map/ppermute | solution.py:261
  150.7 12.5 %collective-permute-start.15 = (bf16[128,512]{1,0:T(8,128)(2,1)S(1)}, bf16[128,512]{1,0:T(8,128)(2,1)S(1)}, u32[]{:S(2)}, u32[]{:S(2)}) collective-permute-start(bf16[128,512]{1,0:T(8,128)(2,1)S(1)} %get-tuple-element.44), channel_id=1, source_target_pairs={{0,2},{1,3},{2,0},{3,1},{4,6},{5,7},{6,4},{7,5},{8,10},{9,11},{10,... | collective-permute-start | bytes 393224 | tf_op jit(solution)/shard_map/ppermute | solution.py:261
  153.8 9.4 %collective-permute-start.16 = (bf16[128,512]{1,0:T(8,128)(2,1)S(1)}, bf16[128,512]{1,0:T(8,128)(2,1)S(1)}, u32[]{:S(2)}, u32[]{:S(2)}) collective-permute-start(bf16[128,512]{1,0:T(8,128)(2,1)S(1)} %get-tuple-element.45), channel_id=1, source_target_pairs={{0,3},{1,0},{2,1},{3,2},{4,7},{5,4},{6,5},{7,6},{8,11},{9,8},{10,9... | collective-permute-start | bytes 393224 | tf_op jit(solution)/shard_map/ppermute | solution.py:261

commit v4 on v3

--- a/solution.py
+++ b/solution.py
@@ -151,9 +151,11 @@
     me = lax.axis_index("dp")
     choose = route_expert.shape[1]
     routes = jnp.concatenate([route_expert.astype(jnp.float32), route_weight], axis=1)
-    arrived = gather_tokens(tokens)
+    halves = gather_chips(tokens)
+    cot_mine, halves = lax.optimization_barrier((gather_columns(cotangent), halves))
+    arrived = gather_pair(halves)
     routes = gather_small(routes.T[None]).swapaxes(1, 2).reshape(-1, 2 * choose)
-    cot_all = gather_tokens(gather_columns(cotangent))
+    cot_all = gather_pair(gather_chips(cot_mine))
     experts, weights = routes[:, :choose], routes[:, choose:]
     chosen = experts == me.astype(jnp.float32)
     row_weight = jnp.sum(jnp.where(chosen, weights, 0.0), axis=1, keepdims=True)
@@ -198,19 +200,22 @@
             up_in, up_local, (((1,), (0,)), ((), ())), preferred_element_type=jnp.float32
         )
     ).astype(jnp.bfloat16)
+    input_part, gate_late, up_late, hidden_late = lax.optimization_barrier(
+        (input_part, gate_in, up_in, hidden)
+    )
     token_grad = reduce_home(input_part)
     route_row = jnp.sum(hidden.astype(jnp.float32) * hidden_grad, axis=1, keepdims=True)
     route_row = route_row / jnp.where(row_weight > 0.0, row_weight, 1.0)
     route_part = jnp.where(chosen, route_row, 0.0)
     route_grad = sum_shares(sum_tokens(route_part.reshape(-1, tokens.shape[0], choose)))
     down_grad = lax.dot_general(
-        hidden, out_grad, (((0,), (0,)), ((), ())), preferred_element_type=jnp.float32
+        hidden_late, out_grad, (((0,), (0,)), ((), ())), preferred_element_type=jnp.float32
     )
     gate_grad = lax.dot_general(
-        gate_in, arrived, (((0,), (0,)), ((), ())), preferred_element_type=jnp.float32
+        gate_late, arrived, (((0,), (0,)), ((), ())), preferred_element_type=jnp.float32
     )
     up_grad = lax.dot_general(
-        up_in, arrived, (((0,), (0,)), ((), ())), preferred_element_type=jnp.float32
+        up_late, arrived, (((0,), (0,)), ((), ())), preferred_element_type=jnp.float32
     )
     return (mixed, token_grad, route_grad, gate_grad[None], up_grad[None], down_grad[None])
 
@@ -236,7 +241,7 @@
     return jnp.where(first, block, other), jnp.where(first, other, block)
 
 
-def gather_tokens(mine):
+def gather_chips(mine):
     rows, width = mine.shape
     upper = bits()[1:]
     halves = []
@@ -246,8 +251,12 @@
             axis = len(upper) - 1 - upper.index(bit)
             block = jnp.concatenate(in_order(block, bit), axis=axis)
         halves.append(block.reshape(-1, rows, width // 2))
+    return halves
+
+
+def gather_pair(halves):
     both = [jnp.stack(in_order(half, bits()[0]), axis=1) for half in halves]
-    return jnp.concatenate(both, axis=-1).reshape(-1, width)
+    return jnp.concatenate(both, axis=-1).reshape(-1, 2 * halves[0].shape[-1])
 
 
 def gather_small(block):

time: 164 us -> 157 us (0.957)
  other arithmetic: 18.4 us -> 14.6 us
  local copies, waits for them, and re-layouts: 10.9 us -> 7.96 us
  waiting for transfers between devices: 65.6 us -> 62.9 us
  starting transfers between devices: 43.1 us -> 44.9 us
    convert_element_type x1, other arithmetic: 4.2 us -> 0.77 us  [dense(): (cot_all.astype(jnp.float32) * row_weight * scale).astype(jnp.bfloat16)]
    convert_element_type x1, local copies, waits for them, and re-layouts: 3.88 us -> 1.1 us  [dense(): cot_all.astype(jnp.float32) * row_weight * scale]
    ppermute x30, waiting for transfers between devices: 56.1 us -> 53.3 us  [swap(): return lax.ppermute(block, 'dp', [(i, i ^ bit) for i in range(owners)])]
    ppermute x30, starting transfers between devices: 25.2 us -> 27 us  [swap(): return lax.ppermute(block, 'dp', [(i, i ^ bit) for i in range(owners)])]
  transfers between devices with their start and end apart: 42 -> 42, of which waited for: 18 -> 16; matrix products, arithmetic and copies ran while one was open for 16% -> 14% of each run, Pallas kernels for 0% -> 0%
where the time goes in v4:
time: 157 us; the launch traced here: 156 us
  waiting for transfers between devices  62.9 us (40%)
  starting transfers between devices  44.9 us (29%)
  matrix products  24.5 us (16%)
  other arithmetic  14.6 us (9%)
  local copies, waits for them, and re-layouts  7.96 us (5%)
    ppermute x30, waiting for transfers between devices, swap(): return lax.ppermute(block, 'dp', [(i, i ^ bit) for i in range(owners)])  53.3 us
    ppermute x30, starting transfers between devices, swap(): return lax.ppermute(block, 'dp', [(i, i ^ bit) for i in range(owners)])  27 us
    ppermute x12, starting transfers between devices, shift(): lax.ppermute(block, 'expert', [(i, (i + by) % shares) for i in range(shar...  18 us
    ppermute x12, waiting for transfers between devices, shift(): lax.ppermute(block, 'expert', [(i, (i + by) % shares) for i in range(shar...  9.54 us
    dot_general x1, matrix products, dense(): lax.dot_general(hidden_late, out_grad, (((0,), (0,)), ((), ())), preferre...  3.27 us
    dot_general x1, matrix products, dense(): lax.dot_general(up_late, arrived, (((0,), (0,)), ((), ())), preferred_ele...  3.27 us
    dot_general x1, matrix products, dense(): lax.dot_general(gate_late, arrived, (((0,), (0,)), ((), ())), preferred_e...  3.26 us
  transfers between devices with their start and end apart: 42, of which 16 were waited for; matrix products, arithmetic and copies ran while one was open for 14% of the time, Pallas kernels for 0%

profile of v4, /device:TPU:0, one launch (start us, length us, event | category | flops | bytes accessed | tf_op | source)
XLA Modules:
  0.0 156.2 jit_solution(12497118199795235008)
XLA Ops:
  0.6 3.1 %collective-permute-start = (bf16[128,512]{1,0:T(8,128)(2,1)}, bf16[128,512]{1,0:T(8,128)(2,1)S(1)}, u32[]{:S(2)}, u32[]{:S(2)}) collective-permute-start(bf16[128,512]{1,0:T(8,128)(2,1)} %param.19), channel_id=1, source_target_pairs={{0,1},{1,2},{2,3},{3,0},{4,5},{5,6},{6,7},{7,4},{8,9},{9,10},{10,1... | collective-permute-start | bytes 393224 | tf_op jit(solution)/shard_map/ppermute | solution.py:270
  3.7 2.6 %collective-permute-start.1 = (bf16[128,512]{1,0:T(8,128)(2,1)}, bf16[128,512]{1,0:T(8,128)(2,1)S(1)}, u32[]{:S(2)}, u32[]{:S(2)}) collective-permute-start(bf16[128,512]{1,0:T(8,128)(2,1)} %param.19), channel_id=1, source_target_pairs={{0,2},{1,3},{2,0},{3,1},{4,6},{5,7},{6,4},{7,5},{8,10},{9,11},{10,... | collective-permute-start | bytes 393224 | tf_op jit(solution)/shard_map/ppermute | solution.py:270
  6.3 1.1 slice_bitcast_fusion.2
  7.4 1.6 collective-permute-start.3
  8.9 1.5 collective-permute-start.5
  10.5 0.7 convert_element_type.162
  11.1 0.7 maximum_bitcast_fusion.1
  11.8 0.9 constant_dynamic-slice_fusion.20
  12.8 0.9 constant_dynamic-update-slice_fusion.3
  13.7 0.7 reduce
  14.4 0.7 reduce.1
  15.2 1.4 collective-permute-start.2
  16.6 0.7 broadcast_select_fusion.22
  17.3 1.1 broadcast_select_fusion.11
  18.5 0.6 collective-permute-start.6
  19.1 1.5 collective-permute-start.10
  21.4 11.3 %collective-permute-done.6 = bf16[2,1,128,1024]{3,2,1,0:T(8,128)(2,1)S(1)} collective-permute-done((bf16[2,1,128,1024]{3,2,1,0:T(8,128)(2,1)S(1)}, bf16[2,1,128,1024]{3,2,1,0:T(8,128)(2,1)S(1)}, u32[]{:S(2)}, u32[]{:S(2)}) %collective-permute-start.6) | collective-permute-done | bytes 524320 | tf_op jit(solution)/shard_map/ppermute | solution.py:225
  32.8 1.3 collective-permute-done.4
  34.4 0.6 collective-permute-start.20
  35.5 1.6 %collective-permute-start.11 = (f32[4,8,128]{2,1,0:T(8,128)S(1)}, f32[4,8,128]{2,1,0:T(8,128)S(1)}, u32[]{:S(2)}, u32[]{:S(2)}) collective-permute-start(f32[4,8,128]{2,1,0:T(8,128)S(1)} %pad_maximum_fusion.11), channel_id=1, source_target_pairs={{0,16},{4,20},{8,24},{12,28},{16,0},{20,4},{24,8},{28,12},{1,17},{... | collective-permute-start | bytes 49160 | tf_op jit(solution)/shard_map/ppermute | solution.py:225
  37.1 4.3 %collective-permute-done.20 = bf16[1,1,128,1024]{3,2,1,0:T(8,128)(2,1)S(1)} collective-permute-done((bf16[1,1,128,1024]{3,2,1,0:T(8,128)(2,1)S(1)}, bf16[1,1,128,1024]{3,2,1,0:T(8,128)(2,1)S(1)}, u32[]{:S(2)}, u32[]{:S(2)}) %collective-permute-start.20) | collective-permute-done | bytes 262176 | tf_op jit(solution)/shard_map/ppermute | solution.py:225
  42.7 1.6 collective-permute-start.24
  44.6 8.7 %collective-permute-done.21 = bf16[1,2,128,1024]{3,2,1,0:T(8,128)(2,1)S(1)} collective-permute-done((bf16[1,2,128,1024]{3,2,1,0:T(8,128)(2,1)S(1)}, bf16[1,2,128,1024]{3,2,1,0:T(8,128)(2,1)S(1)}, u32[]{:S(2)}, u32[]{:S(2)}) %collective-permute-start.21) | collective-permute-done | bytes 524320 | tf_op jit(solution)/shard_map/ppermute | solution.py:225
  53.6 3.6 %collective-permute-done.24 = bf16[2,1,128,1024]{3,2,1,0:T(8,128)(2,1)S(1)} collective-permute-done((bf16[2,1,128,1024]{3,2,1,0:T(8,128)(2,1)S(1)}, bf16[2,1,128,1024]{3,2,1,0:T(8,128)(2,1)S(1)}, u32[]{:S(2)}, u32[]{:S(2)}) %collective-permute-start.24) | collective-permute-done | bytes 524320 | tf_op jit(solution)/shard_map/ppermute | solution.py:225
  58.2 1.0 copy-done.3
  59.3 2.8 %convolution_multiply_fusion.1 = f32[1024,352]{0,1:T(8,128)} fusion(bf16[1024,2048]{1,0:T(8,128)(2,1)S(1)} %bitcast.131, bf16[1,352,2048]{2,1,0:T(8,128)(2,1)S(1)} %copy-done.3, f32[352]{0:T(512)S(1)} %reduce), kind=kOutput, calls=%fused_computation.23 | convolution fusion | flops 1476755456 | bytes 7079296 | tf_op jit(solution)/shard_map/dot_general | solution.py:165
  62.7 1.3 maximum_convert_fusion
  64.2 1.1 copy.23
  65.7 0.8 fusion.1
  67.1 1.9 %fusion.2 = f32[1024,352]{0,1:T(8,128)S(1)} fusion(bf16[1024,1024]{1,0:T(8,128)(2,1)S(1)} %bitcast.136, bf16[1024,1024]{1,0:T(8,128)(2,1)S(1)} %bitcast.135, f32[2048]{0:T(1024)S(1)} %bitcast.140, f32[1024]{0:T(1024)S(1)} %get-tuple-element.22, bf16[1,352,2048]{2,1,0:T(8,128)(2,1)S(1)} %copy-done.5), kind=kOutput, calls=%fused_computation.6 | convolution fusion | flops 1491075072 | bytes 7090176 | tf_op jit(solution)/shard_map/dot_general | solution.py:188
  69.7 2.5 %multiply_reduce_fusion = (f32[1024]{0:T(1024)S(1)}, bf16[1024,352]{0,1:T(8,128)(2,1)S(1)}, bf16[1024,352]{0,1:T(8,128)(2,1)S(1)}, bf16[1024,352]{0,1:T(8,128)(2,1)S(1)}) fusion(f32[1024,352]{0,1:T(8,128)S(1)} %fusion.2, f32[1024,352]{0,1:T(8,128)S(1)} %copy-done.6, f32[352]{0:T(512)S(1)} %reduce, f32[352]{0:T(512)S(1)} %reduce.1, ...), kind=kOutput, calls=%fused_computation.31 | convolution fusion | flops 1483963392 | bytes 10689280 | tf_op jit(solution)/shard_map/dot_general | solution.py:171
  72.2 2.4 %fusion.12 = f32[1024,2048]{1,0:T(8,128)S(1)} fusion(bf16[1024,352]{0,1:T(8,128)(2,1)S(1)} %get-tuple-element.17, bf16[1,352,2048]{2,1,0:T(8,128)(2,1)S(1)} %copy-done.4), kind=kOutput, calls=%fused_computation.28 | convolution fusion | flops 1476395008 | bytes 10551296 | tf_op jit(solution)/shard_map/dot_general | solution.py:196
  74.6 2.4 %multiply_convert_fusion.1 = bf16[1024,2048]{1,0:T(8,128)(2,1)S(1)} fusion(bf16[1024,352]{0,1:T(8,128)(2,1)S(1)} %get-tuple-element.19, f32[2048]{0:T(1024)S(1)} %bitcast.141, f32[1024]{0:T(1024)S(1)} %get-tuple-element.22, bf16[1,352,2048]{2,1,0:T(8,128)(2,1)S(1)} %copy-done.5), kind=kOutput, calls=%fused_computation.5 | convolution fusion | flops 1482686464 | bytes 6369280 | tf_op jit(solution)/shard_map/dot_general | solution.py:180
  77.0 2.8 %add_convert_fusion = bf16[1024,2048]{1,0:T(8,128)(2,1)S(1)} fusion(f32[1024,2048]{1,0:T(8,128)S(1)} %fusion.12, bf16[1024,352]{0,1:T(8,128)(2,1)S(1)} %get-tuple-element.18, bf16[1,352,2048]{2,1,0:T(8,128)(2,1)S(1)} %copy-done), kind=kOutput, calls=%fused_computation.3 | convolution fusion | flops 1480589312 | bytes 14745600 | tf_op jit(solution)/shard_map/dot_general | solution.py:199
  79.8 3.3 %convolution_bitcast_fusion.1 = f32[1,352,2048]{2,1,0:T(8,128)} fusion(bf16[1024,352]{0,1:T(8,128)(2,1)S(1)} %get-tuple-element.18, bf16[1024,2048]{1,0:T(8,128)(2,1)S(1)} %bitcast.133), kind=kOutput, calls=%fused_computation.17 | convolution fusion | flops 1476395008 | bytes 7798784 | tf_op jit(solution)/shard_map/dot_general | solution.py:217
  83.0 3.3 %convolution_bitcast_fusion.2 = f32[1,352,2048]{2,1,0:T(8,128)} fusion(bf16[1024,352]{0,1:T(8,128)(2,1)S(1)} %get-tuple-element.17, bf16[1024,2048]{1,0:T(8,128)(2,1)S(1)} %bitcast.134), kind=kOutput, calls=%fused_computation.18 | convolution fusion | flops 1476395008 | bytes 7798784 | tf_op jit(solution)/shard_map/dot_general | solution.py:214
  88.1 1.6 collective-permute-start.35
  89.6 1.5 collective-permute-start.37
  91.7 1.5 collective-permute-start.36
  93.2 1.6 collective-permute-start.38
  95.3 1.6 %collective-permute-done.38 = f32[1,1,1,128,2]{3,4,2,1,0:T(2,128)S(1)} collective-permute-done((f32[1,1,1,128,2]{3,4,2,1,0:T(2,128)S(1)}, f32[1,1,1,128,2]{3,4,2,1,0:T(2,128)S(1)}, u32[]{:S(2)}, u32[]{:S(2)}) %collective-permute-start.38) | collective-permute-done | bytes 1056 | tf_op jit(solution)/shard_map/ppermute | solution.py:225
  96.9 0.7 collective-permute-start.39
  98.0 2.8 %collective-permute-start.41 = (f32[128,4]{0,1:T(4,128)S(1)}, f32[128,4]{0,1:T(4,128)S(1)}, u32[]{:S(2)}, u32[]{:S(2)}) collective-permute-start(f32[128,4]{0,1:T(4,128)S(1)} %pad_maximum_fusion.13), channel_id=1, source_target_pairs={{0,3},{1,0},{2,1},{3,2},{4,7},{5,4},{6,5},{7,6},{8,11},{9,8},{10,9... | collective-permute-start | bytes 6152 | tf_op jit(solution)/shard_map/ppermute | solution.py:270
  100.8 3.3 %convolution_bitcast_fusion = f32[1,352,2048]{2,1,0:T(8,128)} fusion(bf16[1024,352]{0,1:T(8,128)(2,1)S(1)} %get-tuple-element.19, bf16[1024,2048]{1,0:T(8,128)(2,1)S(1)} %fusion.1), kind=kOutput, calls=%fused_computation.16 | convolution fusion | flops 1476395008 | bytes 7798784 | tf_op jit(solution)/shard_map/dot_general | solution.py:211
  104.6 0.8 add_convert_fusion.1
  105.7 1.5 collective-permute-start.29
  107.2 0.6 collective-permute-start.27
  107.9 0.8 add_convert_fusion.2
  109.0 1.6 %collective-permute-start.15 = (bf16[1,2,1,128,1024]{4,3,2,1,0:T(8,128)(2,1)S(1)}, bf16[1,2,1,128,1024]{4,3,2,1,0:T(8,128)(2,1)S(1)}, u32[]{:S(2)}, u32[]{:S(2)}) collective-permute-start(bf16[1,2,1,128,1024]{4,3,2,1,0:T(8,128)(2,1)S(1)} %constant_dynamic-slice_fusion.16), channel_id=1, source_target_pairs={{0,16},{4,20},{8,24},{12,28},{16,0},{20,4},{24,8},{28,12},{1,17},{... | collective-permute-start | bytes 1572872 | tf_op jit(solution)/shard_map/ppermute | solution.py:225
  111.2 9.5 %collective-permute-done.29 = bf16[1,2,1,128,1024]{4,3,2,1,0:T(8,128)(2,1)S(1)} collective-permute-done((bf16[1,2,1,128,1024]{4,3,2,1,0:T(8,128)(2,1)S(1)}, bf16[1,2,1,128,1024]{4,3,2,1,0:T(8,128)(2,1)S(1)}, u32[]{:S(2)}, u32[]{:S(2)}) %collective-permute-start.29) | collective-permute-done | bytes 524320 | tf_op jit(solution)/shard_map/ppermute | solution.py:225
  120.9 1.6 collective-permute-start.30
  123.3 8.6 %collective-permute-done.15 = bf16[1,2,1,128,1024]{4,3,2,1,0:T(8,128)(2,1)S(1)} collective-permute-done((bf16[1,2,1,128,1024]{4,3,2,1,0:T(8,128)(2,1)S(1)}, bf16[1,2,1,128,1024]{4,3,2,1,0:T(8,128)(2,1)S(1)}, u32[]{:S(2)}, u32[]{:S(2)}) %collective-permute-start.15) | collective-permute-done | bytes 524320 | tf_op jit(solution)/shard_map/ppermute | solution.py:225
  132.1 1.6 collective-permute-start.16
  134.5 2.9 %collective-permute-done.30 = bf16[1,1,1,128,1024]{4,3,2,1,0:T(8,128)(2,1)S(1)} collective-permute-done((bf16[1,1,1,128,1024]{4,3,2,1,0:T(8,128)(2,1)S(1)}, bf16[1,1,1,128,1024]{4,3,2,1,0:T(8,128)(2,1)S(1)}, u32[]{:S(2)}, u32[]{:S(2)}) %collective-permute-start.30) | collective-permute-done | bytes 262176 | tf_op jit(solution)/shard_map/ppermute | solution.py:225
  137.8 0.6 collective-permute-start.31
  138.5 1.3 collective-permute-start.32
  139.7 2.8 %collective-permute-start.33 = (bf16[128,512]{1,0:T(8,128)(2,1)S(1)}, bf16[128,512]{1,0:T(8,128)(2,1)S(1)}, u32[]{:S(2)}, u32[]{:S(2)}) collective-permute-start(bf16[128,512]{1,0:T(8,128)(2,1)S(1)} %get-tuple-element.56), channel_id=1, source_target_pairs={{0,3},{1,0},{2,1},{3,2},{4,7},{5,4},{6,5},{7,6},{8,11},{9,8},{10,9... | collective-permute-start | bytes 393224 | tf_op jit(solution)/shard_map/ppermute | solution.py:270
  143.0 1.2 collective-permute-start.18
  144.3 1.9 %collective-permute-done.31 = bf16[128,512]{1,0:T(8,128)(2,1)S(1)} collective-permute-done((bf16[128,512]{1,0:T(8,128)(2,1)S(1)}, bf16[128,512]{1,0:T(8,128)(2,1)S(1)}, u32[]{:S(2)}, u32[]{:S(2)}) %collective-permute-start.31) | collective-permute-done | bytes 131104 | tf_op jit(solution)/shard_map/ppermute | solution.py:270
  146.2 1.0 collective-permute-start.19
  147.1 5.1 %collective-permute-done.32 = bf16[128,512]{1,0:T(8,128)(2,1)S(1)} collective-permute-done((bf16[128,512]{1,0:T(8,128)(2,1)S(1)}, bf16[128,512]{1,0:T(8,128)(2,1)S(1)}, u32[]{:S(2)}, u32[]{:S(2)}) %collective-permute-start.32) | collective-permute-done | bytes 131104 | tf_op jit(solution)/shard_map/ppermute | solution.py:270
  152.2 0.8 add_convert_fusion.11
  153.0 2.4 %collective-permute-done.18 = bf16[128,512]{1,0:T(8,128)(2,1)S(1)} collective-permute-done((bf16[128,512]{1,0:T(8,128)(2,1)S(1)}, bf16[128,512]{1,0:T(8,128)(2,1)S(1)}, u32[]{:S(2)}, u32[]{:S(2)}) %collective-permute-start.18) | collective-permute-done | bytes 131104 | tf_op jit(solution)/shard_map/ppermute | solution.py:270
  155.5 0.8 add_convert_fusion.12
  (129 shorter events, 14.9 us)
Async XLA Ops:
  0.6 68.3 %copy-start = (bf16[1,352,2048]{2,1,0:T(8,128)(2,1)S(1)}, bf16[1,352,2048]{2,1,0:T(8,128)(2,1)}, u32[]{:S(2)}) copy-start(bf16[1,352,2048]{2,1,0:T(8,128)(2,1)} %param.14) | copy-start | bytes 4325380
  0.6 19.9 %collective-permute-start = (bf16[128,512]{1,0:T(8,128)(2,1)}, bf16[128,512]{1,0:T(8,128)(2,1)S(1)}, u32[]{:S(2)}, u32[]{:S(2)}) collective-permute-start(bf16[128,512]{1,0:T(8,128)(2,1)} %param.19), channel_id=1, source_target_pairs={{0,1},{1,2},{2,3},{3,0},{4,5},{5,6},{6,7},{7,4},{8,9},{9,10},{10,1... | collective-permute-start | bytes 393224 | tf_op jit(solution)/shard_map/ppermute | solution.py:270
  3.7 17.5 %collective-permute-start.1 = (bf16[128,512]{1,0:T(8,128)(2,1)}, bf16[128,512]{1,0:T(8,128)(2,1)S(1)}, u32[]{:S(2)}, u32[]{:S(2)}) collective-permute-start(bf16[128,512]{1,0:T(8,128)(2,1)} %param.19), channel_id=1, source_target_pairs={{0,2},{1,3},{2,0},{3,1},{4,6},{5,7},{6,4},{7,5},{8,10},{9,11},{10,... | collective-permute-start | bytes 393224 | tf_op jit(solution)/shard_map/ppermute | solution.py:270
  7.4 9.9 %collective-permute-start.3 = (bf16[1,1,128,1024]{3,2,1,0:T(8,128)(2,1)S(1)}, bf16[1,1,128,1024]{3,2,1,0:T(8,128)(2,1)S(1)}, u32[]{:S(2)}, u32[]{:S(2)}) collective-permute-start(bf16[1,1,128,1024]{3,2,1,0:T(8,128)(2,1)S(1)} %get-tuple-element.67), channel_id=1, source_target_pairs={{0,8},{4,12},{8,0},{12,4},{16,24},{20,28},{24,16},{28,20},{1,9},{5... | collective-permute-start | bytes 786440 | tf_op jit(solution)/shard_map/ppermute | solution.py:225
  8.9 8.3 %collective-permute-start.5 = (bf16[1,1,128,1024]{3,2,1,0:T(8,128)(2,1)S(1)}, bf16[1,1,128,1024]{3,2,1,0:T(8,128)(2,1)S(1)}, u32[]{:S(2)}, u32[]{:S(2)}) collective-permute-start(bf16[1,1,128,1024]{3,2,1,0:T(8,128)(2,1)S(1)} %get-tuple-element.66), channel_id=1, source_target_pairs={{0,16},{4,20},{8,24},{12,28},{16,0},{20,4},{24,8},{28,12},{1,17},{... | collective-permute-start | bytes 786440 | tf_op jit(solution)/shard_map/ppermute | solution.py:225
  11.8 3.3 %collective-permute-start.9 = (f32[1,8,128]{2,1,0:T(8,128)S(1)}, f32[1,8,128]{2,1,0:T(8,128)S(1)}, u32[]{:S(2)}, u32[]{:S(2)}) collective-permute-start(f32[1,8,128]{2,1,0:T(8,128)S(1)} %maximum_bitcast_fusion.1), channel_id=1, source_target_pairs={{0,4},{4,0},{8,12},{12,8},{16,20},{20,16},{24,28},{28,24},{1,5},{5... | collective-permute-start | bytes 12296 | tf_op jit(solution)/shard_map/ppermute | solution.py:225
  15.2 6.2 %collective-permute-start.2 = (bf16[128,512]{1,0:T(8,128)(2,1)}, bf16[128,512]{1,0:T(8,128)(2,1)S(1)}, u32[]{:S(2)}, u32[]{:S(2)}) collective-permute-start(bf16[128,512]{1,0:T(8,128)(2,1)} %param.19), channel_id=1, source_target_pairs={{0,3},{1,0},{2,1},{3,2},{4,7},{5,4},{6,5},{7,6},{8,11},{9,8},{10,9... | collective-permute-start | bytes 393224 | tf_op jit(solution)/shard_map/ppermute | solution.py:270
  18.5 14.2 %collective-permute-start.6 = (bf16[2,1,128,1024]{3,2,1,0:T(8,128)(2,1)S(1)}, bf16[2,1,128,1024]{3,2,1,0:T(8,128)(2,1)S(1)}, u32[]{:S(2)}, u32[]{:S(2)}) collective-permute-start(bf16[2,1,128,1024]{3,2,1,0:T(8,128)(2,1)S(1)} %pad_maximum_fusion.8), channel_id=1, source_target_pairs={{0,8},{4,12},{8,0},{12,4},{16,24},{20,28},{24,16},{28,20},{1,9},{5... | collective-permute-start | bytes 1572872 | tf_op jit(solution)/shard_map/ppermute | solution.py:225
  19.1 16.5 %collective-permute-start.10 = (f32[2,8,128]{2,1,0:T(8,128)S(1)}, f32[2,8,128]{2,1,0:T(8,128)S(1)}, u32[]{:S(2)}, u32[]{:S(2)}) collective-permute-start(f32[2,8,128]{2,1,0:T(8,128)S(1)} %pad_maximum_fusion.12), channel_id=1, source_target_pairs={{0,8},{4,12},{8,0},{12,4},{16,24},{20,28},{24,16},{28,20},{1,9},{5... | collective-permute-start | bytes 24584 | tf_op jit(solution)/shard_map/ppermute | solution.py:225
  20.6 13.5 %collective-permute-start.4 = (bf16[1,2,128,1024]{3,2,1,0:T(8,128)(2,1)S(1)}, bf16[1,2,128,1024]{3,2,1,0:T(8,128)(2,1)S(1)}, u32[]{:S(2)}, u32[]{:S(2)}) collective-permute-start(bf16[1,2,128,1024]{3,2,1,0:T(8,128)(2,1)S(1)} %pad_maximum_fusion.7), channel_id=1, source_target_pairs={{0,16},{4,20},{8,24},{12,28},{16,0},{20,4},{24,8},{28,12},{1,17},{... | collective-permute-start | bytes 1572872 | tf_op jit(solution)/shard_map/ppermute | solution.py:225
  34.4 7.0 %collective-permute-start.20 = (bf16[1,1,128,1024]{3,2,1,0:T(8,128)(2,1)S(1)}, bf16[1,1,128,1024]{3,2,1,0:T(8,128)(2,1)S(1)}, u32[]{:S(2)}, u32[]{:S(2)}) collective-permute-start(bf16[1,1,128,1024]{3,2,1,0:T(8,128)(2,1)S(1)} %get-tuple-element.62), channel_id=1, source_target_pairs={{0,8},{4,12},{8,0},{12,4},{16,24},{20,28},{24,16},{28,20},{1,9},{5... | collective-permute-start | bytes 786440 | tf_op jit(solution)/shard_map/ppermute | solution.py:225
  35.0 6.9 %collective-permute-start.23 = (bf16[1,1,128,1024]{3,2,1,0:T(8,128)(2,1)S(1)}, bf16[1,1,128,1024]{3,2,1,0:T(8,128)(2,1)S(1)}, u32[]{:S(2)}, u32[]{:S(2)}) collective-permute-start(bf16[1,1,128,1024]{3,2,1,0:T(8,128)(2,1)S(1)} %get-tuple-element.63), channel_id=1, source_target_pairs={{0,16},{4,20},{8,24},{12,28},{16,0},{20,4},{24,8},{28,12},{1,17},{... | collective-permute-start | bytes 786440 | tf_op jit(solution)/shard_map/ppermute | solution.py:225
  35.5 7.0 %collective-permute-start.11 = (f32[4,8,128]{2,1,0:T(8,128)S(1)}, f32[4,8,128]{2,1,0:T(8,128)S(1)}, u32[]{:S(2)}, u32[]{:S(2)}) collective-permute-start(f32[4,8,128]{2,1,0:T(8,128)S(1)} %pad_maximum_fusion.11), channel_id=1, source_target_pairs={{0,16},{4,20},{8,24},{12,28},{16,0},{20,4},{24,8},{28,12},{1,17},{... | collective-permute-start | bytes 49160 | tf_op jit(solution)/shard_map/ppermute | solution.py:225
  42.0 11.3 %collective-permute-start.21 = (bf16[1,2,128,1024]{3,2,1,0:T(8,128)(2,1)S(1)}, bf16[1,2,128,1024]{3,2,1,0:T(8,128)(2,1)S(1)}, u32[]{:S(2)}, u32[]{:S(2)}) collective-permute-start(bf16[1,2,128,1024]{3,2,1,0:T(8,128)(2,1)S(1)} %pad_maximum_fusion.9), channel_id=1, source_target_pairs={{0,16},{4,20},{8,24},{12,28},{16,0},{20,4},{24,8},{28,12},{1,17},{... | collective-permute-start | bytes 1572872 | tf_op jit(solution)/shard_map/ppermute | solution.py:225
  42.6 14.8 %collective-permute-start.7 = (bf16[4,128,1024]{2,1,0:T(8,128)(2,1)S(1)}, bf16[4,128,1024]{2,1,0:T(8,128)(2,1)S(1)}, u32[]{:S(2)}, u32[]{:S(2)}) collective-permute-start(bf16[4,128,1024]{2,1,0:T(8,128)(2,1)S(1)} %bitcast.127), channel_id=1, source_target_pairs={{0,4},{4,0},{8,12},{12,8},{16,20},{20,16},{24,28},{28,24},{1,5},{5... | collective-permute-start | bytes 3145736 | tf_op jit(solution)/shard_map/ppermute | solution.py:225
  42.7 14.4 %collective-permute-start.24 = (bf16[2,1,128,1024]{3,2,1,0:T(8,128)(2,1)S(1)}, bf16[2,1,128,1024]{3,2,1,0:T(8,128)(2,1)S(1)}, u32[]{:S(2)}, u32[]{:S(2)}) collective-permute-start(bf16[2,1,128,1024]{3,2,1,0:T(8,128)(2,1)S(1)} %pad_maximum_fusion.10), channel_id=1, source_target_pairs={{0,8},{4,12},{8,0},{12,4},{16,24},{20,28},{24,16},{28,20},{1,9},{5... | collective-permute-start | bytes 1572872 | tf_op jit(solution)/shard_map/ppermute | solution.py:225
  44.3 13.4 %collective-permute-start.8 = (bf16[4,128,1024]{2,1,0:T(8,128)(2,1)S(1)}, bf16[4,128,1024]{2,1,0:T(8,128)(2,1)S(1)}, u32[]{:S(2)}, u32[]{:S(2)}) collective-permute-start(bf16[4,128,1024]{2,1,0:T(8,128)(2,1)S(1)} %bitcast.125), channel_id=1, source_target_pairs={{0,4},{4,0},{8,12},{12,8},{16,20},{20,16},{24,28},{28,24},{1,5},{5... | collective-permute-start | bytes 3145736 | tf_op jit(solution)/shard_map/ppermute | solution.py:225
  53.5 8.6 %collective-permute-start.22 = (bf16[4,128,1024]{2,1,0:T(8,128)(2,1)S(1)}, bf16[4,128,1024]{2,1,0:T(8,128)(2,1)S(1)}, u32[]{:S(2)}, u32[]{:S(2)}) collective-permute-start(bf16[4,128,1024]{2,1,0:T(8,128)(2,1)S(1)} %bitcast.129), channel_id=1, source_target_pairs={{0,4},{4,0},{8,12},{12,8},{16,20},{20,16},{24,28},{28,24},{1,5},{5... | collective-permute-start | bytes 3145736 | tf_op jit(solution)/shard_map/ppermute | solution.py:225
  57.3 5.2 %collective-permute-start.25 = (bf16[4,128,1024]{2,1,0:T(8,128)(2,1)S(1)}, bf16[4,128,1024]{2,1,0:T(8,128)(2,1)S(1)}, u32[]{:S(2)}, u32[]{:S(2)}) collective-permute-start(bf16[4,128,1024]{2,1,0:T(8,128)(2,1)S(1)} %bitcast.130), channel_id=1, source_target_pairs={{0,4},{4,0},{8,12},{12,8},{16,20},{20,16},{24,28},{28,24},{1,5},{5... | collective-permute-start | bytes 3145736 | tf_op jit(solution)/shard_map/ppermute | solution.py:225
  57.8 1.4 copy-start.3
  58.2 3.9 %copy-start.1 = (bf16[4,2,128,2048]{3,2,1,0:T(8,128)(2,1)}, bf16[4,2,128,2048]{3,2,1,0:T(8,128)(2,1)S(1)}, u32[]{:S(2)}) copy-start(bf16[4,2,128,2048]{3,2,1,0:T(8,128)(2,1)S(1)} %maximum_maximum_fusion) | copy-start | bytes 12582916
  65.7 1.4 copy-start.5
  67.1 2.2 %copy-start.2 = (bf16[4,2,128,2048]{3,2,1,0:T(8,128)(2,1)S(1)}, bf16[4,2,128,2048]{3,2,1,0:T(8,128)(2,1)}, u32[]{:S(2)}) copy-start(bf16[4,2,128,2048]{3,2,1,0:T(8,128)(2,1)} %copy-done.1) | copy-start | bytes 12582916
  67.1 2.6 %copy-start.6 = (f32[1024,352]{0,1:T(8,128)S(1)}, f32[1024,352]{0,1:T(8,128)}, u32[]{:S(2)}) copy-start(f32[1024,352]{0,1:T(8,128)} %convolution_multiply_fusion.1) | copy-start | bytes 4325380
  69.7 2.5 %copy-start.4 = (bf16[1,352,2048]{2,1,0:T(8,128)(2,1)S(1)}, bf16[1,352,2048]{2,1,0:T(8,128)(2,1)}, u32[]{:S(2)}) copy-start(bf16[1,352,2048]{2,1,0:T(8,128)(2,1)} %param.13) | copy-start | bytes 4325380
  86.3 1.7 %collective-permute-start.34 = (f32[2,2,1,128,4]{3,4,2,1,0:T(4,128)S(1)}, f32[2,2,1,128,4]{3,4,2,1,0:T(4,128)S(1)}, u32[]{:S(2)}, u32[]{:S(2)}) collective-permute-start(f32[2,2,1,128,4]{3,4,2,1,0:T(4,128)S(1)} %constant_dynamic-slice_fusion.8), channel_id=1, source_target_pairs={{0,4},{4,0},{8,12},{12,8},{16,20},{20,16},{24,28},{28,24},{1,5},{5... | collective-permute-start | bytes 24584 | tf_op jit(solution)/shard_map/ppermute | solution.py:225
  87.1 17.5 %collective-permute-start.26 = (bf16[2,2,1,128,2048]{4,3,2,1,0:T(8,128)(2,1)S(1)}, bf16[2,2,1,128,2048]{4,3,2,1,0:T(8,128)(2,1)S(1)}, u32[]{:S(2)}, u32[]{:S(2)}) collective-permute-start(bf16[2,2,1,128,2048]{4,3,2,1,0:T(8,128)(2,1)S(1)} %constant_dynamic-slice_fusion.14), channel_id=1, source_target_pairs={{0,4},{4,0},{8,12},{12,8},{16,20},{20,16},{24,28},{28,24},{1,5},{5... | collective-permute-start | bytes 6291464 | tf_op jit(solution)/shard_map/ppermute | solution.py:225
  87.5 20.4 %collective-permute-start.12 = (bf16[2,2,1,128,2048]{4,3,2,1,0:T(8,128)(2,1)S(1)}, bf16[2,2,1,128,2048]{4,3,2,1,0:T(8,128)(2,1)S(1)}, u32[]{:S(2)}, u32[]{:S(2)}) collective-permute-start(bf16[2,2,1,128,2048]{4,3,2,1,0:T(8,128)(2,1)S(1)} %constant_dynamic-slice_fusion.19), channel_id=1, source_target_pairs={{0,4},{4,0},{8,12},{12,8},{16,20},{20,16},{24,28},{28,24},{1,5},{5... | collective-permute-start | bytes 6291464 | tf_op jit(solution)/shard_map/ppermute | solution.py:225
  88.1 3.7 %collective-permute-start.35 = (f32[2,1,1,128,2]{3,4,2,1,0:T(2,128)S(1)}, f32[2,1,1,128,2]{3,4,2,1,0:T(2,128)S(1)}, u32[]{:S(2)}, u32[]{:S(2)}) collective-permute-start(f32[2,1,1,128,2]{3,4,2,1,0:T(2,128)S(1)} %constant_dynamic-slice_fusion.6), channel_id=1, source_target_pairs={{0,8},{4,12},{8,0},{12,4},{16,24},{20,28},{24,16},{28,20},{1,9},{5... | collective-permute-start | bytes 6152 | tf_op jit(solution)/shard_map/ppermute | solution.py:225
  89.6 3.6 %collective-permute-start.37 = (f32[1,2,1,128,2]{3,4,2,1,0:T(2,128)S(1)}, f32[1,2,1,128,2]{3,4,2,1,0:T(2,128)S(1)}, u32[]{:S(2)}, u32[]{:S(2)}) collective-permute-start(f32[1,2,1,128,2]{3,4,2,1,0:T(2,128)S(1)} %constant_dynamic-slice_fusion.2), channel_id=1, source_target_pairs={{0,16},{4,20},{8,24},{12,28},{16,0},{20,4},{24,8},{28,12},{1,17},{... | collective-permute-start | bytes 6152 | tf_op jit(solution)/shard_map/ppermute | solution.py:225
  91.7 3.6 %collective-permute-start.36 = (f32[1,1,1,128,2]{3,4,2,1,0:T(2,128)S(1)}, f32[1,1,1,128,2]{3,4,2,1,0:T(2,128)S(1)}, u32[]{:S(2)}, u32[]{:S(2)}) collective-permute-start(f32[1,1,1,128,2]{3,4,2,1,0:T(2,128)S(1)} %constant_dynamic-slice_fusion.4), channel_id=1, source_target_pairs={{0,16},{4,20},{8,24},{12,28},{16,0},{20,4},{24,8},{28,12},{1,17},{... | collective-permute-start | bytes 3080 | tf_op jit(solution)/shard_map/ppermute | solution.py:225
  93.2 3.6 %collective-permute-start.38 = (f32[1,1,1,128,2]{3,4,2,1,0:T(2,128)S(1)}, f32[1,1,1,128,2]{3,4,2,1,0:T(2,128)S(1)}, u32[]{:S(2)}, u32[]{:S(2)}) collective-permute-start(f32[1,1,1,128,2]{3,4,2,1,0:T(2,128)S(1)} %constant_dynamic-slice_fusion), channel_id=1, source_target_pairs={{0,8},{4,12},{8,0},{12,4},{16,24},{20,28},{24,16},{28,20},{1,9},{5... | collective-permute-start | bytes 3080 | tf_op jit(solution)/shard_map/ppermute | solution.py:225
  96.9 7.1 %collective-permute-start.39 = (f32[128,4]{0,1:T(4,128)S(1)}, f32[128,4]{0,1:T(4,128)S(1)}, u32[]{:S(2)}, u32[]{:S(2)}) collective-permute-start(f32[128,4]{0,1:T(4,128)S(1)} %pad_maximum_fusion.13), channel_id=1, source_target_pairs={{0,1},{1,2},{2,3},{3,0},{4,5},{5,6},{6,7},{7,4},{8,9},{9,10},{10,1... | collective-permute-start | bytes 6152 | tf_op jit(solution)/shard_map/ppermute | solution.py:270
  97.6 6.4 %collective-permute-start.40 = (f32[128,4]{0,1:T(4,128)S(1)}, f32[128,4]{0,1:T(4,128)S(1)}, u32[]{:S(2)}, u32[]{:S(2)}) collective-permute-start(f32[128,4]{0,1:T(4,128)S(1)} %pad_maximum_fusion.13), channel_id=1, source_target_pairs={{0,2},{1,3},{2,0},{3,1},{4,6},{5,7},{6,4},{7,5},{8,10},{9,11},{10,... | collective-permute-start | bytes 6152 | tf_op jit(solution)/shard_map/ppermute | solution.py:270
  98.0 6.1 %collective-permute-start.41 = (f32[128,4]{0,1:T(4,128)S(1)}, f32[128,4]{0,1:T(4,128)S(1)}, u32[]{:S(2)}, u32[]{:S(2)}) collective-permute-start(f32[128,4]{0,1:T(4,128)S(1)} %pad_maximum_fusion.13), channel_id=1, source_target_pairs={{0,3},{1,0},{2,1},{3,2},{4,7},{5,4},{6,5},{7,6},{8,11},{9,8},{10,9... | collective-permute-start | bytes 6152 | tf_op jit(solution)/shard_map/ppermute | solution.py:270
  105.7 14.9 %collective-permute-start.29 = (bf16[1,2,1,128,1024]{4,3,2,1,0:T(8,128)(2,1)S(1)}, bf16[1,2,1,128,1024]{4,3,2,1,0:T(8,128)(2,1)S(1)}, u32[]{:S(2)}, u32[]{:S(2)}) collective-permute-start(bf16[1,2,1,128,1024]{4,3,2,1,0:T(8,128)(2,1)S(1)} %constant_dynamic-slice_fusion.11), channel_id=1, source_target_pairs={{0,16},{4,20},{8,24},{12,28},{16,0},{20,4},{24,8},{28,12},{1,17},{... | collective-permute-start | bytes 1572872 | tf_op jit(solution)/shard_map/ppermute | solution.py:225
  107.2 15.2 %collective-permute-start.27 = (bf16[2,1,1,128,1024]{4,3,2,1,0:T(8,128)(2,1)S(1)}, bf16[2,1,1,128,1024]{4,3,2,1,0:T(8,128)(2,1)S(1)}, u32[]{:S(2)}, u32[]{:S(2)}) collective-permute-start(bf16[2,1,1,128,1024]{4,3,2,1,0:T(8,128)(2,1)S(1)} %constant_dynamic-slice_fusion.13), channel_id=1, source_target_pairs={{0,8},{4,12},{8,0},{12,4},{16,24},{20,28},{24,16},{28,20},{1,9},{5... | collective-permute-start | bytes 1572872 | tf_op jit(solution)/shard_map/ppermute | solution.py:225
  109.0 22.9 %collective-permute-start.15 = (bf16[1,2,1,128,1024]{4,3,2,1,0:T(8,128)(2,1)S(1)}, bf16[1,2,1,128,1024]{4,3,2,1,0:T(8,128)(2,1)S(1)}, u32[]{:S(2)}, u32[]{:S(2)}) collective-permute-start(bf16[1,2,1,128,1024]{4,3,2,1,0:T(8,128)(2,1)S(1)} %constant_dynamic-slice_fusion.16), channel_id=1, source_target_pairs={{0,16},{4,20},{8,24},{12,28},{16,0},{20,4},{24,8},{28,12},{1,17},{... | collective-permute-start | bytes 1572872 | tf_op jit(solution)/shard_map/ppermute | solution.py:225
  110.6 23.1 %collective-permute-start.13 = (bf16[2,1,1,128,1024]{4,3,2,1,0:T(8,128)(2,1)S(1)}, bf16[2,1,1,128,1024]{4,3,2,1,0:T(8,128)(2,1)S(1)}, u32[]{:S(2)}, u32[]{:S(2)}) collective-permute-start(bf16[2,1,1,128,1024]{4,3,2,1,0:T(8,128)(2,1)S(1)} %constant_dynamic-slice_fusion.18), channel_id=1, source_target_pairs={{0,8},{4,12},{8,0},{12,4},{16,24},{20,28},{24,16},{28,20},{1,9},{5... | collective-permute-start | bytes 1572872 | tf_op jit(solution)/shard_map/ppermute | solution.py:225
  120.9 16.5 %collective-permute-start.30 = (bf16[1,1,1,128,1024]{4,3,2,1,0:T(8,128)(2,1)S(1)}, bf16[1,1,1,128,1024]{4,3,2,1,0:T(8,128)(2,1)S(1)}, u32[]{:S(2)}, u32[]{:S(2)}) collective-permute-start(bf16[1,1,1,128,1024]{4,3,2,1,0:T(8,128)(2,1)S(1)} %constant_dynamic-slice_fusion.10), channel_id=1, source_target_pairs={{0,8},{4,12},{8,0},{12,4},{16,24},{20,28},{24,16},{28,20},{1,9},{5... | collective-permute-start | bytes 786440 | tf_op jit(solution)/shard_map/ppermute | solution.py:225
  122.7 14.8 %collective-permute-start.28 = (bf16[1,1,1,128,1024]{4,3,2,1,0:T(8,128)(2,1)S(1)}, bf16[1,1,1,128,1024]{4,3,2,1,0:T(8,128)(2,1)S(1)}, u32[]{:S(2)}, u32[]{:S(2)}) collective-permute-start(bf16[1,1,1,128,1024]{4,3,2,1,0:T(8,128)(2,1)S(1)} %constant_dynamic-slice_fusion.12), channel_id=1, source_target_pairs={{0,16},{4,20},{8,24},{12,28},{16,0},{20,4},{24,8},{28,12},{1,17},{... | collective-permute-start | bytes 786440 | tf_op jit(solution)/shard_map/ppermute | solution.py:225
  132.1 10.4 %collective-permute-start.16 = (bf16[1,1,1,128,1024]{4,3,2,1,0:T(8,128)(2,1)S(1)}, bf16[1,1,1,128,1024]{4,3,2,1,0:T(8,128)(2,1)S(1)}, u32[]{:S(2)}, u32[]{:S(2)}) collective-permute-start(bf16[1,1,1,128,1024]{4,3,2,1,0:T(8,128)(2,1)S(1)} %constant_dynamic-slice_fusion.15), channel_id=1, source_target_pairs={{0,8},{4,12},{8,0},{12,4},{16,24},{20,28},{24,16},{28,20},{1,9},{5... | collective-permute-start | bytes 786440 | tf_op jit(solution)/shard_map/ppermute | solution.py:225
  133.9 8.7 %collective-permute-start.14 = (bf16[1,1,1,128,1024]{4,3,2,1,0:T(8,128)(2,1)S(1)}, bf16[1,1,1,128,1024]{4,3,2,1,0:T(8,128)(2,1)S(1)}, u32[]{:S(2)}, u32[]{:S(2)}) collective-permute-start(bf16[1,1,1,128,1024]{4,3,2,1,0:T(8,128)(2,1)S(1)} %constant_dynamic-slice_fusion.17), channel_id=1, source_target_pairs={{0,16},{4,20},{8,24},{12,28},{16,0},{20,4},{24,8},{28,12},{1,17},{... | collective-permute-start | bytes 786440 | tf_op jit(solution)/shard_map/ppermute | solution.py:225
  137.8 8.3 %collective-permute-start.31 = (bf16[128,512]{1,0:T(8,128)(2,1)S(1)}, bf16[128,512]{1,0:T(8,128)(2,1)S(1)}, u32[]{:S(2)}, u32[]{:S(2)}) collective-permute-start(bf16[128,512]{1,0:T(8,128)(2,1)S(1)} %get-tuple-element.54), channel_id=1, source_target_pairs={{0,1},{1,2},{2,3},{3,0},{4,5},{5,6},{6,7},{7,4},{8,9},{9,10},{10,1... | collective-permute-start | bytes 393224 | tf_op jit(solution)/shard_map/ppermute | solution.py:270
  138.5 13.8 %collective-permute-start.32 = (bf16[128,512]{1,0:T(8,128)(2,1)S(1)}, bf16[128,512]{1,0:T(8,128)(2,1)S(1)}, u32[]{:S(2)}, u32[]{:S(2)}) collective-permute-start(bf16[128,512]{1,0:T(8,128)(2,1)S(1)} %get-tuple-element.55), channel_id=1, source_target_pairs={{0,2},{1,3},{2,0},{3,1},{4,6},{5,7},{6,4},{7,5},{8,10},{9,11},{10,... | collective-permute-start | bytes 393224 | tf_op jit(solution)/shard_map/ppermute | solution.py:270
  139.7 12.5 %collective-permute-start.33 = (bf16[128,512]{1,0:T(8,128)(2,1)S(1)}, bf16[128,512]{1,0:T(8,128)(2,1)S(1)}, u32[]{:S(2)}, u32[]{:S(2)}) collective-permute-start(bf16[128,512]{1,0:T(8,128)(2,1)S(1)} %get-tuple-element.56), channel_id=1, source_target_pairs={{0,3},{1,0},{2,1},{3,2},{4,7},{5,4},{6,5},{7,6},{8,11},{9,8},{10,9... | collective-permute-start | bytes 393224 | tf_op jit(solution)/shard_map/ppermute | solution.py:270
  143.0 10.0 %collective-permute-start.17 = (bf16[128,512]{1,0:T(8,128)(2,1)S(1)}, bf16[128,512]{1,0:T(8,128)(2,1)S(1)}, u32[]{:S(2)}, u32[]{:S(2)}) collective-permute-start(bf16[128,512]{1,0:T(8,128)(2,1)S(1)} %get-tuple-element.57), channel_id=1, source_target_pairs={{0,1},{1,2},{2,3},{3,0},{4,5},{5,6},{6,7},{7,4},{8,9},{9,10},{10,1... | collective-permute-start | bytes 393224 | tf_op jit(solution)/shard_map/ppermute | solution.py:270
  143.0 12.4 %collective-permute-start.18 = (bf16[128,512]{1,0:T(8,128)(2,1)S(1)}, bf16[128,512]{1,0:T(8,128)(2,1)S(1)}, u32[]{:S(2)}, u32[]{:S(2)}) collective-permute-start(bf16[128,512]{1,0:T(8,128)(2,1)S(1)} %get-tuple-element.58), channel_id=1, source_target_pairs={{0,2},{1,3},{2,0},{3,1},{4,6},{5,7},{6,4},{7,5},{8,10},{9,11},{10,... | collective-permute-start | bytes 393224 | tf_op jit(solution)/shard_map/ppermute | solution.py:270
  146.2 9.3 %collective-permute-start.19 = (bf16[128,512]{1,0:T(8,128)(2,1)S(1)}, bf16[128,512]{1,0:T(8,128)(2,1)S(1)}, u32[]{:S(2)}, u32[]{:S(2)}) collective-permute-start(bf16[128,512]{1,0:T(8,128)(2,1)S(1)} %get-tuple-element.59), channel_id=1, source_target_pairs={{0,3},{1,0},{2,1},{3,2},{4,7},{5,4},{6,5},{7,6},{8,11},{9,8},{10,9... | collective-permute-start | bytes 393224 | tf_op jit(solution)/shard_map/ppermute | solution.py:270
